TPU v7x, 256 devices: a whole 4x4x8 slice. The times are simulated.
256 devices in a mesh: ens: 2 (over z_hi), tile: 128 (over x, y, z_lo, core).
Axes of the slice: x: 4, y: 4, z: 8 (z_hi: 2, z_lo: 4; z = z_hi * 4 + z_lo), core: 2. Of those that a mesh axis runs over, the one named last changes fastest.
Arguments:
- fields: bfloat16 [2, 128, 64, 16, 128], P('ens', 'tile'), may hold values from -6 to 6
- cotangent: bfloat16 [2, 128, 64, 16, 128], P('ens', 'tile'), may hold values from -6 to 6
- kernel_first: bfloat16 [9, 64, 64], replicated, may hold values from -0.25 to 0.25
- kernel_second: bfloat16 [9, 128, 64], replicated, may hold values from -0.25 to 0.25
- kernel_third: bfloat16 [9, 128, 128], replicated, may hold values from -0.1875 to 0.1875
- closing_filter_weights: bfloat16 [9, 64, 192], replicated, may hold values from -0.15625 to 0.15625
- offset_first: float32 [64], replicated, may hold values from -3 to 3
- offset_second: float32 [128], replicated, may hold values from -3 to 3
- offset_third: float32 [128], replicated, may hold values from -3 to 3
- closing_shift_values: float32 [64], replicated, may hold values from -3 to 3
- codes: int32 [128, 4], P('tile'), may hold values from 0 to 3
- filter_stride_spread: int32 [4], replicated, may hold values from 1 to 4, as said below
Outputs:
- network_predicted_state: bfloat16 [2, 128, 64, 16, 128], P('ens', 'tile')
- state_input_derivative: float32 [2, 128, 64, 16, 128], P('ens', 'tile')
- initial_filter_derivative: float32 [9, 64, 64], replicated
- latter_filter_derivative: float32 [9, 128, 64], replicated
- penultimate_filter_derivative: float32 [9, 128, 128], replicated
- closing_filter_derivative: float32 [9, 64, 192], replicated
- initial_shift_derivative: float32 [64], replicated
- latter_shift_derivative: float32 [128], replicated
- penultimate_shift_derivative: float32 [128], replicated
- closing_shift_derivative: float32 [64], replicated
Inputs may be any that keep to these rules, and one draw needn't show every extreme that they name: `codes`: bit 0 picks which of the two parallel edges of the sending tile is sent, bit 1 reverses it. `filter_stride_spread`: at least one layer has dilation 4 and one has dilation 1.
All inputs are finite; a program needn't handle non-finite values.
Results may differ from a plain program's by a relative error of at most 0.009.
Values may be sent and summed in bfloat16 or wider, within the bound.
A program may use at most 128 MiB of HBM per device.

v0:
```python
import math

import jax
import jax.numpy as jnp
from jax import lax
from jax.sharding import PartitionSpec as P

DMAX = 4
TILE_ROW = 8


def shifted(array, axis, by):
    devices = lax.axis_size(axis)
    return lax.ppermute(array, axis, [(i, (i + by) % devices) for i in range(devices)])


def exact_gelu(values):
    return jax.nn.gelu(values, approximate=False)


def gelu_slope(values):
    return jax.vjp(exact_gelu, values)[1](jnp.ones_like(values))[0]


def edge_columns(values, flag, margin):
    extent = values.shape[-1]
    picked = jnp.where(flag % 2 == 1, values[..., extent - margin :], values[..., :margin])
    return jnp.where(flag // 2 == 1, jnp.flip(picked, -2), picked)


def edge_rows(values, flag, margin):
    extent = values.shape[-2]
    picked = jnp.where(flag % 2 == 1, values[..., extent - margin :, :], values[..., :margin, :])
    return jnp.where(flag // 2 == 1, jnp.flip(picked, -1), picked)


def return_columns(summed, incoming, flag, margin):
    extent = summed.shape[-1]
    unflipped = jnp.where(flag // 2 == 1, jnp.flip(incoming, -2), incoming)
    nothing = jnp.zeros_like(unflipped)
    summed = summed.at[..., :margin].add(jnp.where(flag % 2 == 0, unflipped, nothing))
    return summed.at[..., extent - margin :].add(jnp.where(flag % 2 == 1, unflipped, nothing))


def return_rows(summed, incoming, flag, margin):
    extent = summed.shape[-2]
    unflipped = jnp.where(flag // 2 == 1, jnp.flip(incoming, -1), incoming)
    nothing = jnp.zeros_like(unflipped)
    summed = summed.at[..., :margin, :].add(jnp.where(flag % 2 == 0, unflipped, nothing))
    return summed.at[..., extent - margin :, :].add(jnp.where(flag % 2 == 1, unflipped, nothing))


def surround(values, flags, margin):
    toward_right = edge_columns(values, flags[3], margin)
    toward_left = edge_columns(values, flags[2], margin)
    leftward = shifted(toward_right, "tile", 1)
    rightward = shifted(toward_left, "tile", -1)
    widened = jnp.concatenate([leftward, values, rightward], axis=-1)
    toward_lower = edge_rows(widened, flags[1], margin)
    toward_upper = edge_rows(widened, flags[0], margin)
    upper_rim = shifted(toward_lower, "tile", TILE_ROW)
    lower_rim = shifted(toward_upper, "tile", -TILE_ROW)
    return jnp.concatenate([upper_rim, widened, lower_rim], axis=-2)


def fold_rims(padded, flags, margin):
    rows_all = padded.shape[-2]
    upper = padded[..., :margin, :]
    lower = padded[..., rows_all - margin :, :]
    inner = padded[..., margin : rows_all - margin, :]
    from_upper = shifted(upper, "tile", -TILE_ROW)
    from_lower = shifted(lower, "tile", TILE_ROW)
    inner = return_rows(inner, from_lower, flags[0], margin)
    inner = return_rows(inner, from_upper, flags[1], margin)
    cols_all = inner.shape[-1]
    left_part = inner[..., :margin]
    right_part = inner[..., cols_all - margin :]
    core = inner[..., margin : cols_all - margin]
    back_left = shifted(left_part.astype(jnp.bfloat16), "tile", -1).astype(left_part.dtype)
    back_right = shifted(right_part.astype(jnp.bfloat16), "tile", 1).astype(right_part.dtype)
    core = return_columns(core, back_right, flags[2], margin)
    return return_columns(core, back_left, flags[3], margin)


def start_of(row_tap, col_tap, spacing, border):
    zero = jnp.int32(0)
    return (zero, zero, border + (row_tap - 1) * spacing, border + (col_tap - 1) * spacing)


def convolve(padded, kernel, spacing, border):
    members, channels, rows_pad, cols_pad = padded.shape
    rows, cols = (rows_pad - 2 * border, cols_pad - 2 * border)
    summed = jnp.zeros((members, kernel.shape[1], rows, cols), jnp.float32)
    for row_tap in range(3):
        for col_tap in range(3):
            section = lax.dynamic_slice(
                padded, start_of(row_tap, col_tap, spacing, border), (members, channels, rows, cols)
            )
            summed = summed + jnp.einsum(
                "oc,mchw->mohw",
                kernel[3 * row_tap + col_tap],
                section,
                preferred_element_type=jnp.float32,
            )
    return summed


def kernel_terms(padded, grad, spacing, border):
    members, channels, rows_pad, cols_pad = padded.shape
    rows, cols = (rows_pad - 2 * border, cols_pad - 2 * border)
    listed = []
    for row_tap in range(3):
        for col_tap in range(3):
            section = lax.dynamic_slice(
                padded, start_of(row_tap, col_tap, spacing, border), (members, channels, rows, cols)
            )
            listed.append(
                jnp.einsum("mohw,mchw->oc", grad, section, preferred_element_type=jnp.float32)
            )
    return jnp.stack(listed)


def spread_back(grad, kernel, spacing, border):
    members, outs_count, rows, cols = grad.shape
    channels = kernel.shape[2]
    summed = jnp.zeros((members, channels, rows + 2 * border, cols + 2 * border), jnp.float32)
    for row_tap in range(3):
        for col_tap in range(3):
            begin = start_of(row_tap, col_tap, spacing, border)
            current = lax.dynamic_slice(summed, begin, (members, channels, rows, cols))
            summed = lax.dynamic_update_slice(
                summed,
                current
                + jnp.einsum(
                    "oc,mohw->mchw",
                    kernel[3 * row_tap + col_tap],
                    grad,
                    preferred_element_type=jnp.float32,
                ),
                begin,
            )
    return summed


def coarsen(values):
    lead = values.shape[:-2]
    rows, cols = (values.shape[-2], values.shape[-1])
    blocks = values.astype(jnp.float32).reshape(lead + (rows // 2, 2, cols // 2, 2))
    return jnp.mean(blocks, axis=(-3, -1)).astype(jnp.bfloat16)


def refine(values):
    return jnp.repeat(jnp.repeat(values, 2, axis=-2), 2, axis=-1)


def collapse(values):
    lead = values.shape[:-2]
    rows, cols = (values.shape[-2], values.shape[-1])
    return jnp.sum(values.reshape(lead + (rows // 2, 2, cols // 2, 2)), axis=(-3, -1))


def shards(
    fields,
    cotangent,
    kernel_first,
    kernel_second,
    kernel_third,
    closing_filter_weights,
    offset_first,
    offset_second,
    offset_third,
    closing_shift_values,
    codes,
    filter_stride_spread,
):
    border = DMAX
    flags = codes[0]
    start_fields = fields[:, 0]
    upstream = cotangent[:, 0]

    def back_all(grad, kernel, spacing):
        return fold_rims(spread_back(grad, kernel, spacing, border), flags, border)

    first_pad = surround(start_fields, flags, border)
    first_pre = (
        convolve(first_pad, kernel_first, filter_stride_spread[0], border)
        + offset_first[:, None, None]
    )
    first_act = exact_gelu(first_pre).astype(jnp.bfloat16)
    pooled = coarsen(first_act)
    second_pad = surround(pooled, flags, border)
    second_pre = (
        convolve(second_pad, kernel_second, filter_stride_spread[1], border)
        + offset_second[:, None, None]
    )
    second_act = exact_gelu(second_pre).astype(jnp.bfloat16)
    third_pad = surround(second_act, flags, border)
    third_pre = (
        convolve(third_pad, kernel_third, filter_stride_spread[2], border)
        + offset_third[:, None, None]
    )
    third_act = exact_gelu(third_pre).astype(jnp.bfloat16)
    joined = jnp.concatenate([refine(third_act), first_act], axis=-3)
    merged_halo_margin = surround(joined, flags, border)
    network_predicted_state = (
        convolve(merged_halo_margin, closing_filter_weights, filter_stride_spread[3], border)
        + closing_shift_values[:, None, None]
    ).astype(jnp.bfloat16)
    coarse_count = kernel_third.shape[1]
    joined_grad = back_all(upstream, closing_filter_weights, filter_stride_spread[3])
    coarse_sum = collapse(joined_grad[:, :coarse_count])
    skip_grad = joined_grad[:, coarse_count:]
    third_delta = (coarse_sum * gelu_slope(third_pre)).astype(jnp.bfloat16)
    second_delta = (
        back_all(third_delta, kernel_third, filter_stride_spread[2]) * gelu_slope(second_pre)
    ).astype(jnp.bfloat16)
    pooled_grad = back_all(second_delta, kernel_second, filter_stride_spread[1])
    first_grad = skip_grad + 0.25 * refine(pooled_grad)
    first_delta = (first_grad * gelu_slope(first_pre)).astype(jnp.bfloat16)
    state_input_derivative = back_all(first_delta, kernel_first, filter_stride_spread[0])
    terms_fourth = kernel_terms(merged_halo_margin, upstream, filter_stride_spread[3], border)
    terms_third = kernel_terms(third_pad, third_delta, filter_stride_spread[2], border)
    terms_second = kernel_terms(second_pad, second_delta, filter_stride_spread[1], border)
    terms_first = kernel_terms(first_pad, first_delta, filter_stride_spread[0], border)
    axes_sum = (0, 2, 3)
    bias_first = jnp.sum(first_delta.astype(jnp.float32), axis=axes_sum)
    bias_second = jnp.sum(second_delta.astype(jnp.float32), axis=axes_sum)
    bias_third = jnp.sum(third_delta.astype(jnp.float32), axis=axes_sum)
    bias_fourth = jnp.sum(upstream.astype(jnp.float32), axis=axes_sum)
    summed = lax.psum(
        (
            terms_first,
            terms_second,
            terms_third,
            terms_fourth,
            bias_first,
            bias_second,
            bias_third,
            bias_fourth,
        ),
        ("ens", "tile"),
    )
    members_count = start_fields.shape[0] * lax.axis_size("ens")
    scale = jnp.float32(
        1.0
        / math.sqrt(
            members_count * lax.axis_size("tile") * start_fields.shape[2] * start_fields.shape[3]
        )
    )
    scaled = [entry * scale for entry in summed]
    return (
        network_predicted_state[:, None],
        state_input_derivative[:, None],
        scaled[0],
        scaled[1],
        scaled[2],
        scaled[3],
        scaled[4],
        scaled[5],
        scaled[6],
        scaled[7],
    )


def solution(mesh):
    in_specs = (
        P("ens", "tile", None, None, None),
        P("ens", "tile", None, None, None),
        P(),
        P(),
        P(),
        P(),
        P(),
        P(),
        P(),
        P(),
        P("tile", None),
        P(),
    )
    out_specs = (
        P("ens", "tile", None, None, None),
        P("ens", "tile", None, None, None),
        P(),
        P(),
        P(),
        P(),
        P(),
        P(),
        P(),
        P(),
    )
    return jax.shard_map(shards, mesh=mesh, in_specs=in_specs, out_specs=out_specs, check_vma=False)
```

profile of v0, /device:TPU:1, one launch (start us, length us, event | category | flops | bytes accessed | tf_op | source)
XLA Modules:
  0.0 920.6 jit_solution(14360712835263554858)
XLA Ops:
  14.5 3.3 collective-permute-start.1
  22.2 2.7 broadcast_in_dim.42
  24.9 11.5 %dynamic_update_slice.108 = f32[1,192,24,136]{3,1,2,0:T(8,128)} dynamic-update-slice(f32[1,192,24,136]{3,1,2,0:T(8,128)} %broadcast_in_dim.42, f32[1,192,16,128]{3,1,2,0:T(8,128)S(1)} %convolution_bitcast_fusion, s32[]{:T(128)} %constant.1024.clone.1, s32[]{:T(128)} %constant.1024.clone.1, s32[]{:T(128)S(6)} %select_n.896, s32[]{:T(128)S(6)} %select_n.897) | dynamic-update-slice | bytes 3145732 | tf_op jit(solution)/shard_map/dynamic_update_slice | solution.py:131
  38.9 11.6 %dynamic_update_slice.109 = f32[1,192,24,136]{3,1,2,0:T(8,128)} dynamic-update-slice(f32[1,192,24,136]{3,1,2,0:T(8,128)} %dynamic_update_slice.108, f32[1,192,16,128]{3,1,2,0:T(8,128)S(1)} %bitcast_add_fusion.6, s32[]{:T(128)} %constant.1024.clone.1, s32[]{:T(128)} %constant.1024.clone.1, s32[]{:T(128)S(6)} %select_n.896, s32[]{:T(128)} %constant.1031.clone.1) | dynamic-update-slice | bytes 3145732 | tf_op jit(solution)/shard_map/dynamic_update_slice | solution.py:131
  52.8 11.6 %dynamic_update_slice.110 = f32[1,192,24,136]{3,1,2,0:T(8,128)} dynamic-update-slice(f32[1,192,24,136]{3,1,2,0:T(8,128)} %dynamic_update_slice.109, f32[1,192,16,128]{3,1,2,0:T(8,128)S(1)} %bitcast_add_fusion.5, s32[]{:T(128)} %constant.1024.clone.1, s32[]{:T(128)} %constant.1024.clone.1, s32[]{:T(128)S(6)} %select_n.896, s32[]{:T(128)S(6)} %select_n.898) | dynamic-update-slice | bytes 3145732 | tf_op jit(solution)/shard_map/dynamic_update_slice | solution.py:131
  66.8 11.6 %dynamic_update_slice.111 = f32[1,192,24,136]{3,1,2,0:T(8,128)} dynamic-update-slice(f32[1,192,24,136]{3,1,2,0:T(8,128)} %dynamic_update_slice.110, f32[1,192,16,128]{3,1,2,0:T(8,128)S(1)} %bitcast_add_fusion.4, s32[]{:T(128)} %constant.1024.clone.1, s32[]{:T(128)} %constant.1024.clone.1, s32[]{:T(128)} %constant.1031.clone.1, s32[]{:T(128)S(6)} %select_n.897) | dynamic-update-slice | bytes 3145732 | tf_op jit(solution)/shard_map/dynamic_update_slice | solution.py:131
  80.9 11.6 %dynamic_update_slice.112 = f32[1,192,24,136]{3,1,2,0:T(8,128)} dynamic-update-slice(f32[1,192,24,136]{3,1,2,0:T(8,128)} %dynamic_update_slice.111, f32[1,192,16,128]{3,1,2,0:T(8,128)S(1)} %slice_add_fusion.4, s32[]{:T(128)} %constant.1024.clone.1, s32[]{:T(128)} %constant.1024.clone.1, s32[]{:T(128)} %constant.1031.clone.1, s32[]{:T(128)} %constant.1031.clone.1) | dynamic-update-slice | bytes 3145732 | tf_op jit(solution)/shard_map/dynamic_update_slice | solution.py:131
  100.7 11.6 %dynamic_update_slice.113 = f32[1,192,24,136]{3,1,2,0:T(8,128)} dynamic-update-slice(f32[1,192,24,136]{3,1,2,0:T(8,128)} %dynamic_update_slice.112, f32[1,192,16,128]{3,1,2,0:T(8,128)S(1)} %bitcast_add_fusion.3, s32[]{:T(128)} %constant.1024.clone.1, s32[]{:T(128)} %constant.1024.clone.1, s32[]{:T(128)} %constant.1031.clone.1, s32[]{:T(128)S(6)} %select_n.898) | dynamic-update-slice | bytes 3145732 | tf_op jit(solution)/shard_map/dynamic_update_slice | solution.py:131
  112.9 4.8 collective-permute-start.3
  123.5 11.5 %dynamic_update_slice.114 = f32[1,192,24,136]{3,1,2,0:T(8,128)} dynamic-update-slice(f32[1,192,24,136]{3,1,2,0:T(8,128)} %dynamic_update_slice.113, f32[1,192,16,128]{3,1,2,0:T(8,128)S(1)} %bitcast_add_fusion.2, s32[]{:T(128)} %constant.1024.clone.1, s32[]{:T(128)} %constant.1024.clone.1, s32[]{:T(128)S(6)} %select_n.899, s32[]{:T(128)S(6)} %select_n.897) | dynamic-update-slice | bytes 3145732 | tf_op jit(solution)/shard_map/dynamic_update_slice | solution.py:131
  142.3 4.3 collective-permute-start.5
  149.2 11.5 %dynamic_update_slice.115 = f32[1,192,24,136]{3,1,2,0:T(8,128)} dynamic-update-slice(f32[1,192,24,136]{3,1,2,0:T(8,128)} %dynamic_update_slice.114, f32[1,192,16,128]{3,1,2,0:T(8,128)S(1)} %bitcast_add_fusion.1, s32[]{:T(128)} %constant.1024.clone.1, s32[]{:T(128)} %constant.1024.clone.1, s32[]{:T(128)S(6)} %select_n.899, s32[]{:T(128)} %constant.1031.clone.1) | dynamic-update-slice | bytes 3145732 | tf_op jit(solution)/shard_map/dynamic_update_slice | solution.py:131
  161.0 3.9 collective-permute-start.7
  170.5 11.5 %dynamic_update_slice.116 = f32[1,192,24,136]{3,1,2,0:T(8,128)} dynamic-update-slice(f32[1,192,24,136]{3,1,2,0:T(8,128)} %dynamic_update_slice.115, f32[1,192,16,128]{3,1,2,0:T(8,128)S(1)} %bitcast_add_fusion, s32[]{:T(128)} %constant.1024.clone.1, s32[]{:T(128)} %constant.1024.clone.1, s32[]{:T(128)S(6)} %select_n.899, s32[]{:T(128)S(6)} %select_n.898) | dynamic-update-slice | bytes 3145732 | tf_op jit(solution)/shard_map/dynamic_update_slice | solution.py:131
  186.7 8.7 collective-permute-start.9
  199.8 4.8 collective-permute-start.17
  209.8 2.7 rev.123
  214.0 2.7 rev.122
  220.2 4.0 collective-permute-done.10
  231.0 9.0 reverse.4
  242.4 9.0 reverse.5
  265.0 12.1 %collective-permute-start.19 = (bf16[1,192,16,4]{1,2,3,0:T(8,128)(2,1)}, bf16[1,192,16,4]{1,2,3,0:T(8,128)(2,1)}, u32[]{:S(2)}, u32[]{:S(2)}) collective-permute-start(bf16[1,192,16,4]{1,2,3,0:T(8,128)(2,1)} %copy.164), channel_id=1, source_target_pairs={{0,127},{1,0},{2,1},{3,2},{4,3},{5,4},{6,5},{7,6},{8,7},{9,8},{10,... | collective-permute-start | bytes 73736 | tf_op jit(solution)/shard_map/ppermute | solution.py:14
  279.4 3.5 slice_add_fusion.3
  282.9 8.0 scatter-add.120
  290.9 3.1 slice_add_fusion.2
  294.1 15.2 %scatter-add.121 = f32[1,192,16,128]{3,1,2,0:T(8,128)S(1)} dynamic-update-slice(f32[1,192,16,128]{3,1,2,0:T(8,128)S(1)} %copy-done.1, f32[1,192,16,4]{3,1,2,0:T(8,128)} %slice_add_fusion.2, s32[]{:T(128)} %constant.1024.clone.1, s32[]{:T(128)} %constant.1024.clone.1, s32[]{:T(128)} %constant.1024.clone.1, s32[]{:T(128)} %constant.1066.clone.1) | dynamic-update-slice | bytes 98308 | tf_op jit(solution)/shard_map/scatter-add | solution.py:42
  311.8 13.2 %scatter-add.124 = f32[1,192,16,128]{3,1,2,0:T(8,128)S(1)} dynamic-update-slice(f32[1,192,16,128]{3,1,2,0:T(8,128)S(1)} %scatter-add.121, f32[1,192,16,4]{3,1,2,0:T(8,128)} %slice_add_fusion.1, s32[]{:T(128)} %constant.1024.clone.1, s32[]{:T(128)} %constant.1024.clone.1, s32[]{:T(128)} %constant.1024.clone.1, s32[]{:T(128)} %constant.1024.clone.1) | dynamic-update-slice | bytes 98308 | tf_op jit(solution)/shard_map/scatter-add | solution.py:41
  326.6 15.2 %scatter-add.125 = f32[1,192,16,128]{3,1,2,0:T(8,128)S(1)} dynamic-update-slice(f32[1,192,16,128]{3,1,2,0:T(8,128)S(1)} %scatter-add.124, f32[1,192,16,4]{3,1,2,0:T(8,128)} %slice_add_fusion, s32[]{:T(128)} %constant.1024.clone.1, s32[]{:T(128)} %constant.1024.clone.1, s32[]{:T(128)} %constant.1024.clone.1, s32[]{:T(128)} %constant.1066.clone.1) | dynamic-update-slice | bytes 98308 | tf_op jit(solution)/shard_map/scatter-add | solution.py:42
  353.5 7.8 collective-permute-start.13
  372.0 4.8 collective-permute-start.21
  411.2 4.7 collective-permute-start.25
  425.4 6.0 collective-permute-start.27
  431.4 3.3 pad_maximum_fusion
  468.4 3.7 dynamic_update_slice.135
  474.4 5.3 dynamic_update_slice.136
  482.0 5.3 dynamic_update_slice.137
  489.5 3.7 dynamic_update_slice.138
  495.5 5.2 dynamic_update_slice.139
  503.1 5.2 dynamic_update_slice.140
  510.6 3.7 dynamic_update_slice.141
  516.6 5.3 dynamic_update_slice.142
  524.2 5.3 dynamic_update_slice.143
  535.4 4.8 collective-permute-start.29
  551.3 78.7 %all-reduce = (f32[64]{0:T(128)S(1)}, f32[128]{0:T(128)S(1)}, f32[128]{0:T(128)S(1)}, f32[64]{0:T(128)S(1)}) all-reduce(f32[64]{0:T(128)S(1)} %copy-done.51, f32[128]{0:T(128)S(1)} %copy-done.50, f32[128]{0:T(128)S(1)} %copy-done.53, f32[64]{0:T(128)S(1)} %copy-done.49), channel_id=1, replica_groups=mesh['ens'=2,'tile'=128] {'ens','tile'}, use_global_device_ids=true, to_apply=%region_7.8 | all-reduce | flops 384 | bytes 3072 | tf_op jit(solution)/shard_map/psum | solution.py:230
  630.6 2.6 fusion.7
  651.9 3.6 scatter-add.195
  657.8 3.6 scatter-add.197
  662.5 245.6 %all-reduce.4.cloned.1.call-done = (f32[9,64,64]{2,1,0:T(8,128)}, f32[9,128,64]{1,2,0:T(8,128)}, f32[9,128,128]{2,1,0:T(8,128)}, f32[9,64,192]{2,1,0:T(8,128)}) async-done(((f32[9,64,64]{2,1,0:T(8,128)}, f32[9,128,64]{1,2,0:T(8,128)}, f32[9,128,128]{2,1,0:T(8,128)}, f32[9,64,192]{2,1,0:T(8,128)}), (f32[9,64,64]{2,1,0:T(8,128)}, f32[9,128,64]{1,2,0:T(8,128)}, f32[9,128,128]{2,1,0:T(8,128)}, ...) | async-done | bytes 1474576 | tf_op jit(solution)/shard_map/psum | solution.py:230
  (443 shorter events, 241.6 us)
Async XLA Ops:
  7.2 12.1 %copy-start.48 = (s32[4]{0:T(128)S(1)}, s32[4]{0:T(128)}, u32[]{:S(2)}) copy-start(s32[4]{0:T(128)} %param.87) | copy-start | bytes 52
  7.2 14.6 %copy-start.31 = (bf16[9,64,192]{2,1,0:T(8,128)(2,1)S(1)}, bf16[9,64,192]{2,1,0:T(8,128)(2,1)}, u32[]{:S(2)}) copy-start(bf16[9,64,192]{2,1,0:T(8,128)(2,1)} %param.81) | copy-start | bytes 663556
  7.2 14.6 %copy-start = (bf16[1,1,64,16,128]{4,3,2,1,0:T(8,128)(2,1)S(1)}, bf16[1,1,64,16,128]{4,3,2,1,0:T(8,128)(2,1)}, u32[]{:S(2)}) copy-start(bf16[1,1,64,16,128]{4,3,2,1,0:T(8,128)(2,1)} %param.77) | copy-start | bytes 786436
  7.2 900.8 %all-reduce.4.cloned.1.call-start = ((), (), s32[]{:S(2)}) async-start(), calls=%async_computation | async-start | bytes 3538944 | tf_op jit(solution)/shard_map/psum | solution.py:230
  14.5 97.8 %collective-permute-start.1 = (bf16[1,64,16,4]{3,1,2,0:T(8,128)(2,1)S(1)}, bf16[1,64,16,4]{3,1,2,0:T(8,128)(2,1)S(1)}, u32[]{:S(2)}, u32[]{:S(2)}) collective-permute-start(bf16[1,64,16,4]{3,1,2,0:T(8,128)(2,1)S(1)} %reverse_select_fusion.8), channel_id=1, source_target_pairs={{0,127},{1,0},{2,1},{3,2},{4,3},{5,4},{6,5},{7,6},{8,7},{9,8},{10,... | collective-permute-start | bytes 24584 | tf_op jit(solution)/shard_map/ppermute | solution.py:14
  19.3 93.1 %collective-permute-start = (bf16[1,64,16,4]{3,1,2,0:T(8,128)(2,1)}, bf16[1,64,16,4]{3,1,2,0:T(8,128)(2,1)S(1)}, u32[]{:S(2)}, u32[]{:S(2)}) collective-permute-start(bf16[1,64,16,4]{3,1,2,0:T(8,128)(2,1)} %reverse_select_fusion.9), channel_id=1, source_target_pairs={{0,1},{1,2},{2,3},{3,4},{4,5},{5,6},{6,7},{7,8},{8,9},{9,10},{10,1... | collective-permute-start | bytes 24584 | tf_op jit(solution)/shard_map/ppermute | solution.py:14
  112.9 22.0 %collective-permute-start.3 = (bf16[1,64,4,136]{3,1,2,0:T(8,128)(2,1)S(1)}, bf16[1,64,4,136]{3,1,2,0:T(8,128)(2,1)S(1)}, u32[]{:S(2)}, u32[]{:S(2)}) collective-permute-start(bf16[1,64,4,136]{3,1,2,0:T(8,128)(2,1)S(1)} %broadcast_select_fusion.13), channel_id=1, source_target_pairs={{0,120},{1,121},{2,122},{3,123},{4,124},{5,125},{6,126},{7,127},{8... | collective-permute-start | bytes 208904 | tf_op jit(solution)/shard_map/ppermute | solution.py:14
  118.1 16.8 %collective-permute-start.2 = (bf16[1,64,4,136]{3,1,2,0:T(8,128)(2,1)S(1)}, bf16[1,64,4,136]{3,1,2,0:T(8,128)(2,1)S(1)}, u32[]{:S(2)}, u32[]{:S(2)}) collective-permute-start(bf16[1,64,4,136]{3,1,2,0:T(8,128)(2,1)S(1)} %broadcast_select_fusion.16), channel_id=1, source_target_pairs={{0,8},{1,9},{2,10},{3,11},{4,12},{5,13},{6,14},{7,15},{8,16},{9,17... | collective-permute-start | bytes 208904 | tf_op jit(solution)/shard_map/ppermute | solution.py:14
  142.1 41.2 %copy-start.20 = (f32[64,8,64]{2,0,1:T(8,128)}, f32[64,8,64]{2,0,1:T(8,128)S(1)}, u32[]{:S(2)}) copy-start(f32[64,8,64]{2,0,1:T(8,128)S(1)} %copy.130) | copy-start | bytes 393220
  142.3 18.4 %collective-permute-start.5 = (bf16[1,64,8,4]{3,1,2,0:T(8,128)(2,1)S(1)}, bf16[1,64,8,4]{3,1,2,0:T(8,128)(2,1)S(1)}, u32[]{:S(2)}, u32[]{:S(2)}) collective-permute-start(bf16[1,64,8,4]{3,1,2,0:T(8,128)(2,1)S(1)} %reverse_select_fusion.10), channel_id=1, source_target_pairs={{0,127},{1,0},{2,1},{3,2},{4,3},{5,4},{6,5},{7,6},{8,7},{9,8},{10,... | collective-permute-start | bytes 12296 | tf_op jit(solution)/shard_map/ppermute | solution.py:14
  146.7 14.0 %collective-permute-start.4 = (bf16[1,64,8,4]{3,1,2,0:T(8,128)(2,1)S(1)}, bf16[1,64,8,4]{3,1,2,0:T(8,128)(2,1)S(1)}, u32[]{:S(2)}, u32[]{:S(2)}) collective-permute-start(bf16[1,64,8,4]{3,1,2,0:T(8,128)(2,1)S(1)} %reverse_select_fusion.11), channel_id=1, source_target_pairs={{0,1},{1,2},{2,3},{3,4},{4,5},{5,6},{6,7},{7,8},{8,9},{9,10},{10,1... | collective-permute-start | bytes 12296 | tf_op jit(solution)/shard_map/ppermute | solution.py:14
  161.0 21.0 %collective-permute-start.7 = (bf16[1,64,4,72]{3,1,2,0:T(8,128)(2,1)S(1)}, bf16[1,64,4,72]{3,1,2,0:T(8,128)(2,1)S(1)}, u32[]{:S(2)}, u32[]{:S(2)}) collective-permute-start(bf16[1,64,4,72]{3,1,2,0:T(8,128)(2,1)S(1)} %broadcast_select_fusion.26), channel_id=1, source_target_pairs={{0,120},{1,121},{2,122},{3,123},{4,124},{5,125},{6,126},{7,127},{8... | collective-permute-start | bytes 110600 | tf_op jit(solution)/shard_map/ppermute | solution.py:14
  165.0 17.0 %collective-permute-start.6 = (bf16[1,64,4,72]{3,1,2,0:T(8,128)(2,1)S(1)}, bf16[1,64,4,72]{3,1,2,0:T(8,128)(2,1)S(1)}, u32[]{:S(2)}, u32[]{:S(2)}) collective-permute-start(bf16[1,64,4,72]{3,1,2,0:T(8,128)(2,1)S(1)} %broadcast_select_fusion.29), channel_id=1, source_target_pairs={{0,8},{1,9},{2,10},{3,11},{4,12},{5,13},{6,14},{7,15},{8,16},{9,17... | collective-permute-start | bytes 110600 | tf_op jit(solution)/shard_map/ppermute | solution.py:14
  170.5 11.6 %copy-start.43 = (bf16[9,128,64]{1,2,0:T(8,128)(2,1)S(1)}, bf16[9,128,64]{1,2,0:T(8,128)(2,1)}, u32[]{:S(2)}) copy-start(bf16[9,128,64]{1,2,0:T(8,128)(2,1)} %param.79) | copy-start | bytes 442372
  186.7 22.3 %collective-permute-start.9 = (bf16[1,128,8,4]{1,3,2,0:T(4,128)(2,1)}, bf16[1,128,8,4]{1,3,2,0:T(4,128)(2,1)S(1)}, u32[]{:S(2)}, u32[]{:S(2)}) collective-permute-start(bf16[1,128,8,4]{1,3,2,0:T(4,128)(2,1)} %reverse_select_fusion.14), channel_id=1, source_target_pairs={{0,127},{1,0},{2,1},{3,2},{4,3},{5,4},{6,5},{7,6},{8,7},{9,8},{10,... | collective-permute-start | bytes 24584 | tf_op jit(solution)/shard_map/ppermute | solution.py:14
  196.1 13.0 %collective-permute-start.8 = (bf16[1,128,8,4]{1,3,2,0:T(4,128)(2,1)}, bf16[1,128,8,4]{1,3,2,0:T(4,128)(2,1)S(1)}, u32[]{:S(2)}, u32[]{:S(2)}) collective-permute-start(bf16[1,128,8,4]{1,3,2,0:T(4,128)(2,1)} %reverse_select_fusion.15), channel_id=1, source_target_pairs={{0,1},{1,2},{2,3},{3,4},{4,5},{5,6},{6,7},{7,8},{8,9},{9,10},{10,1... | collective-permute-start | bytes 24584 | tf_op jit(solution)/shard_map/ppermute | solution.py:14
  198.7 30.1 %collective-permute-start.16 = (f32[1,192,4,136]{1,3,2,0:T(8,128)}, f32[1,192,4,136]{1,3,2,0:T(8,128)}, u32[]{:S(2)}, u32[]{:S(2)}) collective-permute-start(f32[1,192,4,136]{1,3,2,0:T(8,128)} %copy.155), channel_id=1, source_target_pairs={{0,8},{1,9},{2,10},{3,11},{4,12},{5,13},{6,14},{7,15},{8,16},{9,17... | collective-permute-start | bytes 1253384 | tf_op jit(solution)/shard_map/ppermute | solution.py:14
  199.8 40.2 %collective-permute-start.17 = (f32[1,192,4,136]{1,3,2,0:T(8,128)}, f32[1,192,4,136]{1,3,2,0:T(8,128)}, u32[]{:S(2)}, u32[]{:S(2)}) collective-permute-start(f32[1,192,4,136]{1,3,2,0:T(8,128)} %copy.158), channel_id=1, source_target_pairs={{0,120},{1,121},{2,122},{3,123},{4,124},{5,125},{6,126},{7,127},{8... | collective-permute-start | bytes 1253384 | tf_op jit(solution)/shard_map/ppermute | solution.py:14
  214.0 6.2 collective-permute-start.11
  216.6 10.5 %copy-start.33 = (bf16[9,128,128]{2,1,0:T(8,128)(2,1)S(1)}, bf16[9,128,128]{2,1,0:T(8,128)(2,1)}, u32[]{:S(2)}) copy-start(bf16[9,128,128]{2,1,0:T(8,128)(2,1)} %param.80) | copy-start | bytes 884740
  217.6 6.6 collective-permute-start.10
  259.3 17.8 %collective-permute-start.18 = (bf16[1,192,16,4]{1,2,3,0:T(8,128)(2,1)}, bf16[1,192,16,4]{1,2,3,0:T(8,128)(2,1)}, u32[]{:S(2)}, u32[]{:S(2)}) collective-permute-start(bf16[1,192,16,4]{1,2,3,0:T(8,128)(2,1)} %copy.161), channel_id=1, source_target_pairs={{0,1},{1,2},{2,3},{3,4},{4,5},{5,6},{6,7},{7,8},{8,9},{9,10},{10,1... | collective-permute-start | bytes 73736 | tf_op jit(solution)/shard_map/ppermute | solution.py:14
  265.0 44.3 %collective-permute-start.19 = (bf16[1,192,16,4]{1,2,3,0:T(8,128)(2,1)}, bf16[1,192,16,4]{1,2,3,0:T(8,128)(2,1)}, u32[]{:S(2)}, u32[]{:S(2)}) collective-permute-start(bf16[1,192,16,4]{1,2,3,0:T(8,128)(2,1)} %copy.164), channel_id=1, source_target_pairs={{0,127},{1,0},{2,1},{3,2},{4,3},{5,4},{6,5},{7,6},{8,7},{9,8},{10,... | collective-permute-start | bytes 73736 | tf_op jit(solution)/shard_map/ppermute | solution.py:14
  282.9 8.0 copy-start.10
  353.5 23.2 %collective-permute-start.13 = (bf16[1,192,16,4]{1,2,3,0:T(8,128)(2,1)S(1)}, bf16[1,192,16,4]{1,2,3,0:T(8,128)(2,1)S(1)}, u32[]{:S(2)}, u32[]{:S(2)}) collective-permute-start(bf16[1,192,16,4]{1,2,3,0:T(8,128)(2,1)S(1)} %copy.143), channel_id=1, source_target_pairs={{0,127},{1,0},{2,1},{3,2},{4,3},{5,4},{6,5},{7,6},{8,7},{9,8},{10,... | collective-permute-start | bytes 73736 | tf_op jit(solution)/shard_map/ppermute | solution.py:14
  363.3 13.9 %collective-permute-start.12 = (bf16[1,192,16,4]{1,2,3,0:T(8,128)(2,1)S(1)}, bf16[1,192,16,4]{1,2,3,0:T(8,128)(2,1)}, u32[]{:S(2)}, u32[]{:S(2)}) collective-permute-start(bf16[1,192,16,4]{1,2,3,0:T(8,128)(2,1)S(1)} %copy.142), channel_id=1, source_target_pairs={{0,1},{1,2},{2,3},{3,4},{4,5},{5,6},{6,7},{7,8},{8,9},{9,10},{10,1... | collective-permute-start | bytes 73736 | tf_op jit(solution)/shard_map/ppermute | solution.py:14
  369.2 16.3 %collective-permute-start.20 = (f32[1,128,4,72]{1,3,2,0:T(8,128)}, f32[1,128,4,72]{1,3,2,0:T(8,128)}, u32[]{:S(2)}, u32[]{:S(2)}) collective-permute-start(f32[1,128,4,72]{1,3,2,0:T(8,128)} %get-tuple-element.466), channel_id=1, source_target_pairs={{0,8},{1,9},{2,10},{3,11},{4,12},{5,13},{6,14},{7,15},{8,16},{9,17... | collective-permute-start | bytes 442376 | tf_op jit(solution)/shard_map/ppermute | solution.py:14
  372.0 17.1 %collective-permute-start.21 = (f32[1,128,4,72]{1,3,2,0:T(8,128)}, f32[1,128,4,72]{1,3,2,0:T(8,128)S(1)}, u32[]{:S(2)}, u32[]{:S(2)}) collective-permute-start(f32[1,128,4,72]{1,3,2,0:T(8,128)} %get-tuple-element.465), channel_id=1, source_target_pairs={{0,120},{1,121},{2,122},{3,123},{4,124},{5,125},{6,126},{7,127},{8... | collective-permute-start | bytes 442376 | tf_op jit(solution)/shard_map/ppermute | solution.py:14
  379.7 7.4 copy-start.19
  383.1 48.3 %collective-permute-start.15 = (bf16[1,192,4,136]{3,1,2,0:T(8,128)(2,1)}, bf16[1,192,4,136]{3,1,2,0:T(8,128)(2,1)}, u32[]{:S(2)}, u32[]{:S(2)}) collective-permute-start(bf16[1,192,4,136]{3,1,2,0:T(8,128)(2,1)} %broadcast_select_fusion.4), channel_id=1, source_target_pairs={{0,120},{1,121},{2,122},{3,123},{4,124},{5,125},{6,126},{7,127},{8... | collective-permute-start | bytes 626696 | tf_op jit(solution)/shard_map/ppermute | solution.py:14
  389.3 6.5 copy-start.46
  389.3 7.0 copy-start.44
  389.4 7.2 copy-start.6
  389.4 3.7 collective-permute-start.22
  390.4 41.0 %collective-permute-start.14 = (bf16[1,192,4,136]{3,1,2,0:T(8,128)(2,1)}, bf16[1,192,4,136]{3,1,2,0:T(8,128)(2,1)}, u32[]{:S(2)}, u32[]{:S(2)}) collective-permute-start(bf16[1,192,4,136]{3,1,2,0:T(8,128)(2,1)} %broadcast_select_fusion.7), channel_id=1, source_target_pairs={{0,8},{1,9},{2,10},{3,11},{4,12},{5,13},{6,14},{7,15},{8,16},{9,17... | collective-permute-start | bytes 626696 | tf_op jit(solution)/shard_map/ppermute | solution.py:14
  391.8 3.9 collective-permute-start.23
  407.4 11.2 %copy-start.21 = (f32[64,8,64]{2,0,1:T(8,128)S(1)}, f32[64,8,64]{2,0,1:T(8,128)}, u32[]{:S(2)}) copy-start(f32[64,8,64]{2,0,1:T(8,128)} %copy-done.20) | copy-start | bytes 393220
  411.0 12.1 %collective-permute-start.24 = (f32[1,64,4,72]{3,1,2,0:T(8,128)S(1)}, f32[1,64,4,72]{3,1,2,0:T(8,128)S(1)}, u32[]{:S(2)}, u32[]{:S(2)}) collective-permute-start(f32[1,64,4,72]{3,1,2,0:T(8,128)S(1)} %get-tuple-element.470), channel_id=1, source_target_pairs={{0,8},{1,9},{2,10},{3,11},{4,12},{5,13},{6,14},{7,15},{8,16},{9,17... | collective-permute-start | bytes 221192 | tf_op jit(solution)/shard_map/ppermute | solution.py:14
  411.2 12.1 %collective-permute-start.25 = (f32[1,64,4,72]{3,1,2,0:T(8,128)S(1)}, f32[1,64,4,72]{3,1,2,0:T(8,128)S(1)}, u32[]{:S(2)}, u32[]{:S(2)}) collective-permute-start(f32[1,64,4,72]{3,1,2,0:T(8,128)S(1)} %get-tuple-element.469), channel_id=1, source_target_pairs={{0,120},{1,121},{2,122},{3,123},{4,124},{5,125},{6,126},{7,127},{8... | collective-permute-start | bytes 221192 | tf_op jit(solution)/shard_map/ppermute | solution.py:14
  425.1 16.0 %collective-permute-start.26 = (bf16[1,64,8,4]{3,1,2,0:T(8,128)(2,1)S(1)}, bf16[1,64,8,4]{3,1,2,0:T(8,128)(2,1)S(1)}, u32[]{:S(2)}, u32[]{:S(2)}) collective-permute-start(bf16[1,64,8,4]{3,1,2,0:T(8,128)(2,1)S(1)} %get-tuple-element.478), channel_id=1, source_target_pairs={{0,1},{1,2},{2,3},{3,4},{4,5},{5,6},{6,7},{7,8},{8,9},{9,10},{10,1... | collective-permute-start | bytes 12296 | tf_op jit(solution)/shard_map/ppermute | solution.py:14
  425.4 9.3 %copy-start.32 = (bf16[9,64,192]{2,1,0:T(8,128)(2,1)S(1)}, bf16[9,64,192]{2,1,0:T(8,128)(2,1)}, u32[]{:S(2)}) copy-start(bf16[9,64,192]{2,1,0:T(8,128)(2,1)} %param.81) | copy-start | bytes 663556
  425.4 25.6 %collective-permute-start.27 = (bf16[1,64,8,4]{3,1,2,0:T(8,128)(2,1)}, bf16[1,64,8,4]{3,1,2,0:T(8,128)(2,1)S(1)}, u32[]{:S(2)}, u32[]{:S(2)}) collective-permute-start(bf16[1,64,8,4]{3,1,2,0:T(8,128)(2,1)} %get-tuple-element.477), channel_id=1, source_target_pairs={{0,127},{1,0},{2,1},{3,2},{4,3},{5,4},{6,5},{7,6},{8,7},{9,8},{10,... | collective-permute-start | bytes 12296 | tf_op jit(solution)/shard_map/ppermute | solution.py:14
  533.7 7.3 copy-start.36
  535.1 98.6 %collective-permute-start.28 = (f32[1,64,4,136]{3,1,2,0:T(8,128)}, f32[1,64,4,136]{3,1,2,0:T(8,128)}, u32[]{:S(2)}, u32[]{:S(2)}) collective-permute-start(f32[1,64,4,136]{3,1,2,0:T(8,128)} %get-tuple-element.460), channel_id=1, source_target_pairs={{0,8},{1,9},{2,10},{3,11},{4,12},{5,13},{6,14},{7,15},{8,16},{9,17... | collective-permute-start | bytes 417800 | tf_op jit(solution)/shard_map/ppermute | solution.py:14
  535.4 99.5 %collective-permute-start.29 = (f32[1,64,4,136]{3,1,2,0:T(8,128)}, f32[1,64,4,136]{3,1,2,0:T(8,128)}, u32[]{:S(2)}, u32[]{:S(2)}) collective-permute-start(f32[1,64,4,136]{3,1,2,0:T(8,128)} %get-tuple-element.459), channel_id=1, source_target_pairs={{0,120},{1,121},{2,122},{3,123},{4,124},{5,125},{6,126},{7,127},{8... | collective-permute-start | bytes 417800 | tf_op jit(solution)/shard_map/ppermute | solution.py:14
  548.0 82.6 %copy-start.26 = (f32[16,128,64]{1,2,0:T(8,128)S(1)}, f32[16,128,64]{1,2,0:T(8,128)}, u32[]{:S(2)}) copy-start(f32[16,128,64]{1,2,0:T(8,128)} %fusion.95) | copy-start | bytes 1572868
  645.0 5.4 collective-permute-start.30
  649.8 6.5 collective-permute-start.31
  (42 other events, 113.4 us)
Sparse Core Ops, SparseCore 0:
  649.4 258.6 all-reduce.3
where the time goes:
time: 935 us; the launch traced here: 921 us
  local copies, waits for them, and re-layouts  316 us (34%)
  waiting for transfers between devices  253 us (27%)
  matrix products  96.8 us (10%)
  starting transfers between devices  78.7 us (8%)
  blocking collectives  78.7 us (8%)
  other arithmetic  60.1 us (6%)
  between operations  36.9 us (4%)
    psum x1, waiting for transfers between devices, shards(): lax.psum((terms_first, terms_second, terms_third, terms_fourth, bias_firs...  246 us
    dynamic_update_slice x36, local copies, waits for them, and re-layouts, spread_back(): lax.dynamic_update_slice(summed, current + jnp.einsum('oc,mohw->mchw', ke...  161 us
    psum x1, blocking collectives, shards(): lax.psum((terms_first, terms_second, terms_third, terms_fourth, bias_firs...  78.7 us
    ppermute x32, starting transfers between devices, shifted(): lax.ppermute(array, axis, [(i, (i + by) % devices) for i in range(devices)])  78.7 us
    dot_general x36, matrix products, spread_back(): jnp.einsum('oc,mohw->mchw', kernel[3 * row_tap + col_tap], grad, preferre...  43.1 us
    scatter-add x6, local copies, waits for them, and re-layouts, return_columns(): summed.at[..., extent - margin:]  42.6 us
    unnamed x125, local copies, waits for them, and re-layouts  32.6 us
    dot_general x36, matrix products, convolve(): jnp.einsum('oc,mchw->mohw', kernel[3 * row_tap + col_tap], section, prefe...  30.5 us
  transfers between devices with their start and end apart: 33, of which 5 were waited for; matrix products, arithmetic and copies ran while one was open for 32% of the time, Pallas kernels for 0%

commit v1 on v0

v1 whole, which is shorter than its diff:
```python
import functools
import math

import jax
import jax.numpy as jnp
from jax import lax
from jax.experimental import pallas as pl
from jax.experimental.pallas import tpu as pltpu
from jax.sharding import PartitionSpec as P

MESH = pl.DeviceIdType.MESH
BF = jnp.bfloat16
F32 = jnp.float32

RIM = 4
TILE_ROW = 8
LANES = 128
ONES = 16

EXCHANGES = (
    ("fields", 64, 4, 1),
    ("pooled", 64, 4, 1),
    ("first", 64, 4, 1),
    ("second", 128, 4, 1),
    ("third", 128, 2, 1),
    ("b4c", 128, 2, 3),
    ("b4f", 64, 4, 3),
    ("b3", 128, 4, 3),
    ("b2", 64, 4, 3),
    ("b1", 64, 4, 3),
)
OFFSETS = (1, -1, 9, 7, -7, -9, 8, -8)
LAYERS = ((64, 64, 16, 128), (64, 128, 8, 64), (128, 128, 8, 64), (192, 64, 16, 128))


def iota(shape, dim):
    return lax.broadcasted_iota(jnp.int32, shape, dim)


def onehot(cond):
    return jnp.where(cond, 1.0, 0.0).astype(BF)


def mm(a, b):
    return jnp.dot(a, b, preferred_element_type=F32)


def mm_nt(a, b):
    return lax.dot_general(a, b, (((1,), (1,)), ((), ())), preferred_element_type=F32)


def split(values):
    high = values.astype(BF)
    low = (values - high.astype(F32)).astype(BF)
    return jnp.concatenate([high, low], axis=-1)


def cat(parts, axis):
    return parts[0] if len(parts) == 1 else jnp.concatenate(parts, axis=axis)


def log2(m):
    return m.bit_length() - 1


def column_pick(H, W, m, code_right, code_left, shape=(LANES, LANES)):
    lane = iota(shape, 1)
    code = jnp.where(lane < 64, code_right, code_left)
    idx = lane & 63
    row, col = idx >> log2(m), idx & (m - 1)
    col = jnp.where((code & 1) == 1, W - m + col, col)
    row = jnp.where((code >> 1) == 1, H - 1 - row, row)
    valid = idx < H * m
    return jnp.where(valid, row, -1), jnp.where(valid, col, -1)


def halo_target(H, m, code, row):
    w = iota((LANES, LANES), 1)
    picked = jnp.where((code & 1) == 1, H - m + row, row)
    flip = (code >> 1) == 1
    k = w - (LANES - m)
    left = jnp.where(flip, 64 + m * picked + (m - 1 - k), m * picked + k)
    right = jnp.where(flip, m * picked + (m - 1 - w), 64 + m * picked + w)
    return jnp.where(w >= LANES - m, left, jnp.where(w < m, right, -1))


def shift_matrix(W, d):
    source = iota((2 * LANES, 2 * LANES), 0)
    out = iota((2 * LANES, 2 * LANES), 1)
    j = out & (LANES - 1)
    minus = jnp.where(j >= d, j - d, 2 * LANES + j - d)
    plus = jnp.where(j + d < W, j + d, LANES + j + d - W)
    return onehot((source == jnp.where(out < LANES, minus, plus)) & (j < W))


def reversal(W, code, shape=(LANES, LANES)):
    u, w = iota(shape, 0), iota(shape, 1)
    flip = (code >> 1) == 1
    return (u == jnp.where(flip, W - 1 - w, w)) & (w < W)


def pick_rows_matrix(W, code):
    u = iota((2 * LANES, LANES), 0)
    w = iota((2 * LANES, LANES), 1)
    flip = (code >> 1) == 1
    hit = (u & (LANES - 1)) == jnp.where(flip, W - 1 - w, w)
    return onehot(hit & ((u >> 7) == (code & 1)) & (w < W))


def return_rows_matrix(W, code_upper, code_lower, last):
    u = iota((2 * LANES, LANES), 0)
    w = iota((2 * LANES, LANES), 1)
    code = jnp.where(u < LANES, code_upper, code_lower)
    flip = (code >> 1) == 1
    hit = (u & (LANES - 1)) == jnp.where(flip, W - 1 - w, w)
    return onehot(hit & ((code & 1) == last) & (w < W))


def rim_matrix(H, m, code_above, code_below, collapse):
    shape = (2 * LANES, LANES)
    u, lane = iota(shape, 0), iota(shape, 1)
    src = u & (LANES - 1)
    if collapse:
        src = ((src >> 3) << 1) + ((src & 3) >> 1)
    src = src + (u >> 7) * 1024
    idx = lane & 63
    row, k = idx >> log2(m), idx & (m - 1)
    leftward = lane < 64
    valid = idx < H * m
    parts = [onehot((src == (row + m) * m + k + jnp.where(leftward, 1024, 0)) & valid)]
    for code, base in ((code_above, 0), (code_below, H + m)):
        picked = jnp.where((code & 1) == 1, row - (H - m), row)
        flip = jnp.where((code >> 1) == 1, 1, 0)
        kk = jnp.where(flip == 1, m - 1 - k, k)
        left_side = jnp.where(leftward, 1 - flip, flip)
        hit = src == (picked + base) * m + kk + left_side * 1024
        parts.append(onehot(hit & valid & (picked >= 0) & (picked < m)))
    return jnp.concatenate(parts, axis=1)


def edge_matrix(H, d):
    u, v = iota((LANES, LANES), 0), iota((LANES, LANES), 1)
    row, k = v >> 2, v & 3
    parts = []
    for a in range(3):
        h = row - RIM - (a - 1) * d
        inside = (h >= 0) & (h < H)
        parts.append(onehot((u == 4 * h + (4 - d + k)) & inside & (k < d)))
        parts.append(onehot((u == 64 + 4 * h + (k - 4 + d)) & inside & (k >= 4 - d)))
    return jnp.concatenate(parts, axis=1)


def gelu_and_slope(x):
    cdf = 0.5 + 0.5 * lax.erf(x * math.sqrt(0.5))
    pdf = jnp.exp(-0.5 * x * x) * (1.0 / math.sqrt(2.0 * math.pi))
    return x * cdf, cdf + x * pdf


def stacked(values):
    return values.reshape(values.shape[0] * values.shape[1], values.shape[2])


def net_kernel(tiles, names, *refs):
    R = dict(zip(names, refs))
    tile = lax.axis_index("tile")
    ens = lax.axis_index("ens")

    def device(offset):
        return (ens, lax.rem(tile + (offset + tiles), tiles))

    copies = {}
    for x, (name, C, m, sent) in enumerate(EXCHANGES):
        listed = []
        for slot, offset in enumerate(OFFSETS):
            if slot < 6:
                which = 0 if sent == 1 else (0, 0, 2, 2, 1, 1)[slot]
                src = R["cs_" + name].at[which]
                dst = R["cr_" + name].at[slot]
            else:
                src = R["rs_" + name].at[slot - 6]
                dst = R["rr_" + name].at[slot - 6]
            listed.append(
                pltpu.make_async_remote_copy(
                    src_ref=src,
                    dst_ref=dst,
                    send_sem=R["send"].at[x, slot],
                    recv_sem=R["recv"].at[x, slot],
                    device_id=device(offset),
                    device_id_type=MESH,
                )
            )
        copies[name] = listed
    copies["codes"] = [
        pltpu.make_async_remote_copy(
            src_ref=R["code_rows"],
            dst_ref=R["code_near"].at[k],
            send_sem=R["send_code"].at[k],
            recv_sem=R["recv_code"].at[k],
            device_id=device(offset),
            device_id_type=MESH,
        )
        for k, offset in enumerate((8, -8))
    ]

    def start(name):
        for copy in copies[name]:
            copy.start()

    def arrive(name):
        for copy in copies[name]:
            copy.wait_recv()

    barrier = pltpu.get_barrier_semaphore()
    for offset in OFFSETS:
        pl.semaphore_signal(barrier, inc=1, device_id=device(offset), device_id_type=MESH)

    codes = [R["codes"][s] for s in range(4)]
    dil = [R["dil"][i] for i in range(4)]

    shifts = R["shifts"]
    for i, (_, _, _, W) in enumerate(LAYERS):
        shifts[i] = shift_matrix(W, dil[i])
    picks = R["picks"]
    PICK = {(16, 4): 0, (8, 4): 1, (8, 2): 2}
    for (H, m), where in PICK.items():
        _, col = column_pick(H, 128 if H == 16 else 64, m, codes[3], codes[2])
        picks[where] = onehot(iota((LANES, LANES), 0) == col)

    def pick_rows(H, m):
        row, _ = column_pick(H, 128 if H == 16 else 64, m, codes[3], codes[2], (1, LANES))
        return row

    for name, O, H in (("d4", 64, 16), ("d1", 64, 16), ("d3", 128, 8), ("d2", 128, 8)):
        R[name][0 : 2 * RIM] = jnp.zeros((2 * RIM, 3 * O, LANES), BF)
        R[name][2 * RIM + H : 4 * RIM + H] = jnp.zeros((2 * RIM, 3 * O, LANES), BF)
    for name, C, H in (("x4", 192, 16), ("x1", 64, 16), ("x3", 128, 8), ("x2", 64, 8)):
        R[name][:, 3 * C : 3 * C + ONES, :] = jnp.ones((H + 2 * RIM, ONES, LANES), BF)

    def columns_of(x_ref, H, m, C):
        row = pick_rows(H, m)
        total = jnp.zeros((C, LANES), F32)
        for g in range(H // 4):
            y = mm(stacked(x_ref[4 * g : 4 * g + 4]), picks[PICK[(H, m)]])
            for q in range(4):
                total = total + jnp.where(row == 4 * g + q, y[q * C : (q + 1) * C], 0.0)
        return total

    def send_forward(name, x_ref, H, W, m, C):
        R["cs_" + name][0] = columns_of(x_ref, H, m, C).astype(BF)
        both = jnp.concatenate([stacked(x_ref[0:m]), stacked(x_ref[H - m : H])], axis=1)
        for k, side in enumerate((1, 0)):
            rows = mm(both, pick_rows_matrix(W, codes[side])).astype(BF)
            R["rs_" + name][k] = rows.reshape(m, C, LANES)

    def halo_arrays(name):
        near = R["cr_" + name]
        low = iota((1, LANES), 1) < 64
        return [jnp.where(low, near[2 * i], near[2 * i + 1]) for i in range(3)]

    def halo_rows(Z, H, m, code, rows):
        lane = iota((LANES, LANES), 0)
        mats = cat([onehot(lane == halo_target(H, m, code, r)) for r in rows], 1)
        y = mm(Z, mats).astype(BF)
        return cat([y[:, LANES * q : LANES * (q + 1)] for q in range(len(rows))], 0)

    def fill(X3, r0, core, halo, C, S, offs, repeat):
        y = mm(jnp.concatenate([core, halo], axis=1), S).astype(BF)
        for q in range(core.shape[0] // C):
            part = slice(q * C, (q + 1) * C)
            for z in range(repeat):
                r = r0 + q * repeat + z
                X3[r, offs[0] : offs[0] + C, :] = y[part, :LANES]
                X3[r, offs[1] : offs[1] + C, :] = core[part]
                X3[r, offs[2] : offs[2] + C, :] = y[part, LANES:]

    def pad_and_shift(name, x_ref, H, m, C, layer, X3, offs, refine):
        Z, Zu, Zl = halo_arrays(name)
        S = shifts[layer]
        rr = R["rr_" + name]
        code_u = R["code_near"][0, 1:2, :]
        code_l = R["code_near"][1, 0:1, :]
        rep = 2 if refine else 1

        def prepare(core, halo):
            if not refine:
                return core, halo
            u, w = iota((LANES, LANES), 0), iota((LANES, LANES), 1)
            core = mm(core, onehot(u == (w >> 1))).astype(BF)
            near = jnp.where(w < 4, w >> 1, jnp.where(w >= LANES - 4, 64 + (w >> 1), -1))
            return core, mm(halo, onehot(u == near)).astype(BF)

        def body(g, carry):
            rows = [m * g + q for q in range(m)]
            core, halo = prepare(stacked(x_ref[pl.ds(m * g, m)]), halo_rows(Z, H, m, 0, rows))
            fill(X3, RIM + m * rep * g, core, halo, C, S, offs, rep)
            return carry

        lax.fori_loop(0, H // m, body, 0)
        core, halo = prepare(stacked(rr[0]), halo_rows(Zu, H, m, code_u, range(m)))
        fill(X3, 0, core, halo, C, S, offs, rep)
        core, halo = prepare(stacked(rr[1]), halo_rows(Zl, H, m, code_l, range(m)))
        fill(X3, RIM + H * rep, core, halo, C, S, offs, rep)

    def conv(Z3, width, K, d, rows, write):
        def body(i, carry):
            r = 2 * i
            taps = []
            for b in range(3):
                base = r + RIM + (b - 1) * d
                taps.append(
                    jnp.concatenate(
                        [Z3[base, 0:width, :], Z3[base + 1, 0:width, :]], axis=1
                    )
                )
            y = mm(K[...], jnp.concatenate(taps, axis=0))
            write(r, y[:, :LANES])
            write(r + 1, y[:, LANES:])
            return carry

        lax.fori_loop(0, rows // 2, body, 0)

    def weight_terms(X3, C, D3, O, d, rows, acc):
        n = 3 * C + ONES

        def body(i, carry):
            r = 4 * i
            lhs = jnp.concatenate([X3[r + q] for q in range(4)], axis=1)
            taps = []
            for a in range(3):
                base = r + RIM - (a - 1) * d
                taps.append(
                    jnp.concatenate([D3[base + q, O : 2 * O, :] for q in range(4)], axis=1)
                )
            if O == 64:
                taps.append(jnp.zeros((O, 4 * LANES), BF))
            y = mm_nt(lhs, jnp.concatenate(taps, axis=0))
            acc[0:n] = acc[0:n] + y
            return carry

        acc[0:n] = jnp.zeros((n, acc.shape[1]), F32)
        lax.fori_loop(0, rows // 4, body, 0)

    def spread_delta(x_ref, H, O, layer, D3):
        def body(g, carry):
            core = stacked(x_ref[pl.ds(4 * g, 4)])
            y = mm(core, shifts[layer, 0:LANES, :]).astype(BF)
            for q in range(4):
                part = slice(q * O, (q + 1) * O)
                D3[2 * RIM + 4 * g + q, 0:O, :] = y[part, :LANES]
                D3[2 * RIM + 4 * g + q, O : 2 * O, :] = core[part]
                D3[2 * RIM + 4 * g + q, 2 * O : 3 * O, :] = y[part, LANES:]
            return carry

        lax.fori_loop(0, H // 4, body, 0)

    def rims_of(x_ref, H, W, O, layer, K):
        row, col = column_pick(H, W, RIM, 1, 0, (1, LANES))
        _, col_full = column_pick(H, W, RIM, 1, 0)
        pick = onehot(iota((LANES, LANES), 0) == col_full)
        edges = jnp.zeros((O, LANES), F32)
        for g in range(H // 4):
            y = mm(stacked(x_ref[4 * g : 4 * g + 4]), pick)
            for q in range(4):
                edges = edges + jnp.where(row == 4 * g + q, y[q * O : (q + 1) * O], 0.0)
        e = mm(edges.astype(BF), edge_matrix(H, dil[layer])).astype(BF)
        none = jnp.zeros((O, LANES), BF)
        blocks = []
        for b in range(3):
            a = 2 - b
            right = e[:, 2 * a * LANES : (2 * a + 1) * LANES]
            left = e[:, (2 * a + 1) * LANES : (2 * a + 2) * LANES]
            blocks.append(jnp.concatenate([right, none], axis=1))
            blocks.append(jnp.zeros((O, 2 * LANES), BF))
            blocks.append(jnp.concatenate([none, left], axis=1))
        return mm(K[...], jnp.concatenate(blocks, axis=0)).astype(BF)

    def send_backward(name, rims, G, c0, C, H, m, collapse=False):
        code_u = R["code_near"][0, 1:2, :]
        code_l = R["code_near"][1, 0:1, :]
        y = mm(rims, rim_matrix(H, m, code_u, code_l, collapse)).astype(BF)
        for k in range(3):
            R["cs_" + name][k] = y[:, k * LANES : (k + 1) * LANES]
        R["rs_" + name][0] = G[H + m : H + 2 * m, c0 : c0 + C, :].astype(BF)
        R["rs_" + name][1] = G[0:m, c0 : c0 + C, :].astype(BF)

    def fold(name, G, c0, C, H, W, m, write):
        near = R["cr_" + name]
        rr = R["rr_" + name]
        low = iota((1, LANES), 1) < 64
        back = jnp.where(
            low,
            near[1].astype(F32) + near[3].astype(F32) + near[5].astype(F32),
            near[0].astype(F32) + near[2].astype(F32) + near[4].astype(F32),
        )
        row = pick_rows(H, m)
        both = jnp.concatenate([stacked(rr[0]), stacked(rr[1])], axis=1)
        first = mm(both, return_rows_matrix(W, codes[0], codes[1], 0))
        last = mm(both, return_rows_matrix(W, codes[0], codes[1], 1))
        pick = picks[PICK[(H, m)]]
        for g in range(H // m):
            masked = [jnp.where(row == m * g + q, back, 0.0).astype(BF) for q in range(m)]
            y = mm_nt(cat(masked, 0), pick)
            if g == 0:
                y = y + first
            if g == H // m - 1:
                y = y + last
            for q in range(m):
                h = m * g + q
                write(h, G[h + m, c0 : c0 + C, :] + y[q * C : (q + 1) * C])

    send_forward("fields", R["fields"], 16, 128, 4, 64)
    pl.semaphore_wait(barrier, len(OFFSETS))
    start("codes")
    start("fields")

    cot = R["cot"]
    spread_delta(cot, 16, 64, 3, R["d4"])
    G4 = R["g4"]

    def write_g4(r, v):
        G4[r] = v

    conv(R["d4"], 192, R["kt4"], dil[3], 24, write_g4)
    rims4 = rims_of(cot, 16, 128, 64, 3, R["kt4"])
    arrive("codes")
    G4c = R["g4c"]
    u, w = iota((2 * LANES, LANES), 0), iota((2 * LANES, LANES), 1)
    pool = onehot(((u & (LANES - 1)) >> 1) == w)
    for g in range(3):
        pairs = [G4[8 * g + 2 * q, 0:128, :] + G4[8 * g + 2 * q + 1, 0:128, :] for q in range(4)]
        y = mm(split(cat(pairs, 0)), pool)
        G4c[4 * g : 4 * g + 4] = y.reshape(4, 128, LANES)
    send_backward("b4c", rims4[0:128], G4c, 0, 128, 8, 2, True)
    start("b4c")
    send_backward("b4f", rims4[128:192], G4, 128, 64, 16, 4)
    start("b4f")

    arrive("fields")
    pad_and_shift("fields", R["fields"], 16, 4, 64, 0, R["x1"], (0, 64, 128), False)
    first_act, slope1 = R["first_act"], R["slope1"]

    def write_first(r, v):
        act, slope = gelu_and_slope(v + R["off1"][...])
        first_act[r] = act.astype(BF)
        slope1[r] = slope

    conv(R["x1"], 192, R["kf1"], dil[0], 16, write_first)
    pooled = R["pooled"]
    quarter = jnp.where(((u & (LANES - 1)) >> 1) == w, 0.25, 0.0).astype(BF)
    for g in range(2):
        lhs = cat(
            [
                jnp.concatenate([first_act[8 * g + 2 * q], first_act[8 * g + 2 * q + 1]], axis=1)
                for q in range(4)
            ],
            0,
        )
        pooled[4 * g : 4 * g + 4] = mm(lhs, quarter).astype(BF).reshape(4, 64, LANES)
    send_forward("pooled", pooled, 8, 64, 4, 64)
    start("pooled")
    send_forward("first", first_act, 16, 128, 4, 64)
    start("first")

    arrive("b4c")
    arrive("b4f")
    coarse, skip = R["coarse"], R["skip"]

    def write_coarse(r, v):
        coarse[r] = v

    def write_skip(r, v):
        skip[r] = v

    fold("b4c", G4c, 0, 128, 8, 64, 2, write_coarse)
    fold("b4f", G4, 128, 64, 16, 128, 4, write_skip)

    arrive("pooled")
    pad_and_shift("pooled", pooled, 8, 4, 64, 1, R["x2"], (0, 64, 128), False)
    second_act, slope2 = R["second_act"], R["slope2"]
    inside = iota((1, LANES), 1) < 64

    def write_second(r, v):
        act, slope = gelu_and_slope(v + R["off2"][...])
        second_act[r] = jnp.where(inside, act, 0.0).astype(BF)
        slope2[r] = jnp.where(inside, slope, 0.0)

    conv(R["x2"], 192, R["kf2"], dil[1], 8, write_second)
    send_forward("second", second_act, 8, 64, 4, 128)
    start("second")

    arrive("first")
    pad_and_shift("first", first_act, 16, 4, 64, 3, R["x4"], (128, 320, 512), False)

    arrive("second")
    pad_and_shift("second", second_act, 8, 4, 128, 2, R["x3"], (0, 128, 256), False)
    third_act, delta3 = R["third_act"], R["delta3"]

    def write_third(r, v):
        act, slope = gelu_and_slope(v + R["off3"][...])
        third_act[r] = jnp.where(inside, act, 0.0).astype(BF)
        delta3[r] = jnp.where(inside, coarse[r] * slope, 0.0).astype(BF)

    conv(R["x3"], 384, R["kf3"], dil[2], 8, write_third)
    send_forward("third", third_act, 8, 64, 2, 128)
    start("third")
    spread_delta(delta3, 8, 128, 2, R["d3"])
    G3 = R["g3"]

    def write_g3(r, v):
        G3[r] = v

    conv(R["d3"], 384, R["kt3"], dil[2], 16, write_g3)
    send_backward("b3", rims_of(delta3, 8, 64, 128, 2, R["kt3"]), G3, 0, 128, 8, 4)
    start("b3")

    weight_terms(R["x3"], 128, R["d3"], 128, dil[2], 16, R["w3"])
    arrive("third")
    pad_and_shift("third", third_act, 8, 2, 128, 3, R["x4"], (0, 192, 384), True)

    arrive("b3")
    delta2 = R["delta2"]

    def write_delta2(r, v):
        delta2[r] = (v * slope2[r]).astype(BF)

    fold("b3", G3, 0, 128, 8, 64, 4, write_delta2)
    spread_delta(delta2, 8, 128, 1, R["d2"])
    G2 = R["g2"]

    def write_g2(r, v):
        G2[r] = v

    conv(R["d2"], 384, R["kt2"], dil[1], 16, write_g2)
    send_backward("b2", rims_of(delta2, 8, 64, 128, 1, R["kt2"]), G2, 0, 64, 8, 4)
    start("b2")

    state = R["state"]

    def write_state(r, v):
        state[r] = (v + R["off4"][...]).astype(BF)

    conv(R["x4"], 576, R["kf4"], dil[3], 16, write_state)
    weight_terms(R["x2"], 64, R["d2"], 128, dil[1], 16, R["w2"])

    arrive("b2")
    delta1 = R["delta1"]
    repeat = jnp.where((u & (LANES - 1)) == (w >> 1), 0.25, 0.0).astype(BF)

    def write_delta1(r, v):
        wide = mm(split(v), repeat)
        for z in range(2):
            delta1[2 * r + z] = ((skip[2 * r + z] + wide) * slope1[2 * r + z]).astype(BF)

    fold("b2", G2, 0, 64, 8, 64, 4, write_delta1)
    spread_delta(delta1, 16, 64, 0, R["d1"])
    G1 = R["g1"]

    def write_g1(r, v):
        G1[r] = v

    conv(R["d1"], 192, R["kt1"], dil[0], 24, write_g1)
    send_backward("b1", rims_of(delta1, 16, 128, 64, 0, R["kt1"]), G1, 0, 64, 16, 4)
    start("b1")

    weight_terms(R["x4"], 192, R["d4"], 64, dil[3], 24, R["w4"])
    weight_terms(R["x1"], 64, R["d1"], 64, dil[0], 24, R["w1"])
    pay = R["pay"]
    at = 0
    for name, C, chunks in PAYLOAD:
        n = 3 * C + ONES
        for k in range(chunks):
            pay[at : at + n, :] = R[name][0:n, k * LANES : (k + 1) * LANES].astype(BF)
            at += n
    pay[at:, :] = jnp.zeros((pay.shape[0] - at, LANES), BF)

    arrive("b1")
    out = R["grad"]

    def write_out(r, v):
        out[r] = v

    fold("b1", G1, 0, 64, 16, 128, 4, write_out)

    for listed in copies.values():
        for copy in listed:
            copy.wait_send()


PAYLOAD = (("w4", 192, 2), ("w3", 128, 3), ("w2", 64, 3), ("w1", 64, 2))
PAY_ROWS = sum((3 * C + ONES) * chunks for _, C, chunks in PAYLOAD)


def run_net(tiles, pay_rows, operands):
    V = pltpu.VMEM
    scratch = [
        ("shifts", V((4, 256, 256), BF)),
        ("picks", V((3, LANES, LANES), BF)),
        ("x1", V((24, 192 + ONES, LANES), BF)),
        ("x2", V((16, 192 + ONES, LANES), BF)),
        ("x3", V((16, 384 + ONES, LANES), BF)),
        ("x4", V((24, 576 + ONES, LANES), BF)),
        ("d1", V((32, 192, LANES), BF)),
        ("d2", V((24, 384, LANES), BF)),
        ("d3", V((24, 384, LANES), BF)),
        ("d4", V((32, 192, LANES), BF)),
        ("g1", V((24, 64, LANES), F32)),
        ("g2", V((16, 64, LANES), F32)),
        ("g3", V((16, 128, LANES), F32)),
        ("g4", V((24, 192, LANES), F32)),
        ("g4c", V((12, 128, LANES), F32)),
        ("first_act", V((16, 64, LANES), BF)),
        ("slope1", V((16, 64, LANES), F32)),
        ("pooled", V((8, 64, LANES), BF)),
        ("second_act", V((8, 128, LANES), BF)),
        ("slope2", V((8, 128, LANES), F32)),
        ("third_act", V((8, 128, LANES), BF)),
        ("coarse", V((8, 128, LANES), F32)),
        ("skip", V((16, 64, LANES), F32)),
        ("delta1", V((16, 64, LANES), BF)),
        ("delta2", V((8, 128, LANES), BF)),
        ("delta3", V((8, 128, LANES), BF)),
        ("w1", V((208, 256), F32)),
        ("w2", V((208, 384), F32)),
        ("w3", V((400, 384), F32)),
        ("w4", V((592, 256), F32)),
        ("code_near", V((2, 8, LANES), jnp.int32)),
        ("send", pltpu.SemaphoreType.DMA((len(EXCHANGES), 8))),
        ("recv", pltpu.SemaphoreType.DMA((len(EXCHANGES), 8))),
        ("send_code", pltpu.SemaphoreType.DMA((2,))),
        ("recv_code", pltpu.SemaphoreType.DMA((2,))),
    ]
    for name, C, m, sent in EXCHANGES:
        scratch += [
            ("cs_" + name, V((sent, C, LANES), BF)),
            ("rs_" + name, V((2, m, C, LANES), BF)),
            ("cr_" + name, V((6, C, LANES), BF)),
            ("rr_" + name, V((2, m, C, LANES), BF)),
        ]
    names = [n for n, _ in operands] + ["state", "grad", "pay"] + [n for n, _ in scratch]
    smem = pl.BlockSpec(memory_space=pltpu.SMEM)
    vmem = pl.BlockSpec(memory_space=pltpu.VMEM)
    return pl.pallas_call(
        functools.partial(net_kernel, tiles, names),
        out_shape=(
            jax.ShapeDtypeStruct((16, 64, LANES), BF),
            jax.ShapeDtypeStruct((16, 64, LANES), F32),
            jax.ShapeDtypeStruct((pay_rows, LANES), BF),
        ),
        in_specs=[smem if n in ("codes", "dil") else vmem for n, _ in operands],
        out_specs=(vmem, vmem, vmem),
        scratch_shapes=[s for _, s in scratch],
        compiler_params=pltpu.CompilerParams(
            collective_id=0, has_side_effects=True, vmem_limit_bytes=56 * 2**20
        ),
        name="net",
    )(*[v for _, v in operands])


def sum_kernel(sizes, scale, pay, out, from_core, half, buf_xy, buf_z, res, s1, r1, s2, r2, s3, r3, s4, r4, s5, r5):
    n_ens, n_xy, n_low = sizes
    n_z = n_ens * n_low
    ens, tile = lax.axis_index("ens"), lax.axis_index("tile")
    xy = lax.div(tile, 2 * n_low)
    low = lax.div(lax.rem(tile, 2 * n_low), 2)
    core = lax.rem(tile, 2)
    z = ens * n_low + low

    def at(z_, xy_, core_):
        return (lax.div(z_, n_low), (xy_ * n_low + lax.rem(z_, n_low)) * 2 + core_)

    def xy_peer(k):
        return lax.rem(xy + k, n_xy)

    def z_peer(k):
        return lax.rem(z + k, n_z)

    barrier = pltpu.get_barrier_semaphore()

    def greet(device):
        pl.semaphore_signal(barrier, inc=1, device_id=device, device_id_type=MESH)

    greet(at(z, xy, 1 - core))
    for k in range(1, n_xy):
        greet(at(z, xy_peer(k), core))
    for k in range(1, n_z):
        greet(at(z_peer(k), xy, core))
    pl.semaphore_wait(barrier, 1 + (n_xy - 1) + (n_z - 1))

    def remote(src, dst, send, recv, device):
        return pltpu.make_async_remote_copy(
            src_ref=src, dst_ref=dst, send_sem=send, recv_sem=recv, device_id=device, device_id_type=MESH
        )

    pair = remote(pay.at[1 - core], from_core, s1, r1, at(z, xy, 1 - core))
    pair.start()
    pair.wait()

    def add(p, carry):
        half[p] = (pay[core, p].astype(F32) + from_core[p].astype(F32)).astype(BF)
        return carry

    lax.fori_loop(0, n_xy, add, 0)

    def xy_copy(k):
        p = xy_peer(k)
        return remote(half.at[p], buf_xy.at[xy], s2.at[k], r2.at[xy], at(z, p, core))

    def xy_arrival(k):
        p = xy_peer(k)
        return remote(half.at[p], buf_xy.at[p], s2.at[k], r2.at[p], at(z, p, core))

    for k in range(1, n_xy):
        xy_copy(k).start()
    buf_xy[xy] = half[xy]
    for k in range(1, n_xy):
        xy_arrival(k).wait_recv()
    total = buf_xy[0].astype(F32)
    for p in range(1, n_xy):
        total = total + buf_xy[p].astype(F32)
    buf_z[z] = total.astype(BF)

    def z_copy(k):
        return remote(buf_z.at[z], buf_z.at[z], s3.at[k], r3.at[z], at(z_peer(k), xy, core))

    def z_arrival(k):
        p = z_peer(k)
        return remote(buf_z.at[p], buf_z.at[p], s3.at[k], r3.at[p], at(p, xy, core))

    for k in range(1, n_z):
        z_copy(k).start()
    for k in range(1, n_z):
        z_arrival(k).wait_recv()
    total = buf_z[0].astype(F32)
    for p in range(1, n_z):
        total = total + buf_z[p].astype(F32)
    res[core, xy] = (total * scale).astype(BF)

    def back_copy(k):
        return remote(res.at[core, xy], res.at[core, xy], s4.at[k], r4.at[xy], at(z, xy_peer(k), core))

    def back_arrival(k):
        p = xy_peer(k)
        return remote(res.at[core, p], res.at[core, p], s4.at[k], r4.at[p], at(z, p, core))

    for k in range(1, n_xy):
        back_copy(k).start()
    for k in range(1, n_xy):
        back_arrival(k).wait_recv()
    other = remote(res.at[core], res.at[core], s5, r5, at(z, xy, 1 - core))
    other.start()
    theirs = remote(res.at[1 - core], res.at[1 - core], s5, r5, at(z, xy, 1 - core))
    theirs.wait_recv()
    out[...] = res[...].astype(F32)
    other.wait_send()
    for k in range(1, n_xy):
        xy_copy(k).wait_send()
        back_copy(k).wait_send()
    for k in range(1, n_z):
        z_copy(k).wait_send()


def run_sum(sizes, scale, pay):
    n_ens, n_xy, n_low = sizes
    n_z = n_ens * n_low
    _, _, q, _ = pay.shape
    V, D = pltpu.VMEM, pltpu.SemaphoreType.DMA
    vmem = pl.BlockSpec(memory_space=pltpu.VMEM)
    return pl.pallas_call(
        functools.partial(sum_kernel, sizes, scale),
        out_shape=jax.ShapeDtypeStruct(pay.shape, F32),
        in_specs=[vmem],
        out_specs=vmem,
        scratch_shapes=[
            V((n_xy, q, LANES), BF),
            V((n_xy, q, LANES), BF),
            V((n_xy, q, LANES), BF),
            V((n_z, q, LANES), BF),
            V((2, n_xy, q, LANES), BF),
            D, D, D((n_xy,)), D((n_xy,)), D((n_z,)), D((n_z,)), D((n_xy,)), D((n_xy,)), D, D,
        ],
        compiler_params=pltpu.CompilerParams(
            collective_id=1, has_side_effects=True, vmem_limit_bytes=48 * 2**20
        ),
        name="total",
    )(pay)


def shards(
    tiles,
    members,
    fields,
    cotangent,
    kernel_first,
    kernel_second,
    kernel_third,
    closing_filter_weights,
    offset_first,
    offset_second,
    offset_third,
    closing_shift_values,
    codes,
    filter_stride_spread,
):
    def forward_weights(k):
        return jnp.transpose(k, (1, 0, 2)).reshape(k.shape[1], 9 * k.shape[2])

    def backward_weights(k):
        return jnp.transpose(k[::-1], (2, 0, 1)).reshape(k.shape[2], 9 * k.shape[1])

    kernels = (kernel_first, kernel_second, kernel_third, closing_filter_weights)
    offsets = (offset_first, offset_second, offset_third, closing_shift_values)
    code_rows = jnp.broadcast_to(jnp.concatenate([codes[0], codes[0]])[:, None], (8, LANES))
    operands = [
        ("codes", codes[0]),
        ("dil", filter_stride_spread),
        ("code_rows", code_rows),
        ("fields", jnp.swapaxes(fields[0, 0], 0, 1)),
        ("cot", jnp.swapaxes(cotangent[0, 0], 0, 1)),
    ]
    for i in range(4):
        operands.append((f"kf{i + 1}", forward_weights(kernels[i])))
        operands.append((f"kt{i + 1}", backward_weights(kernels[i])))
        operands.append((f"off{i + 1}", offsets[i][:, None]))
    n_low = 4
    n_xy = tiles // (2 * n_low)
    pieces = 2 * n_xy
    q = -(-PAY_ROWS // (pieces * 16)) * 16
    state, grad, pay = run_net(tiles, q * pieces, operands)
    H, W = fields.shape[3], fields.shape[4]
    scale = 1.0 / math.sqrt(members * tiles * H * W)
    res = run_sum((members, n_xy, n_low), scale, pay.reshape(2, n_xy, q, LANES))
    res = res.reshape(q * pieces, LANES)
    weights, biases = {}, {}
    at = 0
    for name, C, chunks in PAYLOAD:
        n = 3 * C + ONES
        O = 64 if chunks == 2 else 128
        block = jnp.concatenate([res[at + k * n : at + (k + 1) * n] for k in range(chunks)], axis=1)
        at += n * chunks
        body = block[: 3 * C, : 3 * O].reshape(3, C, 3, O)
        weights[name] = jnp.transpose(body, (2, 0, 3, 1)).reshape(9, O, C)
        biases[name] = block[3 * C, O : 2 * O]
    return (
        jnp.swapaxes(state, 0, 1)[None, None],
        jnp.swapaxes(grad, 0, 1)[None, None],
        weights["w1"],
        weights["w2"],
        weights["w3"],
        weights["w4"],
        biases["w1"],
        biases["w2"],
        biases["w3"],
        biases["w4"],
    )


def solution(mesh):
    big = P("ens", "tile", None, None, None)
    in_specs = (big, big) + (P(),) * 8 + (P("tile", None), P())
    out_specs = (big, big) + (P(),) * 8
    body = functools.partial(shards, mesh.shape["tile"], mesh.shape["ens"])
    return jax.shard_map(body, mesh=mesh, in_specs=in_specs, out_specs=out_specs, check_vma=False)
```

time: 935 us -> 134 us (0.14); the launches traced: 921 us -> 134 us
  local copies, waits for them, and re-layouts: 316 us -> 28 us
  waiting for transfers between devices: 253 us -> 0 us
  Pallas kernels: 0 us -> 104 us
  matrix products: 96.8 us -> 0 us
  blocking collectives: 78.7 us -> 0 us
  starting transfers between devices: 78.7 us -> 0 us
  other arithmetic: 60.1 us -> 0.93 us
  between operations: 36.9 us -> 0.79 us
    psum x1 -> x0, waiting for transfers between devices: 246 us -> none  [shards(): lax.psum((terms_first, terms_second, terms_third, terms_fourth, bias_firs...]
    dynamic_update_slice x36 -> x0, local copies, waits for them, and re-layouts: 161 us -> none  [spread_back(): lax.dynamic_update_slice(summed, current + jnp.einsum('oc,mohw->mchw', ke...]
    pallas_call x0 -> x2, Pallas kernels: none -> 104 us  [the longest x1 69.9 us: run_net(): pl.pallas_call(functools.partial(net_kernel, tiles, names), out_shape=(ja...]
    dot_general x108 -> x0, matrix products: 96.8 us -> none  [the longest x36 43.1 us: spread_back(): jnp.einsum('oc,mohw->mchw', kernel[3 * row_tap + col_tap], grad, preferre...]
    psum x1 -> x0, blocking collectives: 78.7 us -> none  [shards(): lax.psum((terms_first, terms_second, terms_third, terms_fourth, bias_firs...]
    ppermute x32 -> x0, starting transfers between devices: 78.7 us -> none  [shifted(): lax.ppermute(array, axis, [(i, (i + by) % devices) for i in range(devices)])]
    scatter-add x12 -> x0, local copies, waits for them, and re-layouts: 68.8 us -> none  [the longest x6 42.6 us: return_columns(): summed.at[..., extent - margin:]]
    unnamed x125 -> x13, local copies, waits for them, and re-layouts: 32.6 us -> 4.28 us
  transfers between devices with their start and end apart: 33 -> 0, of which waited for: 5 -> 0; matrix products, arithmetic and copies ran while one was open for 32% -> 0% of each run, Pallas kernels for 0% -> 0%
where the time goes in v1:
time: 134 us
  Pallas kernels  104 us (78%)
  local copies, waits for them, and re-layouts  28 us (21%)
    pallas_call x1, Pallas kernels, run_net(): pl.pallas_call(functools.partial(net_kernel, tiles, names), out_shape=(ja...  69.9 us
    pallas_call x1, Pallas kernels, run_sum(): pl.pallas_call(functools.partial(sum_kernel, sizes, scale), out_shape=jax...  34.5 us
    broadcast_in_dim x4, local copies, waits for them, and re-layouts, shards(): operands.append((f'off{i + 1}', offsets[i][:, None]))  5.47 us
    reshape x4, local copies, waits for them, and re-layouts, forward_weights(): return jnp.transpose(k, (1, 0, 2)).reshape(k.shape[1], 9 * k.shape[2])  4.42 us
    unnamed x13, local copies, waits for them, and re-layouts  4.28 us
    reshape x4, local copies, waits for them, and re-layouts, backward_weights(): return jnp.transpose(k[::-1], (2, 0, 1)).reshape(k.shape[2], 9 * k.shape[1])  4.11 us
    transpose x4, local copies, waits for them, and re-layouts, shards(): weights[name] = jnp.transpose(body, (2, 0, 3, 1)).reshape(9, O, C)  3.61 us

profile of v1, /device:TPU:1, one launch (start us, length us, event | category | flops | bytes accessed | tf_op | source)
XLA Modules:
  0.0 134.2 jit_solution(1764776892845928316)
XLA Ops:
  0.6 0.0 copy-start.2
  0.7 0.8 pad_add_fusion
  1.5 0.7 broadcast_in_dim.24.refs_2_
  2.1 1.3 %copy.69.refs_7_ = f32[64,1]{1,0:T(8,128)} copy(f32[64,1]{0,1:T(1,128)} %bitcast.87) | data formatting | bytes 512 | tf_op jit(solution)/shard_map/broadcast_in_dim | solution.py:823
  3.5 1.4 %copy.76.refs_16_ = f32[64,1]{1,0:T(8,128)} copy(f32[64,1]{0,1:T(1,128)} %bitcast.88) | data formatting | bytes 512 | tf_op jit(solution)/shard_map/broadcast_in_dim | solution.py:823
  4.8 1.4 %copy.71.refs_10_ = f32[128,1]{1,0:T(8,128)} copy(f32[128,1]{0,1:T(1,128)} %bitcast.89) | data formatting | bytes 1024 | tf_op jit(solution)/shard_map/broadcast_in_dim | solution.py:823
  6.2 1.4 %copy.74.refs_13_ = f32[128,1]{1,0:T(8,128)} copy(f32[128,1]{0,1:T(1,128)} %bitcast.90) | data formatting | bytes 1024 | tf_op jit(solution)/shard_map/broadcast_in_dim | solution.py:823
  7.6 1.0 copy.63
  8.6 0.0 copy-start.1
  8.7 0.8 copy.67.refs_5_
  9.4 0.9 rev.12
  10.3 0.8 copy.68.refs_6_
  11.1 1.6 %copy_bitcast_fusion.2.refs_9_ = bf16[64,1152]{1,0:T(8,128)(2,1)} fusion(bf16[9,128,64]{1,2,0:T(8,128)(2,1)} %param.15), kind=kLoop, calls=%fused_computation.8 | loop fusion | bytes 294912 | tf_op jit(solution)/shard_map/reshape | solution.py:808
  12.7 1.7 %copy.70.refs_8_ = bf16[128,576]{1,0:T(8,128)(2,1)} copy(bf16[128,576]{0,1:T(8,128)(2,1)} %bitcast.78) | data formatting | bytes 294912 | tf_op jit(solution)/shard_map/reshape | solution.py:805
  14.4 0.0 copy-done.2
  14.4 0.9 copy.73.refs_12_
  15.3 0.0 copy-start.3
  15.3 0.0 copy-start.4
  15.3 0.2 copy.65
  15.5 0.9 copy.72.refs_11_
  16.4 0.0 copy-done.1
  16.5 0.9 copy.75.refs_15_
  17.3 0.2 copy.66
  17.5 1.1 reshape.81.refs_14_
  18.6 0.0 copy-done.3
  18.6 0.0 copy-done.4
  18.6 0.9 copy_bitcast_fusion
  19.5 69.9 %net.1 = (bf16[16,64,128]{2,1,0:T(8,128)(2,1)}, f32[16,64,128]{2,1,0:T(8,128)}, bf16[3584,128]{1,0:T(8,128)(2,1)}) custom-call(s32[4]{0:T(128)} %bitcast.92, s32[4]{0:T(128)} %refs_1_.1, s32[8,128]{1,0:T(8,128)} %broadcast_in_dim.24.refs_2_, bf16[16,64,128]{2,1,0:T(8,128)(2,1)} %get-tuple-element.61.refs_3_, bf16[16,64,128]{2,1,0:T(8,128)(2,1)} %get-tuple-element.60.refs_4_, ...), custom_call_target="tpu_custom_call" | custom-call | tf_op jit(solution)/shard_map/net/pallas_call | solution.py:642
  89.5 0.0 copy-start
  89.5 1.9 %copy.82 = bf16[1,1,64,16,128]{4,3,2,1,0:T(8,128)(2,1)} copy(bf16[1,1,64,16,128]{4,2,3,1,0:T(8,128)(2,1)} %bitcast.86) | data formatting | bytes 524288
  91.4 2.1 %copy.83 = f32[1,1,64,16,128]{4,3,2,1,0:T(8,128)} copy(f32[1,1,64,16,128]{4,2,3,1,0:T(8,128)} %bitcast.83) | data formatting | bytes 1048576
  93.5 0.0 copy-done
  93.5 34.5 %total.1 = f32[2,16,112,128]{3,2,1,0:T(8,128)S(1)} custom-call(bf16[2,16,112,128]{3,2,1,0:T(8,128)(2,1)S(1)} %bitcast.68), custom_call_target="tpu_custom_call" | custom-call | tf_op jit(solution)/shard_map/total/pallas_call | solution.py:768
  128.1 0.6 slice_bitcast_fusion
  128.7 0.5 slice_bitcast_fusion.1
  129.2 0.1 reshape.87
  129.4 0.7 copy.78
  130.1 0.2 reshape.85
  130.3 0.9 copy.77
  131.4 0.2 copy.80
  131.6 0.2 reshape.89
  131.8 1.1 copy.79
  132.9 0.3 reshape.91
  133.2 0.9 copy.81
  (9 shorter events, 0.3 us)
Async XLA Ops:
  0.6 13.8 %copy-start.2 = (bf16[9,128,128]{2,1,0:T(8,128)(2,1)S(1)}, bf16[9,128,128]{2,1,0:T(8,128)(2,1)}, u32[]{:S(2)}) copy-start(bf16[9,128,128]{2,1,0:T(8,128)(2,1)} %param.16) | copy-start | bytes 884740
  8.6 7.8 %copy-start.1 = (bf16[9,64,192]{2,1,0:T(8,128)(2,1)S(1)}, bf16[9,64,192]{2,1,0:T(8,128)(2,1)}, u32[]{:S(2)}) copy-start(bf16[9,64,192]{2,1,0:T(8,128)(2,1)} %param.17) | copy-start | bytes 663556
  15.3 3.2 %copy-start.3 = (bf16[1,1,64,16,128]{4,3,2,1,0:T(8,128)(2,1)S(1)}, bf16[1,1,64,16,128]{4,3,2,1,0:T(8,128)(2,1)}, u32[]{:S(2)}) copy-start(bf16[1,1,64,16,128]{4,3,2,1,0:T(8,128)(2,1)} %param.13) | copy-start | bytes 786436
  15.3 3.2 %copy-start.4 = (bf16[1,1,64,16,128]{4,3,2,1,0:T(8,128)(2,1)S(1)}, bf16[1,1,64,16,128]{4,3,2,1,0:T(8,128)(2,1)}, u32[]{:S(2)}) copy-start(bf16[1,1,64,16,128]{4,3,2,1,0:T(8,128)(2,1)} %param.12) | copy-start | bytes 786436
  89.5 4.1 %copy-start = (bf16[3584,128]{1,0:T(8,128)(2,1)S(1)}, bf16[3584,128]{1,0:T(8,128)(2,1)}, u32[]{:S(2)}) copy-start(bf16[3584,128]{1,0:T(8,128)(2,1)} %get-tuple-element.15) | copy-start | bytes 2752516

commit v2 on v1

v2 whole, which is shorter than its diff:
```python
import functools
import math

import jax
import jax.numpy as jnp
from jax import lax
from jax.experimental import pallas as pl
from jax.experimental.pallas import tpu as pltpu
from jax.sharding import PartitionSpec as P

MESH = pl.DeviceIdType.MESH
BF = jnp.bfloat16
F32 = jnp.float32

RIM = 4
TILE_ROW = 8
LANES = 128
ONES = 16

FIELDS, POOLED, FIRST, SECOND, THIRD, BACK4C, BACK4F, BACK3, BACK2, BACK1 = range(10)
EXCHANGES = (
    (64, 4, 1),
    (64, 4, 1),
    (64, 4, 1),
    (128, 4, 1),
    (128, 2, 1),
    (128, 2, 3),
    (64, 4, 3),
    (128, 4, 3),
    (64, 4, 3),
    (64, 4, 3),
)
OFFSETS = (1, -1, 9, 7, -7, -9, 8, -8)
LAYERS = ((64, 64, 16, 128), (64, 128, 8, 64), (128, 128, 8, 64), (192, 64, 16, 128))


def iota(shape, dim):
    return lax.broadcasted_iota(jnp.int32, shape, dim)


def onehot(cond):
    return jnp.where(cond, 1.0, 0.0).astype(BF)


def mm(a, b):
    return jnp.dot(a, b, preferred_element_type=F32)


def mm_nt(a, b):
    return lax.dot_general(a, b, (((1,), (1,)), ((), ())), preferred_element_type=F32)


def split(values):
    high = values.astype(BF)
    low = (values - high.astype(F32)).astype(BF)
    return jnp.concatenate([high, low], axis=-1)


def cat(parts, axis):
    return parts[0] if len(parts) == 1 else jnp.concatenate(parts, axis=axis)


def log2(m):
    return m.bit_length() - 1


def column_pick(H, W, m, code_right, code_left, shape=(LANES, LANES)):
    lane = iota(shape, 1)
    code = jnp.where(lane < 64, code_right, code_left)
    idx = lane & 63
    row, col = idx >> log2(m), idx & (m - 1)
    col = jnp.where((code & 1) == 1, W - m + col, col)
    row = jnp.where((code >> 1) == 1, H - 1 - row, row)
    valid = idx < H * m
    return jnp.where(valid, row, -1), jnp.where(valid, col, -1)


def halo_target(H, m, code, row):
    w = iota((LANES, LANES), 1)
    picked = jnp.where((code & 1) == 1, H - m + row, row)
    flip = (code >> 1) == 1
    k = w - (LANES - m)
    left = jnp.where(flip, 64 + m * picked + (m - 1 - k), m * picked + k)
    right = jnp.where(flip, m * picked + (m - 1 - w), 64 + m * picked + w)
    return jnp.where(w >= LANES - m, left, jnp.where(w < m, right, -1))


def shift_matrix(W, d):
    source = iota((2 * LANES, 2 * LANES), 0)
    out = iota((2 * LANES, 2 * LANES), 1)
    j = out & (LANES - 1)
    minus = jnp.where(j >= d, j - d, 2 * LANES + j - d)
    plus = jnp.where(j + d < W, j + d, LANES + j + d - W)
    return onehot((source == jnp.where(out < LANES, minus, plus)) & (j < W))


def reversal(W, code, shape=(LANES, LANES)):
    u, w = iota(shape, 0), iota(shape, 1)
    flip = (code >> 1) == 1
    return (u == jnp.where(flip, W - 1 - w, w)) & (w < W)


def pick_rows_matrix(W, code):
    u = iota((2 * LANES, LANES), 0)
    w = iota((2 * LANES, LANES), 1)
    flip = (code >> 1) == 1
    hit = (u & (LANES - 1)) == jnp.where(flip, W - 1 - w, w)
    return onehot(hit & ((u >> 7) == (code & 1)) & (w < W))


def return_rows_matrix(W, code_upper, code_lower, last):
    u = iota((2 * LANES, LANES), 0)
    w = iota((2 * LANES, LANES), 1)
    code = jnp.where(u < LANES, code_upper, code_lower)
    flip = (code >> 1) == 1
    hit = (u & (LANES - 1)) == jnp.where(flip, W - 1 - w, w)
    return onehot(hit & ((code & 1) == last) & (w < W))


def rim_matrix(H, m, code_above, code_below, collapse):
    shape = (2 * LANES, LANES)
    u, lane = iota(shape, 0), iota(shape, 1)
    src = u & (LANES - 1)
    if collapse:
        src = ((src >> 3) << 1) + ((src & 3) >> 1)
    src = src + (u >> 7) * 1024
    idx = lane & 63
    row, k = idx >> log2(m), idx & (m - 1)
    leftward = lane < 64
    valid = idx < H * m
    parts = [onehot((src == (row + m) * m + k + jnp.where(leftward, 1024, 0)) & valid)]
    for code, base in ((code_above, 0), (code_below, H + m)):
        picked = jnp.where((code & 1) == 1, row - (H - m), row)
        flip = jnp.where((code >> 1) == 1, 1, 0)
        kk = jnp.where(flip == 1, m - 1 - k, k)
        left_side = jnp.where(leftward, 1 - flip, flip)
        hit = src == (picked + base) * m + kk + left_side * 1024
        parts.append(onehot(hit & valid & (picked >= 0) & (picked < m)))
    return jnp.concatenate(parts, axis=1)


def edge_matrix(H, d):
    u, v = iota((LANES, LANES), 0), iota((LANES, LANES), 1)
    row, k = v >> 2, v & 3
    parts = []
    for a in range(3):
        h = row - RIM - (a - 1) * d
        inside = (h >= 0) & (h < H)
        parts.append(onehot((u == 4 * h + (4 - d + k)) & inside & (k < d)))
        parts.append(onehot((u == 64 + 4 * h + (k - 4 + d)) & inside & (k >= 4 - d)))
    return jnp.concatenate(parts, axis=1)


def gelu_and_slope(x):
    cdf = 0.5 + 0.5 * lax.erf(x * math.sqrt(0.5))
    pdf = jnp.exp(-0.5 * x * x) * (1.0 / math.sqrt(2.0 * math.pi))
    return x * cdf, cdf + x * pdf


def stacked(values):
    return values.reshape(values.shape[0] * values.shape[1], values.shape[2])


class Refs:
    def __init__(self, **parts):
        self.__dict__.update(parts)


def flatten(part):
    for value in part.__dict__.values():
        yield from value if type(value) is list else [value]


def fill_in(parts, refs):
    named = {}
    for part in parts:
        for key, value in part.__dict__.items():
            named[key] = [next(refs) for _ in value] if type(value) is list else next(refs)
    return named


def net_kernel(tiles, members, scale, tree, *refs):
    R = Refs(**fill_in(tree, iter(refs)))
    tile = lax.axis_index("tile")
    ens = lax.axis_index("ens")

    def device(offset):
        return (ens, lax.rem(tile + (offset + tiles), tiles))

    copies = []
    for x, (C, m, sent) in enumerate(EXCHANGES):
        listed = []
        for slot, offset in enumerate(OFFSETS):
            if slot < 6:
                which = 0 if sent == 1 else (0, 0, 2, 2, 1, 1)[slot]
                src = R.cs[x].at[which]
                dst = R.cr[x].at[slot]
            else:
                src = R.rs[x].at[slot - 6]
                dst = R.rr[x].at[slot - 6]
            listed.append(
                pltpu.make_async_remote_copy(
                    src_ref=src,
                    dst_ref=dst,
                    send_sem=R.send.at[x, slot],
                    recv_sem=R.recv.at[x, slot],
                    device_id=device(offset),
                    device_id_type=MESH,
                )
            )
        copies.append(listed)
    code_copies = [
        pltpu.make_async_remote_copy(
            src_ref=R.code_rows,
            dst_ref=R.code_near.at[k],
            send_sem=R.send_code.at[k],
            recv_sem=R.recv_code.at[k],
            device_id=device(offset),
            device_id_type=MESH,
        )
        for k, offset in enumerate((8, -8))
    ]

    def start(name):
        for copy in copies[name]:
            copy.start()

    def arrive(name):
        for copy in copies[name]:
            copy.wait_recv()

    n_ens, n_low = members, 4
    n_xy, n_z = tiles // (2 * n_low), n_ens * n_low
    xy = lax.div(tile, 2 * n_low)
    low = lax.div(lax.rem(tile, 2 * n_low), 2)
    core = lax.rem(tile, 2)
    z = ens * n_low + low

    def at(z_, xy_, core_):
        return (lax.div(z_, n_low), (xy_ * n_low + lax.rem(z_, n_low)) * 2 + core_)

    def xy_peer(k):
        return lax.rem(xy + k, n_xy)

    def z_peer(k):
        return lax.rem(z + k, n_z)

    def remote(src, dst, send, recv, device_id):
        return pltpu.make_async_remote_copy(
            src_ref=src, dst_ref=dst, send_sem=send, recv_sem=recv, device_id=device_id, device_id_type=MESH
        )

    def each(n, act):
        def body(k, carry):
            act(k)
            return carry

        lax.fori_loop(1, n, body, 0)

    class Sum:
        def __init__(self, tag):
            self.pay, self.from_core = R.pay[tag], R.others[tag]
            self.half, self.buf_xy, self.buf_z = R.half[tag], R.bxy[tag], R.bz[tag]
            self.res = R.res[tag]
            self.pair_sem, self.xy_sem = R.psem[tag], R.xysem[tag]
            self.z_sem = R.zsem[tag]
            partner = at(z, xy, 1 - core)
            self.pair = remote(
                self.pay.at[1 - core], self.from_core, self.pair_sem.at[0], self.pair_sem.at[1], partner
            )
            self.other = remote(
                self.res.at[core], self.res.at[core], self.pair_sem.at[2], self.pair_sem.at[3], partner
            )
            self.theirs = remote(
                self.res.at[1 - core], self.res.at[1 - core], self.pair_sem.at[2], self.pair_sem.at[3], partner
            )

        def xy_copy(self, k):
            p = xy_peer(k)
            return remote(
                self.half.at[p], self.buf_xy.at[xy], self.xy_sem.at[0, k], self.xy_sem.at[1, xy], at(z, p, core)
            )

        def xy_arrival(self, k):
            p = xy_peer(k)
            return remote(
                self.half.at[p], self.buf_xy.at[p], self.xy_sem.at[0, k], self.xy_sem.at[1, p], at(z, p, core)
            )

        def z_copy(self, k):
            here = self.buf_z.at[z]
            return remote(here, here, self.z_sem.at[0, k], self.z_sem.at[1, z], at(z_peer(k), xy, core))

        def z_arrival(self, k):
            p = z_peer(k)
            there = self.buf_z.at[p]
            return remote(there, there, self.z_sem.at[0, k], self.z_sem.at[1, p], at(p, xy, core))

        def back_copy(self, k):
            here = self.res.at[core, xy]
            return remote(here, here, self.xy_sem.at[2, k], self.xy_sem.at[3, xy], at(z, xy_peer(k), core))

        def back_arrival(self, k):
            p = xy_peer(k)
            there = self.res.at[core, p]
            return remote(there, there, self.xy_sem.at[2, k], self.xy_sem.at[3, p], at(z, p, core))

        def first(self):
            self.pair.start()

        def second(self):
            self.pair.wait()

            def add(p, carry):
                mine = self.pay[core, p].astype(F32)
                self.half[p] = (mine + self.from_core[p].astype(F32)).astype(BF)
                return carry

            lax.fori_loop(0, n_xy, add, 0)
            each(n_xy, lambda k: self.xy_copy(k).start())
            self.buf_xy[xy] = self.half[xy]

        def third(self):
            each(n_xy, lambda k: self.xy_arrival(k).wait_recv())
            total = self.buf_xy[0].astype(F32)
            for p in range(1, n_xy):
                total = total + self.buf_xy[p].astype(F32)
            self.buf_z[z] = total.astype(BF)
            each(n_z, lambda k: self.z_copy(k).start())

        def fourth(self):
            each(n_z, lambda k: self.z_arrival(k).wait_recv())
            total = self.buf_z[0].astype(F32)
            for p in range(1, n_z):
                total = total + self.buf_z[p].astype(F32)
            self.res[core, xy] = (total * scale).astype(BF)
            each(n_xy, lambda k: self.back_copy(k).start())

        def fifth(self):
            each(n_xy, lambda k: self.back_arrival(k).wait_recv())
            self.other.start()

        def sixth(self):
            self.theirs.wait_recv()

        def finish(self):
            self.other.wait_send()
            each(n_xy, lambda k: self.xy_copy(k).wait_send())
            each(n_xy, lambda k: self.back_copy(k).wait_send())
            each(n_z, lambda k: self.z_copy(k).wait_send())

    sum_a, sum_b = Sum(0), Sum(1)

    barrier = pltpu.get_barrier_semaphore()

    def greet(device_id):
        pl.semaphore_signal(barrier, inc=1, device_id=device_id, device_id_type=MESH)

    for offset in OFFSETS[:6]:
        greet(device(offset))
    each(n_xy, lambda k: greet(at(z, xy_peer(k), core)))
    each(n_z, lambda k: greet(at(z_peer(k), xy, core)))

    codes = [R.codes[0, s] for s in range(4)]
    tile_rows = iota((8, LANES), 0) & 3
    R.code_rows[...] = jnp.where(
        tile_rows == 0, codes[0], jnp.where(tile_rows == 1, codes[1], jnp.where(tile_rows == 2, codes[2], codes[3]))
    )
    dil = [R.dil[i] for i in range(4)]

    shifts = R.shifts
    for i, (_, _, _, W) in enumerate(LAYERS):
        shifts[i] = shift_matrix(W, dil[i])
    picks = R.picks
    PICK = {(16, 4): 0, (8, 4): 1, (8, 2): 2}
    for (H, m), where in PICK.items():
        _, col = column_pick(H, 128 if H == 16 else 64, m, codes[3], codes[2])
        picks[where] = onehot(iota((LANES, LANES), 0) == col)

    def pick_rows(H, m):
        row, _ = column_pick(H, 128 if H == 16 else 64, m, codes[3], codes[2], (1, LANES))
        return row

    for X3, D3, (C, O, H, _) in zip(R.x, R.d, LAYERS):
        D3[0 : 2 * RIM] = jnp.zeros((2 * RIM, 3 * O, LANES), BF)
        D3[2 * RIM + H : 4 * RIM + H] = jnp.zeros((2 * RIM, 3 * O, LANES), BF)
        X3[:, 3 * C : 3 * C + ONES, :] = jnp.ones((H + 2 * RIM, ONES, LANES), BF)

    def columns_of(x_ref, H, m, C):
        row = pick_rows(H, m)
        total = jnp.zeros((C, LANES), F32)
        for g in range(H // 4):
            y = mm(stacked(x_ref[4 * g : 4 * g + 4]), picks[PICK[(H, m)]])
            for q in range(4):
                total = total + jnp.where(row == 4 * g + q, y[q * C : (q + 1) * C], 0.0)
        return total

    def send_forward(name, x_ref, H, W, m, C):
        R.cs[name][0] = columns_of(x_ref, H, m, C).astype(BF)
        both = jnp.concatenate([stacked(x_ref[0:m]), stacked(x_ref[H - m : H])], axis=1)
        for k, side in enumerate((1, 0)):
            rows = mm(both, pick_rows_matrix(W, codes[side])).astype(BF)
            R.rs[name][k] = rows.reshape(m, C, LANES)

    def halo_arrays(name):
        near = R.cr[name]
        low = iota((1, LANES), 1) < 64
        return [jnp.where(low, near[2 * i], near[2 * i + 1]) for i in range(3)]

    def halo_rows(Z, H, m, code, rows):
        lane = iota((LANES, LANES), 0)
        mats = cat([onehot(lane == halo_target(H, m, code, r)) for r in rows], 1)
        y = mm(Z, mats).astype(BF)
        return cat([y[:, LANES * q : LANES * (q + 1)] for q in range(len(rows))], 0)

    def fill(X3, r0, core, halo, C, S, offs, repeat):
        y = mm(jnp.concatenate([core, halo], axis=1), S).astype(BF)
        for q in range(core.shape[0] // C):
            part = slice(q * C, (q + 1) * C)
            for z in range(repeat):
                r = r0 + q * repeat + z
                X3[r, offs[0] : offs[0] + C, :] = y[part, :LANES]
                X3[r, offs[1] : offs[1] + C, :] = core[part]
                X3[r, offs[2] : offs[2] + C, :] = y[part, LANES:]

    def pad_and_shift(name, x_ref, H, m, C, layer, X3, offs, refine):
        Z, Zu, Zl = halo_arrays(name)
        S = shifts[layer]
        rr = R.rr[name]
        code_u = R.code_near[0, 1:2, :]
        code_l = R.code_near[1, 0:1, :]
        rep = 2 if refine else 1

        def prepare(core, halo):
            if not refine:
                return core, halo
            u, w = iota((LANES, LANES), 0), iota((LANES, LANES), 1)
            core = mm(core, onehot(u == (w >> 1))).astype(BF)
            near = jnp.where(w < 4, w >> 1, jnp.where(w >= LANES - 4, 64 + (w >> 1), -1))
            return core, mm(halo, onehot(u == near)).astype(BF)

        def body(g, carry):
            rows = [m * g + q for q in range(m)]
            core, halo = prepare(stacked(x_ref[pl.ds(m * g, m)]), halo_rows(Z, H, m, 0, rows))
            fill(X3, RIM + m * rep * g, core, halo, C, S, offs, rep)
            return carry

        lax.fori_loop(0, H // m, body, 0, unroll=True)
        core, halo = prepare(stacked(rr[0]), halo_rows(Zu, H, m, code_u, range(m)))
        fill(X3, 0, core, halo, C, S, offs, rep)
        core, halo = prepare(stacked(rr[1]), halo_rows(Zl, H, m, code_l, range(m)))
        fill(X3, RIM + H * rep, core, halo, C, S, offs, rep)

    def conv(Z3, width, K, d, rows, write, from_row=0):
        def body(i, carry):
            r = from_row + 2 * i
            taps = []
            for b in range(3):
                base = r + RIM + (b - 1) * d
                taps.append(
                    jnp.concatenate(
                        [Z3[base, 0:width, :], Z3[base + 1, 0:width, :]], axis=1
                    )
                )
            y = mm(K[...], jnp.concatenate(taps, axis=0))
            write(r, y[:, :LANES])
            write(r + 1, y[:, LANES:])
            return carry

        lax.fori_loop(0, rows // 2, body, 0, unroll=True)

    def weight_terms(X3, C, D3, O, d, rows, acc):
        n = 3 * C + ONES

        def body(i, carry):
            r = 4 * i
            lhs = jnp.concatenate([X3[r + q] for q in range(4)], axis=1)
            taps = []
            for a in range(3):
                base = r + RIM - (a - 1) * d
                taps.append(
                    jnp.concatenate([D3[base + q, O : 2 * O, :] for q in range(4)], axis=1)
                )
            if O == 64:
                taps.append(jnp.zeros((O, 4 * LANES), BF))
            y = mm_nt(lhs, jnp.concatenate(taps, axis=0))
            acc[0:n] = acc[0:n] + y
            return carry

        acc[0:n] = jnp.zeros((n, acc.shape[1]), F32)
        lax.fori_loop(0, rows // 4, body, 0, unroll=True)

    def spread_delta(x_ref, H, O, layer, D3):
        def body(g, carry):
            core = stacked(x_ref[pl.ds(4 * g, 4)])
            y = mm(core, shifts[layer, 0:LANES, :]).astype(BF)
            for q in range(4):
                part = slice(q * O, (q + 1) * O)
                D3[2 * RIM + 4 * g + q, 0:O, :] = y[part, :LANES]
                D3[2 * RIM + 4 * g + q, O : 2 * O, :] = core[part]
                D3[2 * RIM + 4 * g + q, 2 * O : 3 * O, :] = y[part, LANES:]
            return carry

        lax.fori_loop(0, H // 4, body, 0, unroll=True)

    def rims_of(x_ref, H, W, O, layer, K):
        row, col = column_pick(H, W, RIM, 1, 0, (1, LANES))
        _, col_full = column_pick(H, W, RIM, 1, 0)
        pick = onehot(iota((LANES, LANES), 0) == col_full)
        edges = jnp.zeros((O, LANES), F32)
        for g in range(H // 4):
            y = mm(stacked(x_ref[4 * g : 4 * g + 4]), pick)
            for q in range(4):
                edges = edges + jnp.where(row == 4 * g + q, y[q * O : (q + 1) * O], 0.0)
        e = mm(edges.astype(BF), edge_matrix(H, dil[layer])).astype(BF)
        none = jnp.zeros((O, LANES), BF)
        blocks = []
        for b in range(3):
            a = 2 - b
            right = e[:, 2 * a * LANES : (2 * a + 1) * LANES]
            left = e[:, (2 * a + 1) * LANES : (2 * a + 2) * LANES]
            blocks.append(jnp.concatenate([right, none], axis=1))
            blocks.append(jnp.zeros((O, 2 * LANES), BF))
            blocks.append(jnp.concatenate([none, left], axis=1))
        return mm(K[...], jnp.concatenate(blocks, axis=0)).astype(BF)

    def send_backward(name, rims, G, c0, C, H, m, collapse=False):
        code_u = R.code_near[0, 1:2, :]
        code_l = R.code_near[1, 0:1, :]
        y = mm(rims, rim_matrix(H, m, code_u, code_l, collapse)).astype(BF)
        for k in range(3):
            R.cs[name][k] = y[:, k * LANES : (k + 1) * LANES]
        R.rs[name][0] = G[H + m : H + 2 * m, c0 : c0 + C, :].astype(BF)
        R.rs[name][1] = G[0:m, c0 : c0 + C, :].astype(BF)

    def fold(name, G, c0, C, H, W, m, write):
        near = R.cr[name]
        rr = R.rr[name]
        low = iota((1, LANES), 1) < 64
        back = jnp.where(
            low,
            near[1].astype(F32) + near[3].astype(F32) + near[5].astype(F32),
            near[0].astype(F32) + near[2].astype(F32) + near[4].astype(F32),
        )
        row = pick_rows(H, m)
        both = jnp.concatenate([stacked(rr[0]), stacked(rr[1])], axis=1)
        first = mm(both, return_rows_matrix(W, codes[0], codes[1], 0))
        last = mm(both, return_rows_matrix(W, codes[0], codes[1], 1))
        pick = picks[PICK[(H, m)]]
        for g in range(H // m):
            masked = [jnp.where(row == m * g + q, back, 0.0).astype(BF) for q in range(m)]
            y = mm_nt(cat(masked, 0), pick)
            if g == 0:
                y = y + first
            if g == H // m - 1:
                y = y + last
            for q in range(m):
                h = m * g + q
                write(h, G[h + m, c0 : c0 + C, :] + y[q * C : (q + 1) * C])

    def eye(n):
        return onehot(iota((n, n), 0) == iota((n, n), 1))

    def forward_weights(i):
        k, kf = R.k[i], R.kf[i]
        if i == 1:
            for t in range(0, 9, 2):
                block = k[8] if t == 8 else jnp.concatenate([k[t], k[t + 1]], axis=0)
                kf[:, t * 64 : t * 64 + block.shape[0]] = mm_nt(eye(LANES), block).astype(BF)
            return
        C = k.shape[2]
        for t in range(0, 9, 2):
            block = k[t] if t == 8 else jnp.concatenate([k[t], k[t + 1]], axis=1)
            kf[:, t * C : t * C + block.shape[1]] = block

    def backward_weights(i):
        k, kt = R.k[i], R.kt[i]
        if i == 1:
            for t in range(9):
                kt[:, t * LANES : (t + 1) * LANES] = k[8 - t]
            return
        O, C = k.shape[1], k.shape[2]
        for t in range(0, 9, 2):
            block = k[0] if t == 8 else jnp.concatenate([k[8 - t], k[7 - t]], axis=0)
            kt[:, t * O : t * O + block.shape[0]] = mm_nt(eye(C), block).astype(BF)

    def column(i):
        row = R.off[i][...]
        n = row.shape[1]
        return jnp.sum(jnp.where(iota((n, n), 0) == iota((n, n), 1), row, 0.0), axis=1, keepdims=True)

    pu, pw = iota((256, 256), 0), iota((256, 256), 1)
    to_rows = onehot(pw == ((pu & 15) << 4) + (pu >> 4))

    def rows_first(x_ref, out):
        for g in range(4):
            y = mm(to_rows, stacked(x_ref[16 * g : 16 * g + 16])).astype(BF)
            for h in range(16):
                out[h, 16 * g : 16 * g + 16, :] = y[16 * h : 16 * h + 16]

    def channels_first(x_ref, out, parts):
        for g in range(4):
            block = cat([x_ref[h, 16 * g : 16 * g + 16, :] for h in range(16)], 0)
            y = mm(to_rows, block) if parts == 1 else mm(to_rows, split(block))
            if parts == 2:
                y = y[:, :LANES] + y[:, LANES:]
            out[16 * g : 16 * g + 16] = y.astype(out.dtype).reshape(16, 16, LANES)

    def put(ref, start_row, value):
        q = ref.shape[2]
        done = 0
        while done < value.shape[0]:
            piece, inner = divmod(start_row + done, q)
            n = min(q - inner, value.shape[0] - done)
            ref[piece // n_xy, piece % n_xy, inner : inner + n, :] = value[done : done + n].astype(BF)
            done += n

    def get(ref, start_row, count):
        q = ref.shape[2]
        parts, done = [], 0
        while done < count:
            piece, inner = divmod(start_row + done, q)
            n = min(q - inner, count - done)
            parts.append(ref[piece // n_xy, piece % n_xy, inner : inner + n, :])
            done += n
        return cat(parts, 0)

    def put_terms(ref, listed):
        where = 0
        for acc, C, O in listed:
            chunks = 2 if O == 64 else 3
            for k in range(chunks):
                put(ref, where, acc[0 : 3 * C, k * LANES : (k + 1) * LANES])
                where += 3 * C
        for acc, C, O in listed:
            k = 0 if O == 64 else 1
            put(ref, where, acc[3 * C : 3 * C + ONES, k * LANES : (k + 1) * LANES])
            where += ONES
        pieces = ref.shape[0] * ref.shape[1] * ref.shape[2]
        put(ref, where, jnp.zeros((pieces - where, LANES), BF))

    def take_terms(ref, listed):
        sel = [onehot(iota((64, LANES), 1) == iota((64, LANES), 0) + 64 * k) for k in range(2)]
        where = 0
        for w_out, b_out, C, O in listed:
            for a in range(3):
                chunk, side = (a // 2, sel[a % 2]) if O == 64 else (a, eye(LANES))
                for e in range(3):
                    block = get(ref, where + chunk * 3 * C + e * C, C)
                    w_out[3 * a + e] = block.astype(F32) if O > C else mm_nt(side, block)
            where += (2 if O == 64 else 3) * 3 * C
        for w_out, b_out, C, O in listed:
            block = get(ref, where, ONES)
            b_out[...] = mm_nt(block, sel[1])[0:1] if O == 64 else block.astype(F32)[0:1]
            where += ONES

    rows_first(R.fields_in, R.fields)
    send_forward(FIELDS, R.fields, 16, 128, 4, 64)
    pl.semaphore_wait(barrier, 6 + (n_xy - 1) + (n_z - 1))
    for copy in code_copies:
        copy.start()
    start(FIELDS)

    forward_weights(0)
    cot = R.cot
    rows_first(R.cot_in, cot)
    backward_weights(3)
    spread_delta(cot, 16, 64, 3, R.d[3])
    G4 = R.g[3]

    def write_g4(r, v):
        G4[r] = v

    conv(R.d[3], 192, R.kt[3], dil[3], 24, write_g4)
    for i in (1, 2, 3):
        forward_weights(i)
    for i in (2, 1, 0):
        backward_weights(i)
    columns = [column(i) for i in range(4)]

    for copy in code_copies:
        copy.wait_recv()
    arrive(FIELDS)
    pad_and_shift(FIELDS, R.fields, 16, 4, 64, 0, R.x[0], (0, 64, 128), False)
    first_act, slope1 = R.first_act, R.slope1

    def write_first(r, v):
        act, slope = gelu_and_slope(v + columns[0])
        first_act[r] = act.astype(BF)
        slope1[r] = slope

    conv(R.x[0], 192, R.kf[0], dil[0], 16, write_first)
    pooled = R.pooled
    u, w = iota((2 * LANES, LANES), 0), iota((2 * LANES, LANES), 1)
    quarter = jnp.where(((u & (LANES - 1)) >> 1) == w, 0.25, 0.0).astype(BF)
    for g in range(2):
        lhs = cat(
            [
                jnp.concatenate([first_act[8 * g + 2 * q], first_act[8 * g + 2 * q + 1]], axis=1)
                for q in range(4)
            ],
            0,
        )
        pooled[4 * g : 4 * g + 4] = mm(lhs, quarter).astype(BF).reshape(4, 64, LANES)
    send_forward(POOLED, pooled, 8, 64, 4, 64)
    start(POOLED)
    send_forward(FIRST, first_act, 16, 128, 4, 64)
    start(FIRST)
    rims4 = rims_of(cot, 16, 128, 64, 3, R.kt[3])
    G4c = R.g4c
    pool = onehot(((u & (LANES - 1)) >> 1) == w)
    for g in range(3):
        pairs = [G4[8 * g + 2 * q, 0:128, :] + G4[8 * g + 2 * q + 1, 0:128, :] for q in range(4)]
        y = mm(split(cat(pairs, 0)), pool)
        G4c[4 * g : 4 * g + 4] = y.reshape(4, 128, LANES)
    send_backward(BACK4C, rims4[0:128], G4c, 0, 128, 8, 2, True)
    start(BACK4C)
    send_backward(BACK4F, rims4[128:192], G4, 128, 64, 16, 4)
    start(BACK4F)


    arrive(POOLED)
    pad_and_shift(POOLED, pooled, 8, 4, 64, 1, R.x[1], (0, 64, 128), False)
    second_act, slope2 = R.second_act, R.slope2
    inside = iota((1, LANES), 1) < 64

    def write_second(r, v):
        act, slope = gelu_and_slope(v + columns[1])
        second_act[r] = jnp.where(inside, act, 0.0).astype(BF)
        slope2[r] = jnp.where(inside, slope, 0.0)

    conv(R.x[1], 192, R.kf[1], dil[1], 8, write_second)
    send_forward(SECOND, second_act, 8, 64, 4, 128)
    start(SECOND)

    arrive(BACK4C)
    arrive(BACK4F)
    coarse, skip = R.coarse, R.skip

    def write_coarse(r, v):
        coarse[r] = v

    def write_skip(r, v):
        skip[r] = v

    fold(BACK4C, G4c, 0, 128, 8, 64, 2, write_coarse)
    fold(BACK4F, G4, 128, 64, 16, 128, 4, write_skip)

    arrive(FIRST)
    pad_and_shift(FIRST, first_act, 16, 4, 64, 3, R.x[3], (128, 320, 512), False)

    arrive(SECOND)
    pad_and_shift(SECOND, second_act, 8, 4, 128, 2, R.x[2], (0, 128, 256), False)
    third_act, delta3 = R.third_act, R.delta3

    def write_third(r, v):
        act, slope = gelu_and_slope(v + columns[2])
        third_act[r] = jnp.where(inside, act, 0.0).astype(BF)
        delta3[r] = jnp.where(inside, coarse[r] * slope, 0.0).astype(BF)

    conv(R.x[2], 384, R.kf[2], dil[2], 8, write_third)
    send_forward(THIRD, third_act, 8, 64, 2, 128)
    start(THIRD)
    spread_delta(delta3, 8, 128, 2, R.d[2])
    G3 = R.g[2]

    def write_g3(r, v):
        G3[r] = v

    conv(R.d[2], 384, R.kt[2], dil[2], 16, write_g3)
    send_backward(BACK3, rims_of(delta3, 8, 64, 128, 2, R.kt[2]), G3, 0, 128, 8, 4)
    start(BACK3)

    weight_terms(R.x[2], 128, R.d[2], 128, dil[2], 16, R.w[2])
    arrive(THIRD)
    pad_and_shift(THIRD, third_act, 8, 2, 128, 3, R.x[3], (0, 192, 384), True)

    arrive(BACK3)
    delta2 = R.delta2

    def write_delta2(r, v):
        delta2[r] = (v * slope2[r]).astype(BF)

    fold(BACK3, G3, 0, 128, 8, 64, 4, write_delta2)
    spread_delta(delta2, 8, 128, 1, R.d[1])
    G2 = R.g[1]

    def write_g2(r, v):
        G2[r] = v

    conv(R.d[1], 384, R.kt[1], dil[1], 16, write_g2)
    send_backward(BACK2, rims_of(delta2, 8, 64, 128, 1, R.kt[1]), G2, 0, 64, 8, 4)
    start(BACK2)

    weight_terms(R.x[1], 64, R.d[1], 128, dil[1], 16, R.w[1])
    weight_terms(R.x[3], 192, R.d[3], 64, dil[3], 24, R.w[3])
    put_terms(R.pay[0], ((R.w[3], 192, 64), (R.w[2], 128, 128), (R.w[1], 64, 128)))
    sum_a.first()
    state = R.state

    def write_state(r, v):
        state[r] = (v + columns[3]).astype(BF)


    arrive(BACK2)
    delta1 = R.delta1
    repeat = jnp.where((u & (LANES - 1)) == (w >> 1), 0.25, 0.0).astype(BF)

    def write_delta1(r, v):
        wide = mm(split(v), repeat)
        for z in range(2):
            delta1[2 * r + z] = ((skip[2 * r + z] + wide) * slope1[2 * r + z]).astype(BF)

    fold(BACK2, G2, 0, 64, 8, 64, 4, write_delta1)
    spread_delta(delta1, 16, 64, 0, R.d[0])
    weight_terms(R.x[0], 64, R.d[0], 64, dil[0], 24, R.w[0])
    put_terms(R.pay[1], ((R.w[0], 64, 64),))
    sum_b.first()
    G1 = R.g[0]

    def write_g1(r, v):
        G1[r] = v

    conv(R.d[0], 192, R.kt[0], dil[0], 24, write_g1)
    sum_b.second()
    send_backward(BACK1, rims_of(delta1, 16, 128, 64, 0, R.kt[0]), G1, 0, 64, 16, 4)
    start(BACK1)

    sum_a.second()
    conv(R.x[3], 576, R.kf[3], dil[3], 8, write_state)
    sum_b.third()
    arrive(BACK1)
    grad = R.grad

    def write_grad(r, v):
        grad[r] = v

    fold(BACK1, G1, 0, 64, 16, 128, 4, write_grad)
    sum_a.third()
    sum_b.fourth()
    conv(R.x[3], 576, R.kf[3], dil[3], 8, write_state, 8)
    sum_a.fourth()
    sum_b.fifth()
    channels_first(state, R.state_out, 1)
    channels_first(grad, R.grad_out, 2)
    sum_a.fifth()
    sum_b.sixth()
    take_terms(R.res[1], ((R.wo[0], R.bo[0], 64, 64),))
    sum_a.sixth()
    take_terms(R.res[0], ((R.wo[3], R.bo[3], 192, 64), (R.wo[2], R.bo[2], 128, 128), (R.wo[1], R.bo[1], 64, 128)))

    sum_a.finish()
    sum_b.finish()
    for listed in (*copies, code_copies):
        for copy in listed:
            copy.wait_send()


PIECE = (96, 16)


def run_net(tiles, members, scale, operands):
    V, D = pltpu.VMEM, pltpu.SemaphoreType.DMA
    n_xy, n_z = tiles // 8, members * 4
    sizes = [(C, O, H + 2 * RIM) for C, O, H, _ in LAYERS]
    scratch = Refs(
        shifts=V((4, 256, 256), BF),
        picks=V((3, LANES, LANES), BF),
        x=[V((P_, 3 * C + ONES, LANES), BF) for C, O, P_ in sizes],
        d=[V((P_ + 2 * RIM, 3 * O, LANES), BF) for C, O, P_ in sizes],
        g=[V((P_, C, LANES), F32) for C, O, P_ in sizes],
        g4c=V((12, 128, LANES), F32),
        kf=[V((O, 9 * C), BF) for C, O, _ in sizes],
        kt=[V((C, 9 * O), BF) for C, O, _ in sizes],
        w=[V((3 * C + ONES, 256 if O == 64 else 384), F32) for C, O, _ in sizes],
        fields=V((16, 64, LANES), BF),
        cot=V((16, 64, LANES), BF),
        state=V((16, 64, LANES), BF),
        grad=V((16, 64, LANES), F32),
        first_act=V((16, 64, LANES), BF),
        slope1=V((16, 64, LANES), F32),
        pooled=V((8, 64, LANES), BF),
        second_act=V((8, 128, LANES), BF),
        slope2=V((8, 128, LANES), F32),
        third_act=V((8, 128, LANES), BF),
        coarse=V((8, 128, LANES), F32),
        skip=V((16, 64, LANES), F32),
        delta1=V((16, 64, LANES), BF),
        delta2=V((8, 128, LANES), BF),
        delta3=V((8, 128, LANES), BF),
        code_rows=V((8, LANES), jnp.int32),
        code_near=V((2, 8, LANES), jnp.int32),
        send=D((len(EXCHANGES), 8)),
        recv=D((len(EXCHANGES), 8)),
        send_code=D((2,)),
        recv_code=D((2,)),
        pay=[V((2, n_xy, q, LANES), BF) for q in PIECE],
        others=[V((n_xy, q, LANES), BF) for q in PIECE],
        half=[V((n_xy, q, LANES), BF) for q in PIECE],
        bxy=[V((n_xy, q, LANES), BF) for q in PIECE],
        bz=[V((n_z, q, LANES), BF) for q in PIECE],
        res=[V((2, n_xy, q, LANES), BF) for q in PIECE],
        psem=[D((4,)) for q in PIECE],
        xysem=[D((4, n_xy)) for q in PIECE],
        zsem=[D((2, n_z)) for q in PIECE],
        cs=[V((sent, C, LANES), BF) for C, m, sent in EXCHANGES],
        rs=[V((2, m, C, LANES), BF) for C, m, sent in EXCHANGES],
        cr=[V((6, C, LANES), BF) for C, m, sent in EXCHANGES],
        rr=[V((2, m, C, LANES), BF) for C, m, sent in EXCHANGES],
    )
    smem = pl.BlockSpec(memory_space=pltpu.SMEM)
    vmem = pl.BlockSpec(memory_space=pltpu.VMEM)
    shape = jax.ShapeDtypeStruct
    outputs = Refs(
        state_out=shape((64, 16, LANES), BF),
        grad_out=shape((64, 16, LANES), F32),
        wo=[shape((9, C, O) if O > C else (9, O, C), F32) for C, O, _, _ in LAYERS],
        bo=[shape((1, O), F32) for C, O, _, _ in LAYERS],
    )
    inputs = Refs(**operands)
    flat_in, flat_out, flat_scratch = (list(flatten(part)) for part in (inputs, outputs, scratch))
    return pl.pallas_call(
        functools.partial(net_kernel, tiles, members, scale, (inputs, outputs, scratch)),
        out_shape=tuple(flat_out),
        in_specs=[smem if v.dtype == jnp.int32 else vmem for v in flat_in],
        out_specs=(vmem,) * len(flat_out),
        scratch_shapes=flat_scratch,
        compiler_params=pltpu.CompilerParams(
            collective_id=0, has_side_effects=True, vmem_limit_bytes=56 * 2**20
        ),
    )(*flat_in)


def shards(tiles, members, fields, cotangent, k1, k2, k3, k4, off1, off2, off3, off4, codes, dilations):
    operands = dict(
        codes=codes,
        dil=dilations,
        fields_in=fields[0, 0],
        cot_in=cotangent[0, 0],
        k=[k1, jnp.swapaxes(k2, 1, 2), k3, k4],
        off=[off1[None, :], off2[None, :], off3[None, :], off4[None, :]],
    )
    scale = 1.0 / math.sqrt(members * tiles * fields.shape[3] * fields.shape[4])
    state, grad, *rest = run_net(tiles, members, scale, operands)
    rest[1] = jnp.swapaxes(rest[1], 1, 2)
    return (state[None, None], grad[None, None], *rest[:4], *[b[0] for b in rest[4:]])


def solution(mesh):
    big = P("ens", "tile", None, None, None)
    in_specs = (big, big) + (P(),) * 8 + (P("tile", None), P())
    out_specs = (big, big) + (P(),) * 8
    body = functools.partial(shards, mesh.shape["tile"], mesh.shape["ens"])
    return jax.shard_map(body, mesh=mesh, in_specs=in_specs, out_specs=out_specs, check_vma=False)
```

time: 134 us -> 101 us (0.75)
  local copies, waits for them, and re-layouts: 28 us -> 8.84 us
  Pallas kernels: 104 us -> 91.5 us
    pallas_call x2 -> x1, Pallas kernels: 104 us -> 91.5 us  [run_net(): pl.pallas_call(functools.partial(net_kernel, tiles, members, scale, (inpu...]
    reshape x12 -> x0, local copies, waits for them, and re-layouts: 9.38 us -> none  [the longest x4 4.42 us: forward_weights(): return jnp.transpose(k, (1, 0, 2)).reshape(k.shape[1], 9 * k.shape[2])]
    broadcast_in_dim x5 -> x0, local copies, waits for them, and re-layouts: 6.13 us -> none  [the longest x4 5.47 us: shards(): operands.append((f'off{i + 1}', offsets[i][:, None]))]
    transpose x7 -> x0, local copies, waits for them, and re-layouts: 5.78 us -> none  [the longest x4 3.61 us: shards(): weights[name] = jnp.transpose(body, (2, 0, 3, 1)).reshape(9, O, C)]
    unnamed x13 -> x28, local copies, waits for them, and re-layouts: 4.28 us -> 8.84 us
where the time goes in v2:
time: 101 us
  Pallas kernels  91.5 us (91%)
  local copies, waits for them, and re-layouts  8.84 us (9%)
    pallas_call x1, Pallas kernels, run_net(): pl.pallas_call(functools.partial(net_kernel, tiles, members, scale, (inpu...  91.5 us
    unnamed x28, local copies, waits for them, and re-layouts  8.84 us

profile of v2, /device:TPU:1, one launch (start us, length us, event | category | flops | bytes accessed | tf_op | source)
XLA Modules:
  0.0 101.0 jit_solution(11517096190737964936)
XLA Ops:
  0.6 91.5 %shard_map.195 = (bf16[64,16,128]{2,1,0:T(8,128)(2,1)}, f32[64,16,128]{2,1,0:T(8,128)}, f32[9,64,64]{2,1,0:T(8,128)}, f32[9,64,128]{2,1,0:T(8,128)}, f32[9,128,1...) custom-call(s32[1,4]{1,0:T(1,128)} %refs_0_.1, ...), custom_call_target="tpu_custom_call" | custom-call | tf_op jit(solution)/shard_map/pallas_call | solution.py:922
  92.2 0.0 copy-start.2
  92.2 1.7 %copy.32 = bf16[1,1,64,16,128]{4,3,2,1,0:T(8,128)(2,1)} copy(bf16[1,1,64,16,128]{4,3,2,1,0:T(8,128)(2,1)} %bitcast.18) | data formatting | bytes 524288
  93.9 0.0 copy-done.2
  93.9 0.0 copy-start.4
  93.9 0.0 copy-start.3
  93.9 0.8 copy.33
  94.7 0.3 copy-done.4
  95.1 0.0 copy-start.1
  95.1 0.7 copy.34
  95.8 0.0 copy-done.3
  95.8 0.7 copy.35
  96.5 0.0 copy-done.1
  96.5 0.0 copy-start
  96.5 0.8 copy.36
  97.3 0.5 copy-done
  97.8 0.0 copy-start.8
  97.8 0.8 copy.37
  98.6 0.0 copy-done.8
  98.6 0.0 copy-start.7
  98.6 0.5 copy.38
  99.1 0.2 copy-done.7
  99.3 0.0 copy-start.6
  99.3 0.5 copy.39
  99.8 0.2 copy-done.6
  99.9 0.0 copy-start.5
  99.9 0.5 copy.40
  100.4 0.1 copy-done.5
  100.5 0.5 copy.41
Async XLA Ops:
  92.2 1.7 %copy-start.2 = (f32[64,16,128]{2,1,0:T(8,128)S(1)}, f32[64,16,128]{2,1,0:T(8,128)}, u32[]{:S(2)}) copy-start(f32[64,16,128]{2,1,0:T(8,128)} %get-tuple-element.21) | copy-start | bytes 1572868
  93.9 1.1 %copy-start.4 = (f32[9,64,64]{2,1,0:T(8,128)S(1)}, f32[9,64,64]{2,1,0:T(8,128)}, u32[]{:S(2)}) copy-start(f32[9,64,64]{2,1,0:T(8,128)} %get-tuple-element.42) | copy-start | bytes 442372
  93.9 1.8 %copy-start.3 = (f32[9,64,128]{2,1,0:T(8,128)S(1)}, f32[9,64,128]{2,1,0:T(8,128)}, u32[]{:S(2)}) copy-start(f32[9,64,128]{2,1,0:T(8,128)} %get-tuple-element.23) | copy-start | bytes 884740
  95.1 1.4 %copy-start.1 = (f32[9,128,128]{2,1,0:T(8,128)S(1)}, f32[9,128,128]{2,1,0:T(8,128)}, u32[]{:S(2)}) copy-start(f32[9,128,128]{2,1,0:T(8,128)} %get-tuple-element.44) | copy-start | bytes 1769476
  96.5 1.3 %copy-start = (f32[9,64,192]{2,1,0:T(8,128)S(1)}, f32[9,64,192]{2,1,0:T(8,128)}, u32[]{:S(2)}) copy-start(f32[9,64,192]{2,1,0:T(8,128)} %get-tuple-element.45) | copy-start | bytes 1327108
  97.8 0.8 copy-start.8
  98.6 0.7 copy-start.7
  99.3 0.7 copy-start.6
  99.9 0.6 copy-start.5

commit v3 on v2

--- a/solution.py
+++ b/solution.py
@@ -19,16 +19,16 @@
 
 FIELDS, POOLED, FIRST, SECOND, THIRD, BACK4C, BACK4F, BACK3, BACK2, BACK1 = range(10)
 EXCHANGES = (
-    (64, 4, 1),
-    (64, 4, 1),
-    (64, 4, 1),
-    (128, 4, 1),
-    (128, 2, 1),
-    (128, 2, 3),
-    (64, 4, 3),
-    (128, 4, 3),
-    (64, 4, 3),
-    (64, 4, 3),
+    (64, 4, 16, 2),
+    (64, 4, 8, 2),
+    (64, 4, 16, 2),
+    (128, 4, 8, 2),
+    (128, 2, 8, 2),
+    (128, 2, 8, 6),
+    (64, 4, 16, 6),
+    (128, 4, 8, 6),
+    (64, 4, 8, 6),
+    (64, 4, 16, 6),
 )
 OFFSETS = (1, -1, 9, 7, -7, -9, 8, -8)
 LAYERS = ((64, 64, 16, 128), (64, 128, 8, 64), (128, 128, 8, 64), (192, 64, 16, 128))
@@ -179,6 +179,42 @@
     return named
 
 
+def pack(y, width, left):
+    groups = LANES // width
+    n = y.shape[0] // groups
+    group = iota((1, LANES), 1) >> log2(width)
+    out = jnp.zeros((n, LANES), F32)
+    for g in range(groups):
+        by = (g * width - (64 if left else 0)) % LANES
+        part = y[g * n : (g + 1) * n]
+        out = jnp.where(group == g, pltpu.roll(part, by, 1) if by else part, out)
+    return out.astype(BF)
+
+
+def unpack(p, width, left):
+    p = p.astype(F32)
+    parts = []
+    for g in range(LANES // width):
+        by = ((64 if left else 0) - g * width) % LANES
+        parts.append(pltpu.roll(p, by, 1) if by else p)
+    return jnp.concatenate(parts, axis=0)
+
+
+def pack_rows(rows, W):
+    if W == LANES:
+        return rows.astype(BF)
+    n, C, _ = rows.shape
+    second = pltpu.roll(stacked(rows[n // 2 :]), 64, 1)
+    return (stacked(rows[: n // 2]) + second).astype(BF).reshape(n // 2, C, LANES)
+
+
+def unpack_rows(x, W):
+    x = stacked(x)
+    if W == LANES:
+        return x
+    return jnp.concatenate([x, pltpu.roll(x.astype(F32), 64, 1).astype(BF)], axis=0)
+
+
 def net_kernel(tiles, members, scale, tree, *refs):
     R = Refs(**fill_in(tree, iter(refs)))
     tile = lax.axis_index("tile")
@@ -188,11 +224,11 @@
         return (ens, lax.rem(tile + (offset + tiles), tiles))
 
     copies = []
-    for x, (C, m, sent) in enumerate(EXCHANGES):
+    for x, (C, m, H, sent) in enumerate(EXCHANGES):
         listed = []
         for slot, offset in enumerate(OFFSETS):
             if slot < 6:
-                which = 0 if sent == 1 else (0, 0, 2, 2, 1, 1)[slot]
+                which = slot % sent
                 src = R.cs[x].at[which]
                 dst = R.cr[x].at[slot]
             else:
@@ -396,16 +432,22 @@
         return total
 
     def send_forward(name, x_ref, H, W, m, C):
-        R.cs[name][0] = columns_of(x_ref, H, m, C).astype(BF)
+        y = columns_of(x_ref, H, m, C)
+        for side in range(2):
+            R.cs[name][side] = pack(y, m * H, side == 1)
         both = jnp.concatenate([stacked(x_ref[0:m]), stacked(x_ref[H - m : H])], axis=1)
         for k, side in enumerate((1, 0)):
-            rows = mm(both, pick_rows_matrix(W, codes[side])).astype(BF)
-            R.rs[name][k] = rows.reshape(m, C, LANES)
-
-    def halo_arrays(name):
+            rows = mm(both, pick_rows_matrix(W, codes[side]))
+            R.rs[name][k] = pack_rows(rows.reshape(m, C, LANES), W)
+
+    def halo_arrays(name, width):
         near = R.cr[name]
         low = iota((1, LANES), 1) < 64
-        return [jnp.where(low, near[2 * i], near[2 * i + 1]) for i in range(3)]
+        listed = []
+        for i in range(3):
+            right, left = unpack(near[2 * i], width, False), unpack(near[2 * i + 1], width, True)
+            listed.append(jnp.where(low, right, left).astype(BF))
+        return listed
 
     def halo_rows(Z, H, m, code, rows):
         lane = iota((LANES, LANES), 0)
@@ -424,7 +466,8 @@
                 X3[r, offs[2] : offs[2] + C, :] = y[part, LANES:]
 
     def pad_and_shift(name, x_ref, H, m, C, layer, X3, offs, refine):
-        Z, Zu, Zl = halo_arrays(name)
+        Z, Zu, Zl = halo_arrays(name, H * m)
+        W = LANES * H // 16
         S = shifts[layer]
         rr = R.rr[name]
         code_u = R.code_near[0, 1:2, :]
@@ -446,9 +489,9 @@
             return carry
 
         lax.fori_loop(0, H // m, body, 0, unroll=True)
-        core, halo = prepare(stacked(rr[0]), halo_rows(Zu, H, m, code_u, range(m)))
+        core, halo = prepare(unpack_rows(rr[0], W), halo_rows(Zu, H, m, code_u, range(m)))
         fill(X3, 0, core, halo, C, S, offs, rep)
-        core, halo = prepare(stacked(rr[1]), halo_rows(Zl, H, m, code_l, range(m)))
+        core, halo = prepare(unpack_rows(rr[1], W), halo_rows(Zl, H, m, code_l, range(m)))
         fill(X3, RIM + H * rep, core, halo, C, S, offs, rep)
 
     def conv(Z3, width, K, d, rows, write, from_row=0):
@@ -527,23 +570,23 @@
     def send_backward(name, rims, G, c0, C, H, m, collapse=False):
         code_u = R.code_near[0, 1:2, :]
         code_l = R.code_near[1, 0:1, :]
-        y = mm(rims, rim_matrix(H, m, code_u, code_l, collapse)).astype(BF)
-        for k in range(3):
-            R.cs[name][k] = y[:, k * LANES : (k + 1) * LANES]
-        R.rs[name][0] = G[H + m : H + 2 * m, c0 : c0 + C, :].astype(BF)
-        R.rs[name][1] = G[0:m, c0 : c0 + C, :].astype(BF)
+        y = mm(rims, rim_matrix(H, m, code_u, code_l, collapse))
+        for slot, k in enumerate((0, 0, 2, 2, 1, 1)):
+            R.cs[name][slot] = pack(y[:, k * LANES : (k + 1) * LANES], H * m, slot % 2 == 0)
+        W = LANES * H // 16
+        R.rs[name][0] = pack_rows(G[H + m : H + 2 * m, c0 : c0 + C, :], W)
+        R.rs[name][1] = pack_rows(G[0:m, c0 : c0 + C, :], W)
 
     def fold(name, G, c0, C, H, W, m, write):
         near = R.cr[name]
         rr = R.rr[name]
         low = iota((1, LANES), 1) < 64
-        back = jnp.where(
-            low,
-            near[1].astype(F32) + near[3].astype(F32) + near[5].astype(F32),
-            near[0].astype(F32) + near[2].astype(F32) + near[4].astype(F32),
+        to_right, to_left = (
+            near[i].astype(F32) + near[i + 2].astype(F32) + near[i + 4].astype(F32) for i in (1, 0)
         )
+        back = jnp.where(low, unpack(to_right, H * m, False), unpack(to_left, H * m, True))
         row = pick_rows(H, m)
-        both = jnp.concatenate([stacked(rr[0]), stacked(rr[1])], axis=1)
+        both = jnp.concatenate([unpack_rows(rr[0], W), unpack_rows(rr[1], W)], axis=1)
         first = mm(both, return_rows_matrix(W, codes[0], codes[1], 0))
         last = mm(both, return_rows_matrix(W, codes[0], codes[1], 1))
         pick = picks[PICK[(H, m)]]
@@ -705,7 +748,6 @@
     send_forward(POOLED, pooled, 8, 64, 4, 64)
     start(POOLED)
     send_forward(FIRST, first_act, 16, 128, 4, 64)
-    start(FIRST)
     rims4 = rims_of(cot, 16, 128, 64, 3, R.kt[3])
     G4c = R.g4c
     pool = onehot(((u & (LANES - 1)) >> 1) == w)
@@ -714,12 +756,12 @@
         y = mm(split(cat(pairs, 0)), pool)
         G4c[4 * g : 4 * g + 4] = y.reshape(4, 128, LANES)
     send_backward(BACK4C, rims4[0:128], G4c, 0, 128, 8, 2, True)
+    send_backward(BACK4F, rims4[128:192], G4, 128, 64, 16, 4)
+
+
+    arrive(POOLED)
+    start(FIRST)
     start(BACK4C)
-    send_backward(BACK4F, rims4[128:192], G4, 128, 64, 16, 4)
-    start(BACK4F)
-
-
-    arrive(POOLED)
     pad_and_shift(POOLED, pooled, 8, 4, 64, 1, R.x[1], (0, 64, 128), False)
     second_act, slope2 = R.second_act, R.slope2
     inside = iota((1, LANES), 1) < 64
@@ -734,7 +776,6 @@
     start(SECOND)
 
     arrive(BACK4C)
-    arrive(BACK4F)
     coarse, skip = R.coarse, R.skip
 
     def write_coarse(r, v):
@@ -744,12 +785,13 @@
         skip[r] = v
 
     fold(BACK4C, G4c, 0, 128, 8, 64, 2, write_coarse)
-    fold(BACK4F, G4, 128, 64, 16, 128, 4, write_skip)
+
 
     arrive(FIRST)
     pad_and_shift(FIRST, first_act, 16, 4, 64, 3, R.x[3], (128, 320, 512), False)
 
     arrive(SECOND)
+    start(BACK4F)
     pad_and_shift(SECOND, second_act, 8, 4, 128, 2, R.x[2], (0, 128, 256), False)
     third_act, delta3 = R.third_act, R.delta3
 
@@ -771,10 +813,16 @@
     send_backward(BACK3, rims_of(delta3, 8, 64, 128, 2, R.kt[2]), G3, 0, 128, 8, 4)
     start(BACK3)
 
+
     weight_terms(R.x[2], 128, R.d[2], 128, dil[2], 16, R.w[2])
+    arrive(BACK4F)
+    fold(BACK4F, G4, 128, 64, 16, 128, 4, write_skip)
     arrive(THIRD)
     pad_and_shift(THIRD, third_act, 8, 2, 128, 3, R.x[3], (0, 192, 384), True)
 
+    weight_terms(R.x[3], 192, R.d[3], 64, dil[3], 24, R.w[3])
+    put_terms(R.pay[0], ((R.w[3], 192, 64), (R.w[2], 128, 128)))
+    sum_a.first()
     arrive(BACK3)
     delta2 = R.delta2
 
@@ -792,16 +840,15 @@
     send_backward(BACK2, rims_of(delta2, 8, 64, 128, 1, R.kt[1]), G2, 0, 64, 8, 4)
     start(BACK2)
 
-    weight_terms(R.x[1], 64, R.d[1], 128, dil[1], 16, R.w[1])
-    weight_terms(R.x[3], 192, R.d[3], 64, dil[3], 24, R.w[3])
-    put_terms(R.pay[0], ((R.w[3], 192, 64), (R.w[2], 128, 128), (R.w[1], 64, 128)))
-    sum_a.first()
     state = R.state
 
     def write_state(r, v):
         state[r] = (v + columns[3]).astype(BF)
 
 
+    weight_terms(R.x[1], 64, R.d[1], 128, dil[1], 16, R.w[1])
+    sum_a.second()
+    conv(R.x[3], 576, R.kf[3], dil[3], 8, write_state)
     arrive(BACK2)
     delta1 = R.delta1
     repeat = jnp.where((u & (LANES - 1)) == (w >> 1), 0.25, 0.0).astype(BF)
@@ -814,7 +861,7 @@
     fold(BACK2, G2, 0, 64, 8, 64, 4, write_delta1)
     spread_delta(delta1, 16, 64, 0, R.d[0])
     weight_terms(R.x[0], 64, R.d[0], 64, dil[0], 24, R.w[0])
-    put_terms(R.pay[1], ((R.w[0], 64, 64),))
+    put_terms(R.pay[1], ((R.w[1], 64, 128), (R.w[0], 64, 64)))
     sum_b.first()
     G1 = R.g[0]
 
@@ -822,13 +869,16 @@
         G1[r] = v
 
     conv(R.d[0], 192, R.kt[0], dil[0], 24, write_g1)
+    sum_a.third()
     sum_b.second()
     send_backward(BACK1, rims_of(delta1, 16, 128, 64, 0, R.kt[0]), G1, 0, 64, 16, 4)
     start(BACK1)
 
-    sum_a.second()
-    conv(R.x[3], 576, R.kf[3], dil[3], 8, write_state)
+    sum_a.fourth()
+    conv(R.x[3], 576, R.kf[3], dil[3], 8, write_state, 8)
     sum_b.third()
+    channels_first(state, R.state_out, 1)
+    sum_a.fifth()
     arrive(BACK1)
     grad = R.grad
 
@@ -836,18 +886,13 @@
         grad[r] = v
 
     fold(BACK1, G1, 0, 64, 16, 128, 4, write_grad)
-    sum_a.third()
     sum_b.fourth()
-    conv(R.x[3], 576, R.kf[3], dil[3], 8, write_state, 8)
-    sum_a.fourth()
+    channels_first(grad, R.grad_out, 2)
+    sum_a.sixth()
+    take_terms(R.res[0], ((R.wo[3], R.bo[3], 192, 64), (R.wo[2], R.bo[2], 128, 128)))
     sum_b.fifth()
-    channels_first(state, R.state_out, 1)
-    channels_first(grad, R.grad_out, 2)
-    sum_a.fifth()
     sum_b.sixth()
-    take_terms(R.res[1], ((R.wo[0], R.bo[0], 64, 64),))
-    sum_a.sixth()
-    take_terms(R.res[0], ((R.wo[3], R.bo[3], 192, 64), (R.wo[2], R.bo[2], 128, 128), (R.wo[1], R.bo[1], 64, 128)))
+    take_terms(R.res[1], ((R.wo[1], R.bo[1], 64, 128), (R.wo[0], R.bo[0], 64, 64)))
 
     sum_a.finish()
     sum_b.finish()
@@ -856,7 +901,7 @@
             copy.wait_send()
 
 
-PIECE = (96, 16)
+PIECE = (80, 32)
 
 
 def run_net(tiles, members, scale, operands):
@@ -903,10 +948,10 @@
         psem=[D((4,)) for q in PIECE],
         xysem=[D((4, n_xy)) for q in PIECE],
         zsem=[D((2, n_z)) for q in PIECE],
-        cs=[V((sent, C, LANES), BF) for C, m, sent in EXCHANGES],
-        rs=[V((2, m, C, LANES), BF) for C, m, sent in EXCHANGES],
-        cr=[V((6, C, LANES), BF) for C, m, sent in EXCHANGES],
-        rr=[V((2, m, C, LANES), BF) for C, m, sent in EXCHANGES],
+        cs=[V((sent, C * m * H // LANES, LANES), BF) for C, m, H, sent in EXCHANGES],
+        rs=[V((2, m * H // 16, C, LANES), BF) for C, m, H, sent in EXCHANGES],
+        cr=[V((6, C * m * H // LANES, LANES), BF) for C, m, H, sent in EXCHANGES],
+        rr=[V((2, m * H // 16, C, LANES), BF) for C, m, H, sent in EXCHANGES],
     )
     smem = pl.BlockSpec(memory_space=pltpu.SMEM)
     vmem = pl.BlockSpec(memory_space=pltpu.VMEM)

time: 101 us -> 89.9 us (0.89)
  Pallas kernels: 91.5 us -> 80.1 us
    pallas_call x1, Pallas kernels: 91.5 us -> 80.1 us  [run_net(): pl.pallas_call(functools.partial(net_kernel, tiles, members, scale, (inpu...]
where the time goes in v3:
time: 89.9 us; the launch traced here: 89.7 us
  Pallas kernels  80.1 us (89%)
  local copies, waits for them, and re-layouts  8.84 us (10%)
    pallas_call x1, Pallas kernels, run_net(): pl.pallas_call(functools.partial(net_kernel, tiles, members, scale, (inpu...  80.1 us
    unnamed x28, local copies, waits for them, and re-layouts  8.84 us

profile of v3, /device:TPU:1, one launch (start us, length us, event | category | flops | bytes accessed | tf_op | source)
XLA Modules:
  0.0 89.7 jit_solution(14143295925863178167)
XLA Ops:
  0.6 80.1 %shard_map.195 = (bf16[64,16,128]{2,1,0:T(8,128)(2,1)}, f32[64,16,128]{2,1,0:T(8,128)}, f32[9,64,64]{2,1,0:T(8,128)}, f32[9,64,128]{2,1,0:T(8,128)}, f32[9,128,1...) custom-call(s32[1,4]{1,0:T(1,128)} %refs_0_.1, ...), custom_call_target="tpu_custom_call" | custom-call | tf_op jit(solution)/shard_map/pallas_call | solution.py:967
  80.8 0.0 copy-start.2
  80.8 1.7 %copy.32 = bf16[1,1,64,16,128]{4,3,2,1,0:T(8,128)(2,1)} copy(bf16[1,1,64,16,128]{4,3,2,1,0:T(8,128)(2,1)} %bitcast.18) | data formatting | bytes 524288
  82.5 0.0 copy-done.2
  82.5 0.0 copy-start.4
  82.5 0.0 copy-start.3
  82.5 0.8 copy.33
  83.3 0.3 copy-done.4
  83.7 0.0 copy-start.1
  83.7 0.7 copy.34
  84.4 0.0 copy-done.3
  84.4 0.7 copy.35
  85.1 0.0 copy-done.1
  85.1 0.0 copy-start
  85.1 0.8 copy.36
  85.9 0.5 copy-done
  86.4 0.0 copy-start.8
  86.4 0.8 copy.37
  87.2 0.0 copy-done.8
  87.2 0.0 copy-start.7
  87.2 0.5 copy.38
  87.7 0.2 copy-done.7
  87.9 0.0 copy-start.6
  87.9 0.5 copy.39
  88.4 0.2 copy-done.6
  88.5 0.0 copy-start.5
  88.5 0.5 copy.40
  89.1 0.1 copy-done.5
  89.1 0.5 copy.41
Async XLA Ops:
  80.8 1.7 %copy-start.2 = (f32[64,16,128]{2,1,0:T(8,128)S(1)}, f32[64,16,128]{2,1,0:T(8,128)}, u32[]{:S(2)}) copy-start(f32[64,16,128]{2,1,0:T(8,128)} %get-tuple-element.21) | copy-start | bytes 1572868
  82.5 1.1 %copy-start.4 = (f32[9,64,64]{2,1,0:T(8,128)S(1)}, f32[9,64,64]{2,1,0:T(8,128)}, u32[]{:S(2)}) copy-start(f32[9,64,64]{2,1,0:T(8,128)} %get-tuple-element.42) | copy-start | bytes 442372
  82.5 1.8 %copy-start.3 = (f32[9,64,128]{2,1,0:T(8,128)S(1)}, f32[9,64,128]{2,1,0:T(8,128)}, u32[]{:S(2)}) copy-start(f32[9,64,128]{2,1,0:T(8,128)} %get-tuple-element.23) | copy-start | bytes 884740
  83.7 1.4 %copy-start.1 = (f32[9,128,128]{2,1,0:T(8,128)S(1)}, f32[9,128,128]{2,1,0:T(8,128)}, u32[]{:S(2)}) copy-start(f32[9,128,128]{2,1,0:T(8,128)} %get-tuple-element.44) | copy-start | bytes 1769476
  85.1 1.3 %copy-start = (f32[9,64,192]{2,1,0:T(8,128)S(1)}, f32[9,64,192]{2,1,0:T(8,128)}, u32[]{:S(2)}) copy-start(f32[9,64,192]{2,1,0:T(8,128)} %get-tuple-element.45) | copy-start | bytes 1327108
  86.4 0.8 copy-start.8
  87.2 0.7 copy-start.7
  87.9 0.7 copy-start.6
  88.5 0.6 copy-start.5

commit v4 on v3

--- a/solution.py
+++ b/solution.py
@@ -64,8 +64,8 @@
     return m.bit_length() - 1
 
 
-def column_pick(H, W, m, code_right, code_left, shape=(LANES, LANES)):
-    lane = iota(shape, 1)
+def column_pick(H, W, m, code_right, code_left):
+    lane = iota((1, LANES), 1)
     code = jnp.where(lane < 64, code_right, code_left)
     idx = lane & 63
     row, col = idx >> log2(m), idx & (m - 1)
@@ -76,7 +76,7 @@
 
 
 def halo_target(H, m, code, row):
-    w = iota((LANES, LANES), 1)
+    w = iota((1, LANES), 1)
     picked = jnp.where((code & 1) == 1, H - m + row, row)
     flip = (code >> 1) == 1
     k = w - (LANES - m)
@@ -85,69 +85,65 @@
     return jnp.where(w >= LANES - m, left, jnp.where(w < m, right, -1))
 
 
+def take(rows, target):
+    return onehot(iota((rows, target.shape[1]), 0) == target)
+
+
 def shift_matrix(W, d):
-    source = iota((2 * LANES, 2 * LANES), 0)
-    out = iota((2 * LANES, 2 * LANES), 1)
+    out = iota((1, 2 * LANES), 1)
     j = out & (LANES - 1)
     minus = jnp.where(j >= d, j - d, 2 * LANES + j - d)
     plus = jnp.where(j + d < W, j + d, LANES + j + d - W)
-    return onehot((source == jnp.where(out < LANES, minus, plus)) & (j < W))
-
-
-def reversal(W, code, shape=(LANES, LANES)):
-    u, w = iota(shape, 0), iota(shape, 1)
-    flip = (code >> 1) == 1
-    return (u == jnp.where(flip, W - 1 - w, w)) & (w < W)
+    target = jnp.where(out < LANES, minus, plus)
+    return take(2 * LANES, jnp.where(j < W, target, -1))
+
+
+def turned(W, code):
+    w = iota((1, LANES), 1)
+    return jnp.where(w < W, jnp.where((code >> 1) == 1, W - 1 - w, w), -1024)
 
 
 def pick_rows_matrix(W, code):
-    u = iota((2 * LANES, LANES), 0)
-    w = iota((2 * LANES, LANES), 1)
-    flip = (code >> 1) == 1
-    hit = (u & (LANES - 1)) == jnp.where(flip, W - 1 - w, w)
-    return onehot(hit & ((u >> 7) == (code & 1)) & (w < W))
+    return take(2 * LANES, turned(W, code) + LANES * (code & 1))
 
 
 def return_rows_matrix(W, code_upper, code_lower, last):
-    u = iota((2 * LANES, LANES), 0)
-    w = iota((2 * LANES, LANES), 1)
-    code = jnp.where(u < LANES, code_upper, code_lower)
-    flip = (code >> 1) == 1
-    hit = (u & (LANES - 1)) == jnp.where(flip, W - 1 - w, w)
-    return onehot(hit & ((code & 1) == last) & (w < W))
+    parts = []
+    for code in (code_upper, code_lower):
+        parts.append(take(LANES, jnp.where((code & 1) == last, turned(W, code), -1)))
+    return jnp.concatenate(parts, axis=0)
 
 
 def rim_matrix(H, m, code_above, code_below, collapse):
     shape = (2 * LANES, LANES)
-    u, lane = iota(shape, 0), iota(shape, 1)
-    src = u & (LANES - 1)
+    u, lane = iota(shape, 0), iota((1, LANES), 1)
+    src = u
     if collapse:
-        src = ((src >> 3) << 1) + ((src & 3) >> 1)
-    src = src + (u >> 7) * 1024
+        src = (((u & (LANES - 1)) >> 3) << 1) + ((u & 3) >> 1) + ((u >> 7) << 7)
     idx = lane & 63
     row, k = idx >> log2(m), idx & (m - 1)
     leftward = lane < 64
     valid = idx < H * m
-    parts = [onehot((src == (row + m) * m + k + jnp.where(leftward, 1024, 0)) & valid)]
+    targets = [jnp.where(valid, (row + m) * m + k + jnp.where(leftward, LANES, 0), -1)]
     for code, base in ((code_above, 0), (code_below, H + m)):
         picked = jnp.where((code & 1) == 1, row - (H - m), row)
-        flip = jnp.where((code >> 1) == 1, 1, 0)
+        flip = (code >> 1) & 1
         kk = jnp.where(flip == 1, m - 1 - k, k)
         left_side = jnp.where(leftward, 1 - flip, flip)
-        hit = src == (picked + base) * m + kk + left_side * 1024
-        parts.append(onehot(hit & valid & (picked >= 0) & (picked < m)))
-    return jnp.concatenate(parts, axis=1)
+        inside = valid & (picked >= 0) & (picked < m)
+        targets.append(jnp.where(inside, (picked + base) * m + kk + left_side * LANES, -1))
+    return jnp.concatenate([onehot(src == target) for target in targets], axis=1)
 
 
 def edge_matrix(H, d):
-    u, v = iota((LANES, LANES), 0), iota((LANES, LANES), 1)
+    v = iota((1, LANES), 1)
     row, k = v >> 2, v & 3
     parts = []
     for a in range(3):
         h = row - RIM - (a - 1) * d
         inside = (h >= 0) & (h < H)
-        parts.append(onehot((u == 4 * h + (4 - d + k)) & inside & (k < d)))
-        parts.append(onehot((u == 64 + 4 * h + (k - 4 + d)) & inside & (k >= 4 - d)))
+        parts.append(take(LANES, jnp.where(inside & (k < d), 4 * h + (4 - d + k), -1)))
+        parts.append(take(LANES, jnp.where(inside & (k >= 4 - d), 64 + 4 * h + (k - 4 + d), -1)))
     return jnp.concatenate(parts, axis=1)
 
 
@@ -159,6 +155,52 @@
 
 def stacked(values):
     return values.reshape(values.shape[0] * values.shape[1], values.shape[2])
+
+
+def eye(n):
+    return onehot(iota((n, n), 0) == iota((n, n), 1))
+
+
+def to_rows():
+    u, w = iota((256, 256), 0), iota((256, 256), 1)
+    return onehot(w == ((u & 15) << 4) + (u >> 4))
+
+
+def channels_first(x_ref, out, parts):
+    turn = to_rows()
+    for g in range(4):
+        block = cat([x_ref[h, 16 * g : 16 * g + 16, :] for h in range(16)], 0)
+        y = mm(turn, block) if parts == 1 else mm(turn, split(block))
+        if parts == 2:
+            y = y[:, :LANES] + y[:, LANES:]
+        out[16 * g : 16 * g + 16] = y.astype(out.dtype).reshape(16, 16, LANES)
+
+
+def get(ref, start_row, count):
+    n_xy, q = ref.shape[1], ref.shape[2]
+    parts, done = [], 0
+    while done < count:
+        piece, inner = divmod(start_row + done, q)
+        n = min(q - inner, count - done)
+        parts.append(ref[piece // n_xy, piece % n_xy, inner : inner + n, :])
+        done += n
+    return cat(parts, 0)
+
+
+def take_terms(ref, listed):
+    sel = [onehot(iota((64, LANES), 1) == iota((64, LANES), 0) + 64 * k) for k in range(2)]
+    where = 0
+    for w_out, b_out, C, O in listed:
+        for a in range(3):
+            chunk, side = (a // 2, sel[a % 2]) if O == 64 else (a, eye(LANES))
+            for e in range(3):
+                block = get(ref, where + chunk * 3 * C + e * C, C)
+                w_out[3 * a + e] = block.astype(F32) if O > C else mm_nt(side, block)
+        where += (2 if O == 64 else 3) * 3 * C
+    for w_out, b_out, C, O in listed:
+        block = get(ref, where, ONES)
+        b_out[...] = mm_nt(block, sel[1])[0:1] if O == 64 else block.astype(F32)[0:1]
+        where += ONES
 
 
 class Refs:
@@ -411,10 +453,10 @@
     PICK = {(16, 4): 0, (8, 4): 1, (8, 2): 2}
     for (H, m), where in PICK.items():
         _, col = column_pick(H, 128 if H == 16 else 64, m, codes[3], codes[2])
-        picks[where] = onehot(iota((LANES, LANES), 0) == col)
+        picks[where] = take(LANES, col)
 
     def pick_rows(H, m):
-        row, _ = column_pick(H, 128 if H == 16 else 64, m, codes[3], codes[2], (1, LANES))
+        row, _ = column_pick(H, 128 if H == 16 else 64, m, codes[3], codes[2])
         return row
 
     for X3, D3, (C, O, H, _) in zip(R.x, R.d, LAYERS):
@@ -450,8 +492,7 @@
         return listed
 
     def halo_rows(Z, H, m, code, rows):
-        lane = iota((LANES, LANES), 0)
-        mats = cat([onehot(lane == halo_target(H, m, code, r)) for r in rows], 1)
+        mats = cat([take(LANES, halo_target(H, m, code, r)) for r in rows], 1)
         y = mm(Z, mats).astype(BF)
         return cat([y[:, LANES * q : LANES * (q + 1)] for q in range(len(rows))], 0)
 
@@ -477,10 +518,10 @@
         def prepare(core, halo):
             if not refine:
                 return core, halo
-            u, w = iota((LANES, LANES), 0), iota((LANES, LANES), 1)
-            core = mm(core, onehot(u == (w >> 1))).astype(BF)
+            w = iota((1, LANES), 1)
+            core = mm(core, take(LANES, w >> 1)).astype(BF)
             near = jnp.where(w < 4, w >> 1, jnp.where(w >= LANES - 4, 64 + (w >> 1), -1))
-            return core, mm(halo, onehot(u == near)).astype(BF)
+            return core, mm(halo, take(LANES, near)).astype(BF)
 
         def body(g, carry):
             rows = [m * g + q for q in range(m)]
@@ -547,9 +588,8 @@
         lax.fori_loop(0, H // 4, body, 0, unroll=True)
 
     def rims_of(x_ref, H, W, O, layer, K):
-        row, col = column_pick(H, W, RIM, 1, 0, (1, LANES))
-        _, col_full = column_pick(H, W, RIM, 1, 0)
-        pick = onehot(iota((LANES, LANES), 0) == col_full)
+        row, col = column_pick(H, W, RIM, 1, 0)
+        pick = take(LANES, col)
         edges = jnp.zeros((O, LANES), F32)
         for g in range(H // 4):
             y = mm(stacked(x_ref[4 * g : 4 * g + 4]), pick)
@@ -601,9 +641,6 @@
                 h = m * g + q
                 write(h, G[h + m, c0 : c0 + C, :] + y[q * C : (q + 1) * C])
 
-    def eye(n):
-        return onehot(iota((n, n), 0) == iota((n, n), 1))
-
     def forward_weights(i):
         k, kf = R.k[i], R.kf[i]
         if i == 1:
@@ -632,22 +669,12 @@
         n = row.shape[1]
         return jnp.sum(jnp.where(iota((n, n), 0) == iota((n, n), 1), row, 0.0), axis=1, keepdims=True)
 
-    pu, pw = iota((256, 256), 0), iota((256, 256), 1)
-    to_rows = onehot(pw == ((pu & 15) << 4) + (pu >> 4))
-
     def rows_first(x_ref, out):
+        turn = to_rows()
         for g in range(4):
-            y = mm(to_rows, stacked(x_ref[16 * g : 16 * g + 16])).astype(BF)
+            y = mm(turn, stacked(x_ref[16 * g : 16 * g + 16])).astype(BF)
             for h in range(16):
                 out[h, 16 * g : 16 * g + 16, :] = y[16 * h : 16 * h + 16]
-
-    def channels_first(x_ref, out, parts):
-        for g in range(4):
-            block = cat([x_ref[h, 16 * g : 16 * g + 16, :] for h in range(16)], 0)
-            y = mm(to_rows, block) if parts == 1 else mm(to_rows, split(block))
-            if parts == 2:
-                y = y[:, :LANES] + y[:, LANES:]
-            out[16 * g : 16 * g + 16] = y.astype(out.dtype).reshape(16, 16, LANES)
 
     def put(ref, start_row, value):
         q = ref.shape[2]
@@ -657,16 +684,6 @@
             n = min(q - inner, value.shape[0] - done)
             ref[piece // n_xy, piece % n_xy, inner : inner + n, :] = value[done : done + n].astype(BF)
             done += n
-
-    def get(ref, start_row, count):
-        q = ref.shape[2]
-        parts, done = [], 0
-        while done < count:
-            piece, inner = divmod(start_row + done, q)
-            n = min(q - inner, count - done)
-            parts.append(ref[piece // n_xy, piece % n_xy, inner : inner + n, :])
-            done += n
-        return cat(parts, 0)
 
     def put_terms(ref, listed):
         where = 0
@@ -681,21 +698,6 @@
             where += ONES
         pieces = ref.shape[0] * ref.shape[1] * ref.shape[2]
         put(ref, where, jnp.zeros((pieces - where, LANES), BF))
-
-    def take_terms(ref, listed):
-        sel = [onehot(iota((64, LANES), 1) == iota((64, LANES), 0) + 64 * k) for k in range(2)]
-        where = 0
-        for w_out, b_out, C, O in listed:
-            for a in range(3):
-                chunk, side = (a // 2, sel[a % 2]) if O == 64 else (a, eye(LANES))
-                for e in range(3):
-                    block = get(ref, where + chunk * 3 * C + e * C, C)
-                    w_out[3 * a + e] = block.astype(F32) if O > C else mm_nt(side, block)
-            where += (2 if O == 64 else 3) * 3 * C
-        for w_out, b_out, C, O in listed:
-            block = get(ref, where, ONES)
-            b_out[...] = mm_nt(block, sel[1])[0:1] if O == 64 else block.astype(F32)[0:1]
-            where += ONES
 
     rows_first(R.fields_in, R.fields)
     send_forward(FIELDS, R.fields, 16, 128, 4, 64)
@@ -877,7 +879,6 @@
     sum_a.fourth()
     conv(R.x[3], 576, R.kf[3], dil[3], 8, write_state, 8)
     sum_b.third()
-    channels_first(state, R.state_out, 1)
     sum_a.fifth()
     arrive(BACK1)
     grad = R.grad
@@ -887,12 +888,9 @@
 
     fold(BACK1, G1, 0, 64, 16, 128, 4, write_grad)
     sum_b.fourth()
-    channels_first(grad, R.grad_out, 2)
     sum_a.sixth()
-    take_terms(R.res[0], ((R.wo[3], R.bo[3], 192, 64), (R.wo[2], R.bo[2], 128, 128)))
     sum_b.fifth()
     sum_b.sixth()
-    take_terms(R.res[1], ((R.wo[1], R.bo[1], 64, 128), (R.wo[0], R.bo[0], 64, 64)))
 
     sum_a.finish()
     sum_b.finish()
@@ -920,8 +918,6 @@
         w=[V((3 * C + ONES, 256 if O == 64 else 384), F32) for C, O, _ in sizes],
         fields=V((16, 64, LANES), BF),
         cot=V((16, 64, LANES), BF),
-        state=V((16, 64, LANES), BF),
-        grad=V((16, 64, LANES), F32),
         first_act=V((16, 64, LANES), BF),
         slope1=V((16, 64, LANES), F32),
         pooled=V((8, 64, LANES), BF),
@@ -944,7 +940,6 @@
         half=[V((n_xy, q, LANES), BF) for q in PIECE],
         bxy=[V((n_xy, q, LANES), BF) for q in PIECE],
         bz=[V((n_z, q, LANES), BF) for q in PIECE],
-        res=[V((2, n_xy, q, LANES), BF) for q in PIECE],
         psem=[D((4,)) for q in PIECE],
         xysem=[D((4, n_xy)) for q in PIECE],
         zsem=[D((2, n_z)) for q in PIECE],
@@ -957,10 +952,9 @@
     vmem = pl.BlockSpec(memory_space=pltpu.VMEM)
     shape = jax.ShapeDtypeStruct
     outputs = Refs(
-        state_out=shape((64, 16, LANES), BF),
-        grad_out=shape((64, 16, LANES), F32),
-        wo=[shape((9, C, O) if O > C else (9, O, C), F32) for C, O, _, _ in LAYERS],
-        bo=[shape((1, O), F32) for C, O, _, _ in LAYERS],
+        state=shape((16, 64, LANES), BF),
+        grad=shape((16, 64, LANES), F32),
+        res=[shape((2, n_xy, q, LANES), BF) for q in PIECE],
     )
     inputs = Refs(**operands)
     flat_in, flat_out, flat_scratch = (list(flatten(part)) for part in (inputs, outputs, scratch))
@@ -975,6 +969,27 @@
         ),
     )(*flat_in)
 
+def finish_kernel(state, grad, early, late, state_out, grad_out, w1, w2, w3, w4, b1, b2, b3, b4):
+    channels_first(state, state_out, 1)
+    channels_first(grad, grad_out, 2)
+    take_terms(early, ((w4, b4, 192, 64), (w3, b3, 128, 128)))
+    take_terms(late, ((w2, b2, 64, 128), (w1, b1, 64, 64)))
+
+
+def run_finish(raw):
+    vmem = pl.BlockSpec(memory_space=pltpu.VMEM)
+    shape = jax.ShapeDtypeStruct
+    outputs = [shape((64, 16, LANES), BF), shape((64, 16, LANES), F32)]
+    outputs += [shape((9, C, O) if O > C else (9, O, C), F32) for C, O, _, _ in LAYERS]
+    outputs += [shape((1, O), F32) for C, O, _, _ in LAYERS]
+    return pl.pallas_call(
+        finish_kernel,
+        out_shape=tuple(outputs),
+        in_specs=[vmem] * len(raw),
+        out_specs=(vmem,) * len(outputs),
+        compiler_params=pltpu.CompilerParams(vmem_limit_bytes=32 * 2**20),
+    )(*raw)
+
 
 def shards(tiles, members, fields, cotangent, k1, k2, k3, k4, off1, off2, off3, off4, codes, dilations):
     operands = dict(
@@ -986,7 +1001,7 @@
         off=[off1[None, :], off2[None, :], off3[None, :], off4[None, :]],
     )
     scale = 1.0 / math.sqrt(members * tiles * fields.shape[3] * fields.shape[4])
-    state, grad, *rest = run_net(tiles, members, scale, operands)
+    state, grad, *rest = run_finish(run_net(tiles, members, scale, operands))
     rest[1] = jnp.swapaxes(rest[1], 1, 2)
     return (state[None, None], grad[None, None], *rest[:4], *[b[0] for b in rest[4:]])
 

time: 89.9 us -> 86.3 us (0.960)
  local copies, waits for them, and re-layouts: 8.84 us -> 4.02 us
  Pallas kernels: 80.1 us -> 81.4 us
    unnamed x28 -> x8, local copies, waits for them, and re-layouts: 8.84 us -> 4.02 us
    pallas_call x0 -> x1, Pallas kernels: none -> 1.92 us  [run_finish(): pl.pallas_call(finish_kernel, out_shape=tuple(outputs), in_specs=[vmem] *...]
where the time goes in v4:
time: 86.3 us; the launch traced here: 86 us
  Pallas kernels  81.4 us (94%)
  local copies, waits for them, and re-layouts  4.02 us (5%)
    pallas_call x1, Pallas kernels, run_net(): pl.pallas_call(functools.partial(net_kernel, tiles, members, scale, (inpu...  79.4 us
    unnamed x8, local copies, waits for them, and re-layouts  4.02 us
    pallas_call x1, Pallas kernels, run_finish(): pl.pallas_call(finish_kernel, out_shape=tuple(outputs), in_specs=[vmem] *...  1.92 us

profile of v4, /device:TPU:1, one launch (start us, length us, event | category | flops | bytes accessed | tf_op | source)
XLA Modules:
  0.0 86.0 jit_solution(2616427692807640793)
XLA Ops:
  0.6 79.4 %shard_map.195 = (bf16[16,64,128]{2,1,0:T(8,128)(2,1)}, f32[16,64,128]{2,1,0:T(8,128)}, bf16[2,16,80,128]{3,2,1,0:T(8,128)(2,1)}, bf16[2,16,32,128]{3,2,1,0:T(8,128)(2,1)}) custom-call(s32[1,4]{1,0:T(1,128)} %refs_0_.1, s32[4]{0:T(128)} %refs_1_.1, bf16[64,16,128]{2,1,0:T(8,128)(2,1)} %bitcast.14, bf16[64,16,128]{2,1,0:T(8,128)(2,1)} %bitcast.15, ...), custom_call_target="tpu_custom_call" | custom-call | tf_op jit(solution)/shard_map/pallas_call | solution.py:961
  80.1 0.0 copy-start
  80.1 1.1 %copy-done = bf16[2,16,80,128]{3,2,1,0:T(8,128)(2,1)S(1)} copy-done((bf16[2,16,80,128]{3,2,1,0:T(8,128)(2,1)S(1)}, bf16[2,16,80,128]{3,2,1,0:T(8,128)(2,1)}, u32[]{:S(2)}) %copy-start) | copy-done | bytes 655384
  81.2 0.0 copy-start.1
  81.2 1.0 %copy-done.1 = f32[16,64,128]{2,1,0:T(8,128)S(1)} copy-done((f32[16,64,128]{2,1,0:T(8,128)S(1)}, f32[16,64,128]{2,1,0:T(8,128)}, u32[]{:S(2)}) %copy-start.1) | copy-done | bytes 524312
  82.2 0.0 copy-start.2
  82.2 0.9 %copy-done.2 = bf16[16,64,128]{2,1,0:T(8,128)(2,1)S(1)} copy-done((bf16[16,64,128]{2,1,0:T(8,128)(2,1)S(1)}, bf16[16,64,128]{2,1,0:T(8,128)(2,1)}, u32[]{:S(2)}) %copy-start.2) | copy-done | bytes 262168
  83.2 0.0 copy-start.3
  83.2 0.9 %copy-done.3 = bf16[2,16,32,128]{3,2,1,0:T(8,128)(2,1)S(1)} copy-done((bf16[2,16,32,128]{3,2,1,0:T(8,128)(2,1)S(1)}, bf16[2,16,32,128]{3,2,1,0:T(8,128)(2,1)}, u32[]{:S(2)}) %copy-start.3) | copy-done | bytes 262168
  84.1 1.9 %shard_map.196 = (bf16[64,16,128]{2,1,0:T(8,128)(2,1)}, f32[64,16,128]{2,1,0:T(8,128)}, f32[9,64,64]{2,1,0:T(8,128)}, f32[9,64,128]{2,1,0:T(8,128)}, f32[9,128,1...) custom-call(bf16[16,64,128]{2,1,0:T(8,128)(2,1)S(1)} %copy-done.2, ...), custom_call_target="tpu_custom_call" | custom-call | tf_op jit(solution)/shard_map/pallas_call | solution.py:985
Async XLA Ops:
  80.1 1.1 %copy-start = (bf16[2,16,80,128]{3,2,1,0:T(8,128)(2,1)S(1)}, bf16[2,16,80,128]{3,2,1,0:T(8,128)(2,1)}, u32[]{:S(2)}) copy-start(bf16[2,16,80,128]{3,2,1,0:T(8,128)(2,1)} %get-tuple-element.26.early) | copy-start | bytes 1966084
  81.2 1.0 %copy-start.1 = (f32[16,64,128]{2,1,0:T(8,128)S(1)}, f32[16,64,128]{2,1,0:T(8,128)}, u32[]{:S(2)}) copy-start(f32[16,64,128]{2,1,0:T(8,128)} %get-tuple-element.25.grad) | copy-start | bytes 1572868
  82.2 0.9 %copy-start.2 = (bf16[16,64,128]{2,1,0:T(8,128)(2,1)S(1)}, bf16[16,64,128]{2,1,0:T(8,128)(2,1)}, u32[]{:S(2)}) copy-start(bf16[16,64,128]{2,1,0:T(8,128)(2,1)} %get-tuple-element.24.state) | copy-start | bytes 786436
  83.2 0.9 %copy-start.3 = (bf16[2,16,32,128]{3,2,1,0:T(8,128)(2,1)S(1)}, bf16[2,16,32,128]{3,2,1,0:T(8,128)(2,1)}, u32[]{:S(2)}) copy-start(bf16[2,16,32,128]{3,2,1,0:T(8,128)(2,1)} %get-tuple-element.27.late) | copy-start | bytes 786436

commit v5 on v4

--- a/solution.py
+++ b/solution.py
@@ -303,8 +303,8 @@
         for copy in copies[name]:
             copy.start()
 
-    def arrive(name):
-        for copy in copies[name]:
+    def arrive(name, slots=slice(0, 8)):
+        for copy in copies[name][slots]:
             copy.wait_recv()
 
     n_ens, n_low = members, 4
@@ -427,7 +427,74 @@
             each(n_xy, lambda k: self.back_copy(k).wait_send())
             each(n_z, lambda k: self.z_copy(k).wait_send())
 
-    sum_a, sum_b = Sum(0), Sum(1)
+    class LateSum:
+        def __init__(self, tag):
+            self.pay, self.buf_xy, self.buf_z = R.pay[tag], R.bxy[tag], R.bz[tag]
+            self.res, self.xy_sem, self.z_sem = R.res[tag], R.xysem[tag], R.zsem[tag]
+            self.here = z * 2 + core
+
+        def xy_copy(self, k):
+            p = xy_peer(k)
+            sems = self.xy_sem.at[0, k], self.xy_sem.at[1, xy]
+            return remote(self.pay.at[0, p], self.buf_xy.at[xy], *sems, at(z, p, core))
+
+        def xy_arrival(self, k):
+            p = xy_peer(k)
+            sems = self.xy_sem.at[0, k], self.xy_sem.at[1, p]
+            return remote(self.pay.at[0, p], self.buf_xy.at[p], *sems, at(z, p, core))
+
+        def z_copy(self, k):
+            p = lax.rem(self.here + k, 2 * n_z)
+            mine = self.buf_z.at[self.here]
+            sems = self.z_sem.at[0, k], self.z_sem.at[1, self.here]
+            return remote(mine, mine, *sems, at(lax.div(p, 2), xy, lax.rem(p, 2)))
+
+        def z_arrival(self, k):
+            p = lax.rem(self.here + k, 2 * n_z)
+            theirs = self.buf_z.at[p]
+            sems = self.z_sem.at[0, k], self.z_sem.at[1, p]
+            return remote(theirs, theirs, *sems, at(lax.div(p, 2), xy, lax.rem(p, 2)))
+
+        def back_copy(self, k):
+            mine = self.res.at[0, xy]
+            sems = self.xy_sem.at[2, k], self.xy_sem.at[3, xy]
+            return remote(mine, mine, *sems, at(z, xy_peer(k), core))
+
+        def back_arrival(self, k):
+            p = xy_peer(k)
+            theirs = self.res.at[0, p]
+            sems = self.xy_sem.at[2, k], self.xy_sem.at[3, p]
+            return remote(theirs, theirs, *sems, at(z, p, core))
+
+        def first(self):
+            each(n_xy, lambda k: self.xy_copy(k).start())
+            self.buf_xy[xy] = self.pay[0, xy]
+
+        def second(self):
+            each(n_xy, lambda k: self.xy_arrival(k).wait_recv())
+            total = self.buf_xy[0].astype(F32)
+            for p in range(1, n_xy):
+                total = total + self.buf_xy[p].astype(F32)
+            self.buf_z[self.here] = total.astype(BF)
+            each(2 * n_z, lambda k: self.z_copy(k).start())
+
+        def third(self):
+            each(2 * n_z, lambda k: self.z_arrival(k).wait_recv())
+            total = self.buf_z[0].astype(F32)
+            for p in range(1, 2 * n_z):
+                total = total + self.buf_z[p].astype(F32)
+            self.res[0, xy] = (total * scale).astype(BF)
+            each(n_xy, lambda k: self.back_copy(k).start())
+
+        def fourth(self):
+            each(n_xy, lambda k: self.back_arrival(k).wait_recv())
+
+        def finish(self):
+            each(n_xy, lambda k: self.xy_copy(k).wait_send())
+            each(n_xy, lambda k: self.back_copy(k).wait_send())
+            each(2 * n_z, lambda k: self.z_copy(k).wait_send())
+
+    sum_a, sum_b = Sum(0), LateSum(1)
 
     barrier = pltpu.get_barrier_semaphore()
 
@@ -438,6 +505,7 @@
         greet(device(offset))
     each(n_xy, lambda k: greet(at(z, xy_peer(k), core)))
     each(n_z, lambda k: greet(at(z_peer(k), xy, core)))
+    each(n_z, lambda k: greet(at(z_peer(k), xy, 1 - core)))
 
     codes = [R.codes[0, s] for s in range(4)]
     tile_rows = iota((8, LANES), 0) & 3
@@ -482,14 +550,11 @@
             rows = mm(both, pick_rows_matrix(W, codes[side]))
             R.rs[name][k] = pack_rows(rows.reshape(m, C, LANES), W)
 
-    def halo_arrays(name, width):
+    def halo_array(name, width, i):
         near = R.cr[name]
         low = iota((1, LANES), 1) < 64
-        listed = []
-        for i in range(3):
-            right, left = unpack(near[2 * i], width, False), unpack(near[2 * i + 1], width, True)
-            listed.append(jnp.where(low, right, left).astype(BF))
-        return listed
+        right, left = unpack(near[2 * i], width, False), unpack(near[2 * i + 1], width, True)
+        return jnp.where(low, right, left).astype(BF)
 
     def halo_rows(Z, H, m, code, rows):
         mats = cat([take(LANES, halo_target(H, m, code, r)) for r in rows], 1)
@@ -507,7 +572,8 @@
                 X3[r, offs[2] : offs[2] + C, :] = y[part, LANES:]
 
     def pad_and_shift(name, x_ref, H, m, C, layer, X3, offs, refine):
-        Z, Zu, Zl = halo_arrays(name, H * m)
+        arrive(name, slice(0, 2))
+        Z = halo_array(name, H * m, 0)
         W = LANES * H // 16
         S = shifts[layer]
         rr = R.rr[name]
@@ -530,6 +596,8 @@
             return carry
 
         lax.fori_loop(0, H // m, body, 0, unroll=True)
+        arrive(name, slice(2, 8))
+        Zu, Zl = halo_array(name, H * m, 1), halo_array(name, H * m, 2)
         core, halo = prepare(unpack_rows(rr[0], W), halo_rows(Zu, H, m, code_u, range(m)))
         fill(X3, 0, core, halo, C, S, offs, rep)
         core, halo = prepare(unpack_rows(rr[1], W), halo_rows(Zl, H, m, code_l, range(m)))
@@ -701,7 +769,7 @@
 
     rows_first(R.fields_in, R.fields)
     send_forward(FIELDS, R.fields, 16, 128, 4, 64)
-    pl.semaphore_wait(barrier, 6 + (n_xy - 1) + (n_z - 1))
+    pl.semaphore_wait(barrier, 6 + (n_xy - 1) + 2 * (n_z - 1))
     for copy in code_copies:
         copy.start()
     start(FIELDS)
@@ -725,7 +793,6 @@
 
     for copy in code_copies:
         copy.wait_recv()
-    arrive(FIELDS)
     pad_and_shift(FIELDS, R.fields, 16, 4, 64, 0, R.x[0], (0, 64, 128), False)
     first_act, slope1 = R.first_act, R.slope1
 
@@ -761,10 +828,9 @@
     send_backward(BACK4F, rims4[128:192], G4, 128, 64, 16, 4)
 
 
-    arrive(POOLED)
+    pad_and_shift(POOLED, pooled, 8, 4, 64, 1, R.x[1], (0, 64, 128), False)
     start(FIRST)
     start(BACK4C)
-    pad_and_shift(POOLED, pooled, 8, 4, 64, 1, R.x[1], (0, 64, 128), False)
     second_act, slope2 = R.second_act, R.slope2
     inside = iota((1, LANES), 1) < 64
 
@@ -789,12 +855,10 @@
     fold(BACK4C, G4c, 0, 128, 8, 64, 2, write_coarse)
 
 
-    arrive(FIRST)
     pad_and_shift(FIRST, first_act, 16, 4, 64, 3, R.x[3], (128, 320, 512), False)
 
-    arrive(SECOND)
+    pad_and_shift(SECOND, second_act, 8, 4, 128, 2, R.x[2], (0, 128, 256), False)
     start(BACK4F)
-    pad_and_shift(SECOND, second_act, 8, 4, 128, 2, R.x[2], (0, 128, 256), False)
     third_act, delta3 = R.third_act, R.delta3
 
     def write_third(r, v):
@@ -811,15 +875,16 @@
     def write_g3(r, v):
         G3[r] = v
 
-    conv(R.d[2], 384, R.kt[2], dil[2], 16, write_g3)
+    conv(R.d[2], 384, R.kt[2], dil[2], 4, write_g3)
+    conv(R.d[2], 384, R.kt[2], dil[2], 4, write_g3, 12)
     send_backward(BACK3, rims_of(delta3, 8, 64, 128, 2, R.kt[2]), G3, 0, 128, 8, 4)
     start(BACK3)
+    conv(R.d[2], 384, R.kt[2], dil[2], 8, write_g3, 4)
 
 
     weight_terms(R.x[2], 128, R.d[2], 128, dil[2], 16, R.w[2])
     arrive(BACK4F)
     fold(BACK4F, G4, 128, 64, 16, 128, 4, write_skip)
-    arrive(THIRD)
     pad_and_shift(THIRD, third_act, 8, 2, 128, 3, R.x[3], (0, 192, 384), True)
 
     weight_terms(R.x[3], 192, R.d[3], 64, dil[3], 24, R.w[3])
@@ -838,9 +903,11 @@
     def write_g2(r, v):
         G2[r] = v
 
-    conv(R.d[1], 384, R.kt[1], dil[1], 16, write_g2)
+    conv(R.d[1], 384, R.kt[1], dil[1], 4, write_g2)
+    conv(R.d[1], 384, R.kt[1], dil[1], 4, write_g2, 12)
     send_backward(BACK2, rims_of(delta2, 8, 64, 128, 1, R.kt[1]), G2, 0, 64, 8, 4)
     start(BACK2)
+    conv(R.d[1], 384, R.kt[1], dil[1], 8, write_g2, 4)
 
     state = R.state
 
@@ -870,27 +937,26 @@
     def write_g1(r, v):
         G1[r] = v
 
-    conv(R.d[0], 192, R.kt[0], dil[0], 24, write_g1)
-    sum_a.third()
-    sum_b.second()
+    conv(R.d[0], 192, R.kt[0], dil[0], 4, write_g1)
+    conv(R.d[0], 192, R.kt[0], dil[0], 4, write_g1, 20)
     send_backward(BACK1, rims_of(delta1, 16, 128, 64, 0, R.kt[0]), G1, 0, 64, 16, 4)
     start(BACK1)
-
+    sum_a.third()
+    conv(R.d[0], 192, R.kt[0], dil[0], 16, write_g1, 4)
+    sum_b.second()
+    conv(R.x[3], 576, R.kf[3], dil[3], 8, write_state, 8)
     sum_a.fourth()
-    conv(R.x[3], 576, R.kf[3], dil[3], 8, write_state, 8)
+    arrive(BACK1)
+    grad = R.grad
+
+    def write_grad(r, v):
+        grad[r] = v
+
+    fold(BACK1, G1, 0, 64, 16, 128, 4, write_grad)
     sum_b.third()
     sum_a.fifth()
-    arrive(BACK1)
-    grad = R.grad
-
-    def write_grad(r, v):
-        grad[r] = v
-
-    fold(BACK1, G1, 0, 64, 16, 128, 4, write_grad)
     sum_b.fourth()
     sum_a.sixth()
-    sum_b.fifth()
-    sum_b.sixth()
 
     sum_a.finish()
     sum_b.finish()
@@ -899,7 +965,7 @@
             copy.wait_send()
 
 
-PIECE = (80, 32)
+PIECE = (80, 64)
 
 
 def run_net(tiles, members, scale, operands):
@@ -935,14 +1001,14 @@
         recv=D((len(EXCHANGES), 8)),
         send_code=D((2,)),
         recv_code=D((2,)),
-        pay=[V((2, n_xy, q, LANES), BF) for q in PIECE],
-        others=[V((n_xy, q, LANES), BF) for q in PIECE],
-        half=[V((n_xy, q, LANES), BF) for q in PIECE],
+        pay=[V((2 - i, n_xy, q, LANES), BF) for i, q in enumerate(PIECE)],
+        others=[V((n_xy, PIECE[0], LANES), BF)],
+        half=[V((n_xy, PIECE[0], LANES), BF)],
         bxy=[V((n_xy, q, LANES), BF) for q in PIECE],
-        bz=[V((n_z, q, LANES), BF) for q in PIECE],
-        psem=[D((4,)) for q in PIECE],
+        bz=[V((n_z * (i + 1), q, LANES), BF) for i, q in enumerate(PIECE)],
+        psem=[D((4,))],
         xysem=[D((4, n_xy)) for q in PIECE],
-        zsem=[D((2, n_z)) for q in PIECE],
+        zsem=[D((2, n_z * (i + 1))) for i, q in enumerate(PIECE)],
         cs=[V((sent, C * m * H // LANES, LANES), BF) for C, m, H, sent in EXCHANGES],
         rs=[V((2, m * H // 16, C, LANES), BF) for C, m, H, sent in EXCHANGES],
         cr=[V((6, C * m * H // LANES, LANES), BF) for C, m, H, sent in EXCHANGES],
@@ -954,7 +1020,7 @@
     outputs = Refs(
         state=shape((16, 64, LANES), BF),
         grad=shape((16, 64, LANES), F32),
-        res=[shape((2, n_xy, q, LANES), BF) for q in PIECE],
+        res=[shape((2 - i, n_xy, q, LANES), BF) for i, q in enumerate(PIECE)],
     )
     inputs = Refs(**operands)
     flat_in, flat_out, flat_scratch = (list(flatten(part)) for part in (inputs, outputs, scratch))
@@ -987,7 +1053,7 @@
         out_shape=tuple(outputs),
         in_specs=[vmem] * len(raw),
         out_specs=(vmem,) * len(outputs),
-        compiler_params=pltpu.CompilerParams(vmem_limit_bytes=32 * 2**20),
+        compiler_params=pltpu.CompilerParams(vmem_limit_bytes=56 * 2**20),
     )(*raw)
 
 

time: 86.3 us -> 81.1 us (0.940)
  local copies, waits for them, and re-layouts: 4.02 us -> 0 us
  Pallas kernels: 81.4 us -> 80.1 us
    unnamed x8 -> x0, local copies, waits for them, and re-layouts: 4.02 us -> none
    pallas_call x1, Pallas kernels: 79.4 us -> 76.7 us  [run_net(): pl.pallas_call(functools.partial(net_kernel, tiles, members, scale, (inpu...]
    pallas_call x1, Pallas kernels: 1.92 us -> 3.38 us  [run_finish(): pl.pallas_call(finish_kernel, out_shape=tuple(outputs), in_specs=[vmem] *...]
where the time goes in v5:
time: 81.1 us; the launch traced here: 80.9 us
  Pallas kernels  80.1 us (99%)
    pallas_call x1, Pallas kernels, run_net(): pl.pallas_call(functools.partial(net_kernel, tiles, members, scale, (inpu...  76.7 us
    pallas_call x1, Pallas kernels, run_finish(): pl.pallas_call(finish_kernel, out_shape=tuple(outputs), in_specs=[vmem] *...  3.38 us

profile of v5, /device:TPU:1, one launch (start us, length us, event | category | flops | bytes accessed | tf_op | source)
XLA Modules:
  0.0 80.9 jit_solution(11263006387607348640)
XLA Ops:
  0.6 76.7 %shard_map.195 = (bf16[16,64,128]{2,1,0:T(8,128)(2,1)}, f32[16,64,128]{2,1,0:T(8,128)}, bf16[2,16,80,128]{3,2,1,0:T(8,128)(2,1)}, bf16[1,16,64,128]{3,2,1,0:T(8,128)(2,1)}) custom-call(s32[1,4]{1,0:T(1,128)} %refs_0_.1, s32[4]{0:T(128)} %refs_1_.1, bf16[64,16,128]{2,1,0:T(8,128)(2,1)} %bitcast.14, bf16[64,16,128]{2,1,0:T(8,128)(2,1)} %bitcast.15, ...), custom_call_target="tpu_custom_call" | custom-call | tf_op jit(solution)/shard_map/pallas_call | solution.py:1027
  77.3 3.4 %shard_map.196 = (bf16[64,16,128]{2,1,0:T(8,128)(2,1)}, f32[64,16,128]{2,1,0:T(8,128)}, f32[9,64,64]{2,1,0:T(8,128)}, f32[9,64,128]{2,1,0:T(8,128)}, f32[9,128,1...) custom-call(bf16[16,64,128]{2,1,0:T(8,128)(2,1)} %get-tuple-element., ...), custom_call_target="tpu_custom_call" | custom-call | tf_op jit(solution)/shard_map/pallas_call | solution.py:1051

commit v6 on v5

--- a/solution.py
+++ b/solution.py
@@ -264,6 +264,13 @@
 
     def device(offset):
         return (ens, lax.rem(tile + (offset + tiles), tiles))
+
+    brought = [
+        pltpu.make_async_copy(there, here, R.bring.at[i])
+        for i, (there, here) in enumerate(zip(R.far + R.k_far, R.near + R.k))
+    ]
+    for copy in brought:
+        copy.start()
 
     copies = []
     for x, (C, m, H, sent) in enumerate(EXCHANGES):
@@ -767,16 +774,19 @@
         pieces = ref.shape[0] * ref.shape[1] * ref.shape[2]
         put(ref, where, jnp.zeros((pieces - where, LANES), BF))
 
-    rows_first(R.fields_in, R.fields)
+    brought[0].wait()
+    rows_first(R.near[0], R.fields)
     send_forward(FIELDS, R.fields, 16, 128, 4, 64)
     pl.semaphore_wait(barrier, 6 + (n_xy - 1) + 2 * (n_z - 1))
     for copy in code_copies:
         copy.start()
     start(FIELDS)
 
+    for copy in brought[1:]:
+        copy.wait()
     forward_weights(0)
     cot = R.cot
-    rows_first(R.cot_in, cot)
+    rows_first(R.near[1], cot)
     backward_weights(3)
     spread_delta(cot, 16, 64, 3, R.d[3])
     G4 = R.g[3]
@@ -785,10 +795,6 @@
         G4[r] = v
 
     conv(R.d[3], 192, R.kt[3], dil[3], 24, write_g4)
-    for i in (1, 2, 3):
-        forward_weights(i)
-    for i in (2, 1, 0):
-        backward_weights(i)
     columns = [column(i) for i in range(4)]
 
     for copy in code_copies:
@@ -826,6 +832,7 @@
         G4c[4 * g : 4 * g + 4] = y.reshape(4, 128, LANES)
     send_backward(BACK4C, rims4[0:128], G4c, 0, 128, 8, 2, True)
     send_backward(BACK4F, rims4[128:192], G4, 128, 64, 16, 4)
+    forward_weights(1)
 
 
     pad_and_shift(POOLED, pooled, 8, 4, 64, 1, R.x[1], (0, 64, 128), False)
@@ -842,6 +849,10 @@
     conv(R.x[1], 192, R.kf[1], dil[1], 8, write_second)
     send_forward(SECOND, second_act, 8, 64, 4, 128)
     start(SECOND)
+    for i in (2, 3):
+        forward_weights(i)
+    for i in (2, 1, 0):
+        backward_weights(i)
 
     arrive(BACK4C)
     coarse, skip = R.coarse, R.skip
@@ -932,6 +943,7 @@
     weight_terms(R.x[0], 64, R.d[0], 64, dil[0], 24, R.w[0])
     put_terms(R.pay[1], ((R.w[1], 64, 128), (R.w[0], 64, 64)))
     sum_b.first()
+    sum_a.third()
     G1 = R.g[0]
 
     def write_g1(r, v):
@@ -941,11 +953,10 @@
     conv(R.d[0], 192, R.kt[0], dil[0], 4, write_g1, 20)
     send_backward(BACK1, rims_of(delta1, 16, 128, 64, 0, R.kt[0]), G1, 0, 64, 16, 4)
     start(BACK1)
-    sum_a.third()
     conv(R.d[0], 192, R.kt[0], dil[0], 16, write_g1, 4)
+    sum_a.fourth()
     sum_b.second()
     conv(R.x[3], 576, R.kf[3], dil[3], 8, write_state, 8)
-    sum_a.fourth()
     arrive(BACK1)
     grad = R.grad
 
@@ -953,10 +964,10 @@
         grad[r] = v
 
     fold(BACK1, G1, 0, 64, 16, 128, 4, write_grad)
+    sum_a.fifth()
     sum_b.third()
-    sum_a.fifth()
+    sum_a.sixth()
     sum_b.fourth()
-    sum_a.sixth()
 
     sum_a.finish()
     sum_b.finish()
@@ -979,6 +990,9 @@
         d=[V((P_ + 2 * RIM, 3 * O, LANES), BF) for C, O, P_ in sizes],
         g=[V((P_, C, LANES), F32) for C, O, P_ in sizes],
         g4c=V((12, 128, LANES), F32),
+        near=[V(v.shape, BF) for v in operands["far"]],
+        k=[V(v.shape, BF) for v in operands["k_far"]],
+        bring=D((6,)),
         kf=[V((O, 9 * C), BF) for C, O, _ in sizes],
         kt=[V((C, 9 * O), BF) for C, O, _ in sizes],
         w=[V((3 * C + ONES, 256 if O == 64 else 384), F32) for C, O, _ in sizes],
@@ -1027,7 +1041,10 @@
     return pl.pallas_call(
         functools.partial(net_kernel, tiles, members, scale, (inputs, outputs, scratch)),
         out_shape=tuple(flat_out),
-        in_specs=[smem if v.dtype == jnp.int32 else vmem for v in flat_in],
+        in_specs=[
+            smem if v.dtype == jnp.int32 else vmem if v.dtype == F32 else pl.BlockSpec(memory_space=pl.ANY)
+            for v in flat_in
+        ],
         out_specs=(vmem,) * len(flat_out),
         scratch_shapes=flat_scratch,
         compiler_params=pltpu.CompilerParams(
@@ -1061,9 +1078,8 @@
     operands = dict(
         codes=codes,
         dil=dilations,
-        fields_in=fields[0, 0],
-        cot_in=cotangent[0, 0],
-        k=[k1, jnp.swapaxes(k2, 1, 2), k3, k4],
+        far=[fields[0, 0], cotangent[0, 0]],
+        k_far=[k1, jnp.swapaxes(k2, 1, 2), k3, k4],
         off=[off1[None, :], off2[None, :], off3[None, :], off4[None, :]],
     )
     scale = 1.0 / math.sqrt(members * tiles * fields.shape[3] * fields.shape[4])

time: 81.1 us -> 82.8 us (1.021)
  Pallas kernels: 80.1 us -> 81.3 us
    pallas_call x1, Pallas kernels: 76.7 us -> 78 us  [run_net(): pl.pallas_call(functools.partial(net_kernel, tiles, members, scale, (inpu...]
where the time goes in v6:
time: 82.8 us; the launch traced here: 82.2 us
  Pallas kernels  81.3 us (98%)
    pallas_call x1, Pallas kernels, run_net(): pl.pallas_call(functools.partial(net_kernel, tiles, members, scale, (inpu...  78 us
    pallas_call x1, Pallas kernels, run_finish(): pl.pallas_call(finish_kernel, out_shape=tuple(outputs), in_specs=[vmem] *...  3.38 us

profile of v6, /device:TPU:1, one launch (start us, length us, event | category | flops | bytes accessed | tf_op | source)
XLA Modules:
  0.0 82.2 jit_solution(14422224887067263053)
XLA Ops:
  0.6 78.0 %shard_map.195 = (bf16[16,64,128]{2,1,0:T(8,128)(2,1)}, f32[16,64,128]{2,1,0:T(8,128)}, bf16[2,16,80,128]{3,2,1,0:T(8,128)(2,1)}, bf16[1,16,64,128]{3,2,1,0:T(8,128)(2,1)}) custom-call(s32[1,4]{1,0:T(1,128)} %refs_0_.1, s32[4]{0:T(128)} %refs_1_.1, bf16[64,16,128]{2,1,0:T(8,128)(2,1)} %bitcast.14, bf16[64,16,128]{2,1,0:T(8,128)(2,1)} %bitcast.15, ...), custom_call_target="tpu_custom_call" | custom-call | tf_op jit(solution)/shard_map/pallas_call | solution.py:1041
  78.6 3.4 %shard_map.196 = (bf16[64,16,128]{2,1,0:T(8,128)(2,1)}, f32[64,16,128]{2,1,0:T(8,128)}, f32[9,64,64]{2,1,0:T(8,128)}, f32[9,64,128]{2,1,0:T(8,128)}, f32[9,128,1...) custom-call(bf16[16,64,128]{2,1,0:T(8,128)(2,1)} %get-tuple-element., ...), custom_call_target="tpu_custom_call" | custom-call | tf_op jit(solution)/shard_map/pallas_call | solution.py:1068

commit v7 on v6

--- a/solution.py
+++ b/solution.py
@@ -501,7 +501,7 @@
             each(n_xy, lambda k: self.back_copy(k).wait_send())
             each(2 * n_z, lambda k: self.z_copy(k).wait_send())
 
-    sum_a, sum_b = Sum(0), LateSum(1)
+    sum_a, sum_b, sum_c = Sum(0), LateSum(1), LateSum(2)
 
     barrier = pltpu.get_barrier_semaphore()
 
@@ -927,8 +927,11 @@
 
 
     weight_terms(R.x[1], 64, R.d[1], 128, dil[1], 16, R.w[1])
+    put_terms(R.pay[2], ((R.w[1], 64, 128),))
+    sum_c.first()
     sum_a.second()
     conv(R.x[3], 576, R.kf[3], dil[3], 8, write_state)
+    sum_c.second()
     arrive(BACK2)
     delta1 = R.delta1
     repeat = jnp.where((u & (LANES - 1)) == (w >> 1), 0.25, 0.0).astype(BF)
@@ -941,9 +944,8 @@
     fold(BACK2, G2, 0, 64, 8, 64, 4, write_delta1)
     spread_delta(delta1, 16, 64, 0, R.d[0])
     weight_terms(R.x[0], 64, R.d[0], 64, dil[0], 24, R.w[0])
-    put_terms(R.pay[1], ((R.w[1], 64, 128), (R.w[0], 64, 64)))
+    put_terms(R.pay[1], ((R.w[0], 64, 64),))
     sum_b.first()
-    sum_a.third()
     G1 = R.g[0]
 
     def write_g1(r, v):
@@ -953,10 +955,12 @@
     conv(R.d[0], 192, R.kt[0], dil[0], 4, write_g1, 20)
     send_backward(BACK1, rims_of(delta1, 16, 128, 64, 0, R.kt[0]), G1, 0, 64, 16, 4)
     start(BACK1)
+    sum_a.third()
     conv(R.d[0], 192, R.kt[0], dil[0], 16, write_g1, 4)
-    sum_a.fourth()
+    sum_c.third()
     sum_b.second()
     conv(R.x[3], 576, R.kf[3], dil[3], 8, write_state, 8)
+    sum_a.fourth()
     arrive(BACK1)
     grad = R.grad
 
@@ -964,19 +968,21 @@
         grad[r] = v
 
     fold(BACK1, G1, 0, 64, 16, 128, 4, write_grad)
+    sum_b.third()
+    sum_c.fourth()
     sum_a.fifth()
-    sum_b.third()
+    sum_b.fourth()
     sum_a.sixth()
-    sum_b.fourth()
 
     sum_a.finish()
     sum_b.finish()
+    sum_c.finish()
     for listed in (*copies, code_copies):
         for copy in listed:
             copy.wait_send()
 
 
-PIECE = (80, 64)
+PIECE = (80, 32, 48)
 
 
 def run_net(tiles, members, scale, operands):
@@ -1015,14 +1021,14 @@
         recv=D((len(EXCHANGES), 8)),
         send_code=D((2,)),
         recv_code=D((2,)),
-        pay=[V((2 - i, n_xy, q, LANES), BF) for i, q in enumerate(PIECE)],
+        pay=[V((1 if i else 2, n_xy, q, LANES), BF) for i, q in enumerate(PIECE)],
         others=[V((n_xy, PIECE[0], LANES), BF)],
         half=[V((n_xy, PIECE[0], LANES), BF)],
         bxy=[V((n_xy, q, LANES), BF) for q in PIECE],
-        bz=[V((n_z * (i + 1), q, LANES), BF) for i, q in enumerate(PIECE)],
+        bz=[V((n_z * (2 if i else 1), q, LANES), BF) for i, q in enumerate(PIECE)],
         psem=[D((4,))],
         xysem=[D((4, n_xy)) for q in PIECE],
-        zsem=[D((2, n_z * (i + 1))) for i, q in enumerate(PIECE)],
+        zsem=[D((2, n_z * (2 if i else 1))) for i, q in enumerate(PIECE)],
         cs=[V((sent, C * m * H // LANES, LANES), BF) for C, m, H, sent in EXCHANGES],
         rs=[V((2, m * H // 16, C, LANES), BF) for C, m, H, sent in EXCHANGES],
         cr=[V((6, C * m * H // LANES, LANES), BF) for C, m, H, sent in EXCHANGES],
@@ -1034,7 +1040,7 @@
     outputs = Refs(
         state=shape((16, 64, LANES), BF),
         grad=shape((16, 64, LANES), F32),
-        res=[shape((2 - i, n_xy, q, LANES), BF) for i, q in enumerate(PIECE)],
+        res=[shape((1 if i else 2, n_xy, q, LANES), BF) for i, q in enumerate(PIECE)],
     )
     inputs = Refs(**operands)
     flat_in, flat_out, flat_scratch = (list(flatten(part)) for part in (inputs, outputs, scratch))
@@ -1052,11 +1058,12 @@
         ),
     )(*flat_in)
 
-def finish_kernel(state, grad, early, late, state_out, grad_out, w1, w2, w3, w4, b1, b2, b3, b4):
+def finish_kernel(state, grad, early, late, middle, state_out, grad_out, w1, w2, w3, w4, b1, b2, b3, b4):
     channels_first(state, state_out, 1)
     channels_first(grad, grad_out, 2)
     take_terms(early, ((w4, b4, 192, 64), (w3, b3, 128, 128)))
-    take_terms(late, ((w2, b2, 64, 128), (w1, b1, 64, 64)))
+    take_terms(late, ((w1, b1, 64, 64),))
+    take_terms(middle, ((w2, b2, 64, 128),))
 
 
 def run_finish(raw):

time: 82.8 us -> 83.5 us (level)
  Pallas kernels: 81.3 us -> 82.5 us
    pallas_call x1, Pallas kernels: 78 us -> 79.1 us  [run_net(): pl.pallas_call(functools.partial(net_kernel, tiles, members, scale, (inpu...]
where the time goes in v7:
time: 83.5 us; the launch traced here: 83.3 us
  Pallas kernels  82.5 us (99%)
    pallas_call x1, Pallas kernels, run_net(): pl.pallas_call(functools.partial(net_kernel, tiles, members, scale, (inpu...  79.1 us
    pallas_call x1, Pallas kernels, run_finish(): pl.pallas_call(finish_kernel, out_shape=tuple(outputs), in_specs=[vmem] *...  3.39 us

profile of v7, /device:TPU:1, one launch (start us, length us, event | category | flops | bytes accessed | tf_op | source)
XLA Modules:
  0.0 83.3 jit_solution(4363609188647740590)
XLA Ops:
  0.6 79.1 %shard_map.195 = (bf16[16,64,128]{2,1,0:T(8,128)(2,1)}, f32[16,64,128]{2,1,0:T(8,128)}, bf16[2,16,80,128]{3,2,1,0:T(8,128)(2,1)}, bf16[1,16,32,128]{3,2,1,0:T(8,128)(2,1)}, bf16[1,16,48,128]{3,2,1,0:T(8,128)(2,1)}) custom-call(s32[1,4]{1,0:T(1,128)} %refs_0_.1, s32[4]{0:T(128)} %refs_1_.1, bf16[64,16,128]{2,1,0:T(8,128)(2,1)} %bitcast.14, ...), custom_call_target="tpu_custom_call" | custom-call | tf_op jit(solution)/shard_map/pallas_call | solution.py:1047
  79.7 3.4 %shard_map.196 = (bf16[64,16,128]{2,1,0:T(8,128)(2,1)}, f32[64,16,128]{2,1,0:T(8,128)}, f32[9,64,64]{2,1,0:T(8,128)}, f32[9,64,128]{2,1,0:T(8,128)}, f32[9,128,1...) custom-call(bf16[16,64,128]{2,1,0:T(8,128)(2,1)} %get-tuple-element., ...), custom_call_target="tpu_custom_call" | custom-call | tf_op jit(solution)/shard_map/pallas_call | solution.py:1075
